TPU v7x, 512 devices: a whole 4x4x16 slice. The times are simulated.
512 devices in a mesh: group: 16 (over z_hi, y, core), dp: 32 (over z_lo, x).
Axes of the slice: x: 4, y: 4, z: 16 (z_hi: 2, z_lo: 8; z = z_hi * 8 + z_lo), core: 2. Of those that a mesh axis runs over, the one named last changes fastest.
Arguments:
- grad: bfloat16 [16, 64, 512, 512], P('group', 'dp'), may hold values from -6 to 6
- stats: float32 [16, 32, 512, 512], P('group', 'dp'), may hold values from -3584 to 3584, as said below
- owner: int32 [32, 2], replicated, may hold values from 0 to 7, all different within a row
Outputs:
- new_stats: float32 [16, 32, 512, 512], P('group', 'dp')
- update: bfloat16 [64, 512, 512], P('dp')
Inputs may be any that keep to these rules, and one draw needn't show every extreme that they name: The entries of a row of owner are different. `stats`: every matrix is symmetric positive definite.
All inputs are finite; a program needn't handle non-finite values.
Results may differ from a plain program's by a relative error of at most 0.03.
Values may be sent and summed in bfloat16 or wider, within the bound.
No kernel may reach another device: no remote copies, remote signals or barrier semaphores. Data moves between devices by JAX's collectives and lax.ppermute only.
A program may use at most 64 MiB of HBM per device.

v0:
```python
import jax
import jax.numpy as jnp
from jax import lax
from jax.sharding import PartitionSpec as P

NEWTON_ITERS = 3


BETA = 0.9
DAMPING = 0.0001


def spread(array, axis, root):
    mine = lax.axis_index(axis) == root
    return lax.psum(jnp.where(mine, array, jnp.zeros_like(array)), axis)


def partner(array, axis, bit):
    return lax.ppermute(array, axis, [(i, i ^ 1 << bit) for i in range(lax.axis_size(axis))])


def matmul(left, right):
    return jnp.dot(left, right, precision=lax.Precision.HIGHEST, preferred_element_type=jnp.float32)


def fourth_root(matrix):
    order = matrix.shape[0]
    eye = jnp.eye(order, dtype=jnp.float32)
    shifted = matrix + DAMPING * eye
    frob = jnp.sqrt(jnp.sum(shifted * shifted))
    current = shifted / frob
    result = eye * frob ** (-0.25)
    for step in range(NEWTON_ITERS):
        factor = (5.0 * eye - current) * 0.25
        result = matmul(result, factor)
        if step + 1 < NEWTON_ITERS:
            square = matmul(factor, factor)
            current = matmul(matmul(square, square), current)
    return result


def spread_half(piece, source):
    return spread(piece, "group", source)


def body(grad, stats, owner):
    group_index = lax.axis_index("group")
    column = lax.axis_index("dp")
    local = grad[0].astype(jnp.float32)
    summed = lax.psum(local.astype(jnp.bfloat16), "group")
    order = summed.shape[1]
    owner_row = lax.dynamic_index_in_dim(owner, column, 0, keepdims=False)
    pair = group_index // 2
    side = group_index % 2
    matches = owner_row == pair
    active = jnp.any(matches)
    slot = jnp.sum(jnp.where(matches, jnp.arange(owner_row.shape[0], dtype=jnp.int32), 0))
    block = lax.dynamic_index_in_dim(summed, slot, 0, keepdims=False)
    dense = block.astype(jnp.float32)
    stat_old = stats[0, 0]
    oriented = jnp.where(side == 0, block, block.T)

    def owned(operand):
        gram = jnp.dot(oriented, oriented.T, preferred_element_type=jnp.float32)
        fresh = BETA * operand + (1.0 - BETA) * gram
        return (fresh, fourth_root(fresh))

    def unowned(operand):
        return (operand, jnp.zeros_like(operand))

    stat_new, root = lax.cond(active, owned, unowned, stat_old)
    new_stats = stat_new[None, None]
    grad_sq = jnp.sum(dense * dense)
    pieces = []
    other = partner(root, "group", 0)
    left = jnp.where(side == 0, root, other)
    right = jnp.where(side == 0, other, root)
    half = order // 2
    left_rows = lax.dynamic_slice_in_dim(left, side * half, half, 0)

    def half_product(operand):
        return matmul(matmul(operand, dense), right)

    def half_zero(operand):
        return jnp.zeros((half, order), jnp.float32)

    partial_block = lax.cond(active, half_product, half_zero, left_rows)
    own_sq = jnp.sum(partial_block * partial_block)
    other_sq = partner(own_sq, "group", 0)
    ratio = jnp.sqrt(grad_sq / (own_sq + other_sq + 1e-06))
    piece = (partial_block * ratio).astype(jnp.bfloat16)
    for index in range(owner_row.shape[0]):
        halves = [spread_half(piece, 2 * owner_row[index] + which) for which in range(2)]
        pieces.append(jnp.concatenate(halves, 0))
    update = jnp.stack(pieces, 0)
    return (new_stats, update)


def solution(mesh):
    in_specs = (P("group", "dp", None, None), P("group", "dp", None, None), P())
    out_specs = (P("group", "dp", None, None), P("dp", None, None))
    return jax.shard_map(body, mesh=mesh, in_specs=in_specs, out_specs=out_specs, check_vma=False)
```

profile of v0, /device:TPU:1, one launch (start us, length us, event | category | flops | bytes accessed | tf_op | source)
XLA Modules:
  0.0 588.4 jit_solution(10187096492803847259)
XLA Ops:
  7.2 0.0 all-reduce.4.cloned.1.call-start
  7.2 2.3 copy.23
  9.5 0.0 all-reduce.4.cloned.1.call-update
  9.5 0.0 all-reduce.6.cloned.1.call-start
  9.6 0.0 copy-start.2
  9.6 0.7 copy-done.2
  10.2 0.7 fusion.52
  11.0 0.7 select_reduce_fusion
  14.2 260.8 %all-reduce.4.cloned.1.call-done = bf16[2,512,512]{2,1,0:T(8,128)(2,1)} async-done(((bf16[2,512,512]{2,1,0:T(8,128)(2,1)}), bf16[2,512,512]{2,1,0:T(8,128)(2,1)}) %all-reduce.4.cloned.1.call-update) | async-done | bytes 1048592 | tf_op jit(solution)/shard_map/psum | solution.py:50
  275.0 0.0 copy-start.1
  275.0 2.0 multiply_reduce_fusion.2
  277.0 0.0 copy-done.1
  277.0 0.0 copy-start
  277.1 0.8 copy-done
  277.8 0.3 conditional.2
  277.8 0.1 broadcast.29
  278.2 2.8 collective-permute-start
  281.0 0.6 fusion.54
  282.9 1.2 convert_element_type.14
  284.1 0.0 collective-permute-done
  284.1 0.9 conditional.3
  284.1 0.9 broadcast.36
  285.0 2.8 collective-permute-start.1
  287.8 0.3 collective-permute-done.1
  289.4 1.8 broadcast_select_fusion.3
  291.3 0.9 broadcast_select_fusion.2
  292.1 0.0 all-reduce.6.cloned.1.call-update
  292.2 287.1 %all-reduce.6.cloned.1.call-done = (bf16[256,512]{1,0:T(8,128)(2,1)}, bf16[256,512]{1,0:T(8,128)(2,1)}, bf16[256,512]{1,0:T(8,128)(2,1)}, bf16[256,512]{1,0:T(8,128)(2,1)}) async-done(((bf16[256,512]{1,0:T(8,128)(2,1)}, bf16[256,512]{1,0:T(8,128)(2,1)}, bf16[256,512]{1,0:T(8,128)(2,1)}, bf16[256,512]{1,0:T(8,128)(2,1)}), (bf16[256,512]{1,0:T(8,128)(2,1)}, bf16[256,512]{1,0:T(8,128)(2,1)}, ...) | async-done | bytes 1048592 | tf_op jit(solution)/shard_map/psum | solution.py:15
  579.2 1.3 maximum_bitcast_fusion
  580.5 1.1 pad_maximum_fusion
  (1 shorter events, 0.0 us)
Async XLA Ops:
  7.2 267.8 %all-reduce.4.cloned.1.call-start = ((), (), s32[]{:S(2)}) async-start(), calls=%async_computation | async-start | bytes 2097152 | tf_op jit(solution)/shard_map/psum | solution.py:50
  9.5 569.7 %all-reduce.6.cloned.1.call-start = ((), (), s32[]{:S(2)}) async-start(), calls=%async_computation.1 | async-start | bytes 2097152 | tf_op jit(solution)/shard_map/psum | solution.py:15
  9.6 0.7 copy-start.2
  275.0 2.0 copy-start.1
  277.0 0.8 copy-start
  278.2 5.9 %collective-permute-start = (f32[512,512]{1,0:T(8,128)S(1)}, f32[512,512]{1,0:T(8,128)S(1)}, u32[]{:S(2)}, u32[]{:S(2)}) collective-permute-start(f32[512,512]{1,0:T(8,128)S(1)} %get-tuple-element.89), channel_id=1, source_target_pairs={{0,32},{32,0},{64,96},{96,64},{128,160},{160,128},{192,224},{224,1... | collective-permute-start | bytes 3145736 | tf_op jit(solution)/shard_map/ppermute | solution.py:19
  285.0 3.1 collective-permute-start.1
Sparse Core Ops, SparseCore 0:
  10.9 264.0 all-reduce.3
  292.3 286.9 all-reduce.5
where the time goes:
time: 589 us; the launch traced here: 588 us
  waiting for transfers between devices  548 us (93%)
  between operations  19.3 us (3%)
  other arithmetic  9.6 us (2%)
    psum x1, waiting for transfers between devices, spread(): return lax.psum(jnp.where(mine, array, jnp.zeros_like(array)), axis)  287 us
    psum x1, waiting for transfers between devices, body(): summed = lax.psum(local.astype(jnp.bfloat16), 'group')  261 us
  transfers between devices with their start and end apart: 4, of which 3 were waited for; matrix products, arithmetic and copies ran while one was open for 1% of the time, Pallas kernels for 0%

commit v1 on v0

v1 whole, which is shorter than its diff:
```python
import functools

import jax
import jax.numpy as jnp
from jax import lax
from jax.experimental import pallas as pl
from jax.experimental.pallas import tpu as pltpu
from jax.sharding import PartitionSpec as P

BETA = 0.9
DAMPING = 0.0001
BS = 512
HALF = BS // 2
QUARTER = BS // 8
PACK = 320
PART = PACK // 4
ROWS = 2 * QUARTER
WIDE = ROWS + PART
LIMIT = 32 * 1024 * 1024

BF = jnp.bfloat16
F32 = jnp.float32

VM = pl.BlockSpec(memory_space=pltpu.VMEM)
SM = pl.BlockSpec(memory_space=pltpu.SMEM)


def call(kernel, shapes, specs, scratch=(), flops=0, nbytes=0):
    return pl.pallas_call(
        kernel,
        out_shape=shapes,
        in_specs=specs,
        out_specs=VM,
        scratch_shapes=list(scratch),
        compiler_params=pltpu.CompilerParams(vmem_limit_bytes=LIMIT),
        cost_estimate=pl.CostEstimate(flops=flops, bytes_accessed=nbytes, transcendentals=0),
    )


def mm(a, b):
    return jnp.dot(a.astype(BF), b.astype(BF), preferred_element_type=F32)


def pack_rows(s, out):
    def put(row, col, value):
        rows, cols = value.shape
        done = 0
        while done < rows:
            part, at = divmod(row + done, PART)
            n = min(rows - done, PART - at)
            out[part, ROWS + at : ROWS + at + n, col : col + cols] = value[done : done + n]
            done += n

    put(0, 0, s[0:128, :].astype(BF))
    put(128, 0, s[128:256, 128:512].astype(BF))
    put(128, 384, s[384:512, 384:512].astype(BF))
    put(256, 0, s[256:320, 256:512].astype(BF))
    put(256, 256, s[320:384, 256:512].astype(BF))


def unpack_rows(p, s):
    top = p[0:128, :].astype(F32)
    s[0:128, :] = top
    s[128:512, 0:128] = top[:, 128:512].T
    second = p[128:256, :].astype(F32)
    s[128:256, 128:512] = second[:, 0:384]
    s[256:512, 128:256] = second[:, 128:384].T
    s[384:512, 384:512] = second[:, 384:512]
    s[256:320, 256:512] = p[256:320, 0:256].astype(F32)
    s[320:384, 256:512] = p[256:320, 256:512].astype(F32)
    s[384:512, 256:384] = s[256:384, 384:512].T


def first_kernel(meta, grad, got, stat, out):
    core = meta[0]
    for b in range(2):
        for y in range(4):
            at = pl.multiple_of(core * HALF + y * QUARTER, QUARTER)
            mine = grad[b, pl.ds(at, QUARTER), :].astype(F32)
            other = got[b, y * QUARTER : (y + 1) * QUARTER, :].astype(F32)
            out[y, b * QUARTER : (b + 1) * QUARTER, :] = (mine + other).astype(BF)
    pack_rows(stat, out)


def second_kernel(meta, got, out):
    total = got[0, 0:ROWS, :].astype(F32)
    for y in range(1, 4):
        total += got[y, 0:ROWS, :].astype(F32)
    out[0:ROWS, :] = total.astype(BF)
    for b in range(2):
        out[ROWS + b * PART : ROWS + (b + 1) * PART, :] = got[meta[4 + b], ROWS:WIDE, :]


def third_kernel(meta, mine, got, out):
    total = (mine[0:ROWS, :].astype(F32) + got[0:ROWS, :].astype(F32)).astype(BF)
    for y in range(4):
        out[y, 0:ROWS, :] = total
    for b in range(2):
        here = meta[6 + b] == 1
        lo = ROWS + b * PART
        rows = slice(lo, lo + PART)

        @pl.when(here)
        def _():
            for y in range(2):
                out[2 * b + y, ROWS:WIDE, :] = mine[rows, :]

        @pl.when(jnp.logical_not(here))
        def _():
            for y in range(2):
                out[2 * b + y, ROWS:WIDE, :] = got[rows, :]


def assemble(core, block, mine, other, dense):
    lo = pl.multiple_of(block * QUARTER, QUARTER)
    for y in range(4):
        at = pl.multiple_of(core * HALF + y * QUARTER, QUARTER)
        dense[pl.ds(at, QUARTER), :] = mine[y, pl.ds(lo, QUARTER), :]
        at = pl.multiple_of((1 - core) * HALF + y * QUARTER, QUARTER)
        dense[pl.ds(at, QUARTER), :] = other[y, pl.ds(lo, QUARTER), :]


def gram_of(core, dense, oriented):
    @pl.when(core == 0)
    def _():
        oriented[...] = dense[...]

    @pl.when(core == 1)
    def _():
        oriented[...] = dense[...].astype(F32).T.astype(BF)

    value = oriented[...]
    return lax.dot_general(value, value, (((1,), (1,)), ((), ())), preferred_element_type=F32)


def newton(current):
    low = current.astype(BF)
    square = (1.0 / 16) * mm(low, low) - (10.0 / 16) * current
    slow = square.astype(BF)
    fourth = (50.0 / 16) * square + mm(slow, slow)
    return (625.0 / 256) * current + mm(fourth, low)


def root_kernel(meta, mine, other, out, dense, oriented, packed, stat):
    core = meta[0]
    assemble(core, meta[3], mine, other, dense)
    for y in range(4):
        packed[y * PART : (y + 1) * PART, :] = mine[y, ROWS:WIDE, :]
    unpack_rows(packed, stat)
    gram = gram_of(core, dense, oriented)
    rows = lax.broadcasted_iota(jnp.int32, (BS, BS), 0)
    cols = lax.broadcasted_iota(jnp.int32, (BS, BS), 1)
    shifted = BETA * stat[...] + (1.0 - BETA) * gram + jnp.where(rows == cols, DAMPING, 0.0)
    frob = jnp.sqrt(jnp.sum(shifted * shifted, keepdims=True))
    m0 = shifted * (1.0 / frob)
    m1 = newton(m0)
    m2 = newton(m1)
    n01 = (-1.25 / 4) * (m0 + m1) + (1.0 / 16) * mm(m0, m1)
    excess = 1.25 * n01 - (1.5625 / 4) * m2 - 0.25 * mm(n01, m2)
    scale = lax.rsqrt(jnp.sqrt(frob))

    @pl.when(core == 0)
    def _():
        block = dense[...]
        out[0:BS, :] = (scale * (1.953125 * block.astype(F32) + mm(excess, block))).astype(BF)
        out[BS : BS + 16, :] = jnp.zeros((16, BS), BF)

    @pl.when(core == 1)
    def _():
        out[0:BS, :] = excess.astype(BF)
        value = jnp.broadcast_to(scale, (16, BS))
        high = value.astype(BF).astype(F32)
        middle = (value - high).astype(BF).astype(F32)
        low = value - high - middle
        row = lax.broadcasted_iota(jnp.int32, (16, BS), 0)
        out[BS : BS + 16, :] = jnp.where(row == 0, high, jnp.where(row == 1, middle, low)).astype(BF)


def stat_kernel(meta, mine, other, stat, out, dense, oriented):
    @pl.when(meta[8] == 1)
    def _():
        assemble(meta[0], meta[9], mine, other, dense)
        out[...] = BETA * stat[...] + (1.0 - BETA) * gram_of(meta[0], dense, oriented)

    @pl.when(meta[8] == 0)
    def _():
        out[...] = stat[...]


def product_kernel(meta, mine, other, first, second, out, dense, left, right, prod):
    core = meta[0]
    assemble(core, meta[3], first, second, dense)

    @pl.when(core == 0)
    def _():
        left[...] = mine[...]
        right[...] = other[...]

    @pl.when(core == 1)
    def _():
        left[...] = other[...]
        right[...] = mine[...]

    tail = right[BS : BS + 16, :].astype(F32)
    scale = tail[0:1, 0:1] + tail[1:2, 0:1] + tail[2:3, 0:1]
    low = left[0:BS, :]
    precond = scale * (1.953125 * low.astype(F32) + mm(low, right[0:BS, :]))
    value = dense[...].astype(F32)
    grad_sq = jnp.sum(value * value, keepdims=True)
    pre_sq = jnp.sum(precond * precond, keepdims=True)
    prod[...] = (precond * jnp.sqrt(grad_sq / (pre_sq + 1e-06))).astype(BF)
    at = pl.multiple_of(lax.rem(meta[2], 2) * HALF + core * (HALF // 2), HALF // 2)
    rows = prod[pl.ds(at, HALF // 2), :]
    for y in range(4):
        out[y] = rows


def last_kernel(meta, mine, other, out):
    here = pl.multiple_of(meta[0] * (HALF // 2), HALF // 2)
    there = pl.multiple_of((1 - meta[0]) * (HALF // 2), HALF // 2)
    for y in range(4):
        lo = (y % 2) * HALF
        out[y // 2, pl.ds(lo + here, HALF // 2), :] = mine[y]
        out[y // 2, pl.ds(lo + there, HALF // 2), :] = other[y]


def body(grad, stats, owner):
    group = lax.axis_index("group")
    column = lax.axis_index("dp")
    core, y, half = group % 2, (group // 2) % 4, group // 8
    row = lax.dynamic_index_in_dim(owner, column, 0, keepdims=False)
    matches = (row == group // 2).astype(jnp.int32)
    meta = jnp.stack(
        [
            core,
            half,
            y,
            y // 2,
            row[0] % 4,
            row[1] % 4,
            (row[0] // 4 == half).astype(jnp.int32),
            (row[1] // 4 == half).astype(jnp.int32),
            jnp.max(matches),
            matches[1],
        ]
    ).astype(jnp.int32)
    along_y = [[h * 8 + 2 * k + c for k in range(4)] for h in range(2) for c in range(2)]
    swap = [(g, g ^ 1) for g in range(16)]
    cross = [(g, g ^ 8) for g in range(16)]

    def exchange(value):
        return lax.all_to_all(value, "group", 0, 0, tiled=True, axis_index_groups=along_y)

    block = grad[0]
    stat = stats[0, 0]
    away = lax.dynamic_slice_in_dim(block, (1 - core) * HALF, HALF, 1)
    got = lax.ppermute(away, "group", swap)
    parts = call(first_kernel, jax.ShapeDtypeStruct((4, WIDE, BS), BF), [SM, VM, VM, VM])(meta, block, got, stat)
    parts = exchange(parts)
    mine = call(second_kernel, jax.ShapeDtypeStruct((ROWS + 2 * PART, BS), BF), [SM, VM])(meta, parts)
    got = lax.ppermute(mine, "group", cross)
    parts = call(third_kernel, jax.ShapeDtypeStruct((4, WIDE, BS), BF), [SM, VM, VM])(meta, mine, got)
    parts = exchange(parts)
    other = lax.ppermute(parts[:, :ROWS], "group", swap)
    square = pltpu.VMEM((BS, BS), BF)
    payload = call(
        root_kernel,
        jax.ShapeDtypeStruct((BS + 16, BS), BF),
        [SM, VM, VM],
        [square, square, pltpu.VMEM((PACK, BS), BF), pltpu.VMEM((BS, BS), F32)],
        flops=10 * 2 * BS**3,
    )(meta, parts, other)
    received = lax.ppermute(payload, "group", swap)
    new_stat = call(
        stat_kernel, jax.ShapeDtypeStruct((BS, BS), F32), [SM, VM, VM, VM], [square, square], flops=2 * BS**3, nbytes=3 << 20
    )(meta, parts, other, stat)
    tall = pltpu.VMEM((BS + 16, BS), BF)
    rows = call(
        product_kernel,
        jax.ShapeDtypeStruct((4, HALF // 2, BS), BF),
        [SM, VM, VM, VM, VM],
        [square, tall, tall, square],
        flops=2 * BS**3,
    )(meta, payload, received, parts, other)
    rows = exchange(rows)
    rest = lax.ppermute(rows, "group", swap)
    update = call(last_kernel, jax.ShapeDtypeStruct((2, BS, BS), BF), [SM, VM, VM])(meta, rows, rest)
    return (new_stat[None, None], update)


def solution(mesh):
    in_specs = (P("group", "dp", None, None), P("group", "dp", None, None), P())
    out_specs = (P("group", "dp", None, None), P("dp", None, None))
    return jax.shard_map(body, mesh=mesh, in_specs=in_specs, out_specs=out_specs, check_vma=False)
```

time: 589 us -> 122 us (0.21)
  the two profiles are of different devices: /device:TPU:1 before, /device:TPU:37 now
where the time goes in v1:
time: 122 us; the launch traced here: 121 us
  blocking collectives  41.5 us (34%)
  waiting for transfers between devices  27.9 us (23%)
  starting transfers between devices  27.6 us (23%)
  Pallas kernels  11.9 us (10%)
  between operations  5.97 us (5%)
  local copies, waits for them, and re-layouts  5.6 us (5%)
    all_to_all x3, blocking collectives, exchange(): lax.all_to_all(value, 'group', 0, 0, tiled=True, axis_index_groups=along_y)  41.5 us
    ppermute x1, waiting for transfers between devices, body(): got = lax.ppermute(mine, 'group', cross)  24.8 us
    ppermute x1, starting transfers between devices, body(): got = lax.ppermute(mine, 'group', cross)  14.5 us
    ppermute x1, starting transfers between devices, body(): other = lax.ppermute(parts[:, :ROWS], 'group', swap)  4.9 us
    pallas_call x1, Pallas kernels, body(): call(root_kernel, jax.ShapeDtypeStruct((BS + 16, BS), BF), [SM, VM, VM],...  4.42 us
    ppermute x1, starting transfers between devices, body(): rest = lax.ppermute(rows, 'group', swap)  3.1 us
    ppermute x1, starting transfers between devices, body(): got = lax.ppermute(away, 'group', swap)  2.58 us
    ppermute x1, starting transfers between devices, body(): received = lax.ppermute(payload, 'group', swap)  2.48 us
  transfers between devices with their start and end apart: 5, of which 3 were waited for; matrix products, arithmetic and copies ran while one was open for 3% of the time, Pallas kernels for 2%

profile of v1, /device:TPU:37, one launch (start us, length us, event | category | flops | bytes accessed | tf_op | source)
XLA Modules:
  0.0 121.2 jit_solution(5124051415831976747)
XLA Ops:
  0.6 0.0 copy-start
  0.7 1.2 dynamic-slice_bitcast_fusion
  1.8 2.6 %collective-permute-start = (bf16[2,256,512]{2,1,0:T(8,128)(2,1)S(1)}, bf16[2,256,512]{2,1,0:T(8,128)(2,1)S(1)}, u32[]{:S(2)}, u32[]{:S(2)}) collective-permute-start(bf16[2,256,512]{2,1,0:T(8,128)(2,1)S(1)} %dynamic-slice_bitcast_fusion), channel_id=1, source_target_pairs={{0,32},{32,0},{64,96},{96,64},{128,160},{160,128},{192,224},{224,1... | collective-permute-start | bytes 1572872 | tf_op jit(solution)/shard_map/ppermute | solution.py:257
  4.5 0.0 copy-start.2
  4.5 0.7 copy-done.2
  5.1 0.8 fusion
  5.9 0.6 fusion.1
  11.6 0.5 slice.21
  12.2 1.4 %stack.47.meta = s32[10]{0:T(128)S(1)} concatenate(s32[1]{0:T(128)} %bitcast, s32[1]{0:T(128)} %bitcast.1, s32[1]{0:T(128)} %bitcast.2, s32[1]{0:T(128)} %bitcast.3, s32[1]{0:T(128)} %bitcast.5, s32[1]{0:T(128)} %bitcast.7, s32[1]{0:T(128)} %bitcast.8, s32[1]{0:T(128)} %bitcast.9, s32[1]{0:T(128)} %bitcast.10, s32[1]{0:T(128)} %bitcast.11), dimensions={0} | concatenate | bytes 80 | tf_op jit(solution)/shard_map/stack | solution.py:233
  13.6 0.0 collective-permute-done.got
  13.6 0.0 copy-done
  13.6 0.0 copy-start.1
  13.6 1.2 %copy-done.1 = bf16[1,2,512,512]{3,2,1,0:T(8,128)(2,1)S(1)} copy-done((bf16[1,2,512,512]{3,2,1,0:T(8,128)(2,1)S(1)}, bf16[1,2,512,512]{3,2,1,0:T(8,128)(2,1)}, u32[]{:S(2)}) %copy-start.1) | copy-done | bytes 1048600
  14.8 0.7 shard_map.50
  15.5 16.5 %all_to_all.15.got = bf16[4,208,512]{2,1,0:T(8,128)(2,1)S(1)} all-to-all(bf16[4,208,512]{2,1,0:T(8,128)(2,1)S(1)} %shard_map.50), channel_id=1, replica_groups={{0,64,128,192},{32,96,160,224},{256,320,384,448},{288,352,416,480},{1,6..., dimensions={0} | all-to-all | bytes 1703936 | tf_op jit(solution)/shard_map/all_to_all | solution.py:252
  32.0 0.6 shard_map.51.mine
  32.7 14.5 %collective-permute-start.1 = (bf16[288,512]{1,0:T(8,128)(2,1)S(1)}, bf16[288,512]{1,0:T(8,128)(2,1)S(1)}, u32[]{:S(2)}, u32[]{:S(2)}) collective-permute-start(bf16[288,512]{1,0:T(8,128)(2,1)S(1)} %shard_map.51.mine), channel_id=1, source_target_pairs={{0,256},{32,288},{64,320},{96,352},{128,384},{160,416},{192,448},{... | collective-permute-start | bytes 884744 | tf_op jit(solution)/shard_map/ppermute | solution.py:261
  47.2 24.8 %collective-permute-done.1.got = bf16[288,512]{1,0:T(8,128)(2,1)S(1)} collective-permute-done((bf16[288,512]{1,0:T(8,128)(2,1)S(1)}, bf16[288,512]{1,0:T(8,128)(2,1)S(1)}, u32[]{:S(2)}, u32[]{:S(2)}) %collective-permute-start.1) | collective-permute-done | bytes 294944 | tf_op jit(solution)/shard_map/ppermute | solution.py:261
  72.0 0.6 shard_map.52
  72.6 13.3 %all_to_all.16.mine.first = bf16[4,208,512]{2,1,0:T(8,128)(2,1)S(1)} all-to-all(bf16[4,208,512]{2,1,0:T(8,128)(2,1)S(1)} %shard_map.52), channel_id=1, replica_groups={{0,64,128,192},{32,96,160,224},{256,320,384,448},{288,352,416,480},{1,6..., dimensions={0} | all-to-all | bytes 1703936 | tf_op jit(solution)/shard_map/all_to_all | solution.py:252
  86.0 4.9 %collective-permute-start.2 = (bf16[4,128,512]{2,1,0:T(8,128)(2,1)S(1)}, bf16[4,128,512]{2,1,0:T(8,128)(2,1)S(1)}, u32[]{:S(2)}, u32[]{:S(2)}) collective-permute-start(bf16[4,128,512]{2,1,0:T(8,128)(2,1)S(1)} %slice.24), channel_id=1, source_target_pairs={{0,32},{32,0},{64,96},{96,64},{128,160},{160,128},{192,224},{224,1... | collective-permute-start | bytes 1572872 | tf_op jit(solution)/shard_map/ppermute | solution.py:264
  90.9 1.5 %collective-permute-done.2.other.second = bf16[4,128,512]{2,1,0:T(8,128)(2,1)S(1)} collective-permute-done((bf16[4,128,512]{2,1,0:T(8,128)(2,1)S(1)}, bf16[4,128,512]{2,1,0:T(8,128)(2,1)S(1)}, u32[]{:S(2)}, u32[]{:S(2)}) %collective-permute-start.2) | collective-permute-done | bytes 524320 | tf_op jit(solution)/shard_map/ppermute | solution.py:264
  92.5 4.4 %shard_map.54.mine = bf16[528,512]{1,0:T(8,128)(2,1)S(1)} custom-call(s32[10]{0:T(128)S(1)} %stack.47.meta, bf16[4,208,512]{2,1,0:T(8,128)(2,1)S(1)} %all_to_all.16.mine.first, bf16[4,128,512]{2,1,0:T(8,128)(2,1)S(1)} %collective-permute-done.2.other.second), custom_call_target="tpu_custom_call" | custom-call | flops 2684354560 | tf_op jit(solution)/shard_map/pallas_call | solution.py:266
  96.9 2.5 %collective-permute-start.3 = (bf16[528,512]{1,0:T(8,128)(2,1)S(1)}, bf16[528,512]{1,0:T(8,128)(2,1)S(1)}, u32[]{:S(2)}, u32[]{:S(2)}) collective-permute-start(bf16[528,512]{1,0:T(8,128)(2,1)S(1)} %shard_map.54.mine), channel_id=1, source_target_pairs={{0,32},{32,0},{64,96},{96,64},{128,160},{160,128},{192,224},{224,1... | collective-permute-start | bytes 1622024 | tf_op jit(solution)/shard_map/ppermute | solution.py:273
  99.4 1.5 %collective-permute-done.3.other = bf16[528,512]{1,0:T(8,128)(2,1)S(1)} collective-permute-done((bf16[528,512]{1,0:T(8,128)(2,1)S(1)}, bf16[528,512]{1,0:T(8,128)(2,1)S(1)}, u32[]{:S(2)}, u32[]{:S(2)}) %collective-permute-start.3) | collective-permute-done | bytes 540704 | tf_op jit(solution)/shard_map/ppermute | solution.py:273
  100.9 1.7 %shard_map.55 = bf16[4,128,512]{2,1,0:T(8,128)(2,1)S(1)} custom-call(s32[10]{0:T(128)S(1)} %stack.47.meta, bf16[528,512]{1,0:T(8,128)(2,1)S(1)} %shard_map.54.mine, bf16[528,512]{1,0:T(8,128)(2,1)S(1)} %collective-permute-done.3.other, bf16[4,208,512]{2,1,0:T(8,128)(2,1)S(1)} %all_to_all.16.mine.first, ...), custom_call_target="tpu_custom_call" | custom-call | flops 268435456 | tf_op jit(solution)/shard_map/pallas_call | solution.py:278
  102.6 11.6 %all_to_all.17.mine = bf16[4,128,512]{2,1,0:T(8,128)(2,1)S(1)} all-to-all(bf16[4,128,512]{2,1,0:T(8,128)(2,1)S(1)} %shard_map.55), channel_id=1, replica_groups={{0,64,128,192},{32,96,160,224},{256,320,384,448},{288,352,416,480},{1,6..., dimensions={0} | all-to-all | bytes 1048576 | tf_op jit(solution)/shard_map/all_to_all | solution.py:252
  114.2 3.1 %collective-permute-start.4 = (bf16[4,128,512]{2,1,0:T(8,128)(2,1)S(1)}, bf16[4,128,512]{2,1,0:T(8,128)(2,1)S(1)}, u32[]{:S(2)}, u32[]{:S(2)}) collective-permute-start(bf16[4,128,512]{2,1,0:T(8,128)(2,1)S(1)} %all_to_all.17.mine), channel_id=1, source_target_pairs={{0,32},{32,0},{64,96},{96,64},{128,160},{160,128},{192,224},{224,1... | collective-permute-start | bytes 1572872 | tf_op jit(solution)/shard_map/ppermute | solution.py:286
  117.3 2.3 %shard_map.53 = f32[512,512]{1,0:T(8,128)} custom-call(s32[10]{0:T(128)S(1)} %stack.47.meta, bf16[4,208,512]{2,1,0:T(8,128)(2,1)S(1)} %all_to_all.16.mine.first, bf16[4,128,512]{2,1,0:T(8,128)(2,1)S(1)} %collective-permute-done.2.other.second, f32[512,512]{1,0:T(8,128)S(1)} %bitcast.18), custom_call_target="tpu_custom_call" | custom-call | flops 268435456 | bytes 3145728 | tf_op jit(solution)/shard_map/pallas_call | solution.py:274
  119.6 0.0 collective-permute-done.4.other
  119.6 1.6 %shard_map.56 = bf16[2,512,512]{2,1,0:T(8,128)(2,1)} custom-call(s32[10]{0:T(128)S(1)} %stack.47.meta, bf16[4,128,512]{2,1,0:T(8,128)(2,1)S(1)} %all_to_all.17.mine, bf16[4,128,512]{2,1,0:T(8,128)(2,1)S(1)} %collective-permute-done.4.other), custom_call_target="tpu_custom_call" | custom-call | tf_op jit(solution)/shard_map/pallas_call | solution.py:287
  (1 shorter events, 0.0 us)
Async XLA Ops:
  0.6 13.0 %copy-start = (f32[1,1,512,512]{3,2,1,0:T(8,128)S(1)}, f32[1,1,512,512]{3,2,1,0:T(8,128)}, u32[]{:S(2)}) copy-start(f32[1,1,512,512]{3,2,1,0:T(8,128)} %param.4) | copy-start | bytes 3145732
  1.8 11.7 %collective-permute-start = (bf16[2,256,512]{2,1,0:T(8,128)(2,1)S(1)}, bf16[2,256,512]{2,1,0:T(8,128)(2,1)S(1)}, u32[]{:S(2)}, u32[]{:S(2)}) collective-permute-start(bf16[2,256,512]{2,1,0:T(8,128)(2,1)S(1)} %dynamic-slice_bitcast_fusion), channel_id=1, source_target_pairs={{0,32},{32,0},{64,96},{96,64},{128,160},{160,128},{192,224},{224,1... | collective-permute-start | bytes 1572872 | tf_op jit(solution)/shard_map/ppermute | solution.py:257
  4.5 0.7 copy-start.2
  13.6 1.2 %copy-start.1 = (bf16[1,2,512,512]{3,2,1,0:T(8,128)(2,1)S(1)}, bf16[1,2,512,512]{3,2,1,0:T(8,128)(2,1)}, u32[]{:S(2)}) copy-start(bf16[1,2,512,512]{3,2,1,0:T(8,128)(2,1)} %param.3) | copy-start | bytes 3145732
  32.7 39.4 %collective-permute-start.1 = (bf16[288,512]{1,0:T(8,128)(2,1)S(1)}, bf16[288,512]{1,0:T(8,128)(2,1)S(1)}, u32[]{:S(2)}, u32[]{:S(2)}) collective-permute-start(bf16[288,512]{1,0:T(8,128)(2,1)S(1)} %shard_map.51.mine), channel_id=1, source_target_pairs={{0,256},{32,288},{64,320},{96,352},{128,384},{160,416},{192,448},{... | collective-permute-start | bytes 884744 | tf_op jit(solution)/shard_map/ppermute | solution.py:261
  86.0 6.4 %collective-permute-start.2 = (bf16[4,128,512]{2,1,0:T(8,128)(2,1)S(1)}, bf16[4,128,512]{2,1,0:T(8,128)(2,1)S(1)}, u32[]{:S(2)}, u32[]{:S(2)}) collective-permute-start(bf16[4,128,512]{2,1,0:T(8,128)(2,1)S(1)} %slice.24), channel_id=1, source_target_pairs={{0,32},{32,0},{64,96},{96,64},{128,160},{160,128},{192,224},{224,1... | collective-permute-start | bytes 1572872 | tf_op jit(solution)/shard_map/ppermute | solution.py:264
  96.9 4.0 %collective-permute-start.3 = (bf16[528,512]{1,0:T(8,128)(2,1)S(1)}, bf16[528,512]{1,0:T(8,128)(2,1)S(1)}, u32[]{:S(2)}, u32[]{:S(2)}) collective-permute-start(bf16[528,512]{1,0:T(8,128)(2,1)S(1)} %shard_map.54.mine), channel_id=1, source_target_pairs={{0,32},{32,0},{64,96},{96,64},{128,160},{160,128},{192,224},{224,1... | collective-permute-start | bytes 1622024 | tf_op jit(solution)/shard_map/ppermute | solution.py:273
  114.2 5.4 %collective-permute-start.4 = (bf16[4,128,512]{2,1,0:T(8,128)(2,1)S(1)}, bf16[4,128,512]{2,1,0:T(8,128)(2,1)S(1)}, u32[]{:S(2)}, u32[]{:S(2)}) collective-permute-start(bf16[4,128,512]{2,1,0:T(8,128)(2,1)S(1)} %all_to_all.17.mine), channel_id=1, source_target_pairs={{0,32},{32,0},{64,96},{96,64},{128,160},{160,128},{192,224},{224,1... | collective-permute-start | bytes 1572872 | tf_op jit(solution)/shard_map/ppermute | solution.py:286

commit v2 on v0

v2 whole, which is shorter than its diff:
```python
import jax
import jax.numpy as jnp
from jax import lax
from jax.experimental import pallas as pl
from jax.experimental.pallas import tpu as pltpu
from jax.sharding import PartitionSpec as P

BETA = 0.9
DAMPING = 0.0001
BS = 512
HALF = 256
CHUNK = 128
STAT = CHUNK + 16
ROWS = CHUNK + STAT
LIMIT = 32 * 1024 * 1024

BF = jnp.bfloat16
F32 = jnp.float32

VM = pl.BlockSpec(memory_space=pltpu.VMEM)
SM = pl.BlockSpec(memory_space=pltpu.SMEM)
SQUARE = pltpu.VMEM((BS, BS), BF)


def call(kernel, shapes, specs, scratch=(), flops=0, nbytes=0):
    many = isinstance(shapes, tuple)
    return pl.pallas_call(
        kernel,
        out_shape=shapes,
        in_specs=specs,
        out_specs=(VM,) * len(shapes) if many else VM,
        scratch_shapes=list(scratch),
        compiler_params=pltpu.CompilerParams(vmem_limit_bytes=LIMIT),
        cost_estimate=pl.CostEstimate(flops=flops, bytes_accessed=nbytes, transcendentals=0),
    )


def array(*shape, dtype=BF):
    return jax.ShapeDtypeStruct(shape, dtype)


def place():
    group = lax.axis_index("group")
    return lax.rem(group, 2), lax.rem(lax.div(group, 2), 4), lax.div(group, 8)


def rows_at(core, chunk):
    return pl.ds(pl.multiple_of(core * HALF + chunk * CHUNK, CHUNK), CHUNK)


def mm(a, b):
    return jnp.dot(a.astype(BF), b.astype(BF), preferred_element_type=F32)


def grid_of(n):
    return lax.broadcasted_iota(jnp.int32, (n, n), 0), lax.broadcasted_iota(jnp.int32, (n, n), 1)


def first_kernel(grad, got, stat, out):
    core, _, _ = place()
    for y in range(4):
        mine = grad[y // 2, rows_at(core, y % 2), :].astype(F32)
        other = got[y // 2, (y % 2) * CHUNK : (y % 2 + 1) * CHUNK, :].astype(F32)
        out[y, 0:CHUNK, :] = (mine + other).astype(BF)
    row, col = grid_of(HALF)
    corner = stat[HALF:BS, HALF:BS]
    fold = jnp.where(row <= col, stat[0:HALF, 0:HALF], corner).astype(BF)
    diagonal = jnp.sum(jnp.where(row == col, corner, 0.0), axis=0, keepdims=True)
    diagonal = jnp.broadcast_to(diagonal, (16, HALF)).astype(BF)
    side = stat[0:HALF, HALF:BS].astype(BF)
    for y in range(4):
        lo = (y % 2) * CHUNK
        out[y, CHUNK : 2 * CHUNK, 0:HALF] = fold[lo : lo + CHUNK]
        out[y, CHUNK : 2 * CHUNK, HALF:BS] = side[lo : lo + CHUNK]
        out[y, 2 * CHUNK : ROWS, 0:HALF] = diagonal
        out[y, 2 * CHUNK : ROWS, HALF:BS] = diagonal


def unpack(packed, diagonal, stat):
    row, col = grid_of(HALF)
    fold = packed[:, 0:HALF].astype(F32)
    turned = fold.T
    stat[0:HALF, 0:HALF] = jnp.where(row <= col, fold, turned)
    stat[HALF:BS, HALF:BS] = jnp.where(row > col, fold, jnp.where(row < col, turned, diagonal))
    side = packed[:, HALF:BS].astype(F32)
    stat[0:HALF, HALF:BS] = side
    stat[HALF:BS, 0:HALF] = side.T


def second_kernel(owner, got, out):
    _, y, _ = place()
    total = got[0, 0:CHUNK, :].astype(F32)
    for source in range(1, 4):
        total += got[source, 0:CHUNK, :].astype(F32)
    out[0:CHUNK, :] = total.astype(BF)
    pair = owner[lax.axis_index("dp"), lax.div(y, 2)]
    out[CHUNK:ROWS, :] = got[lax.rem(pair, 4), CHUNK:ROWS, :]


def third_kernel(owner, mine, got, out):
    _, y, half = place()
    out[0:CHUNK, :] = (mine[0:CHUNK, :].astype(F32) + got[0:CHUNK, :].astype(F32)).astype(BF)
    here = lax.div(owner[lax.axis_index("dp"), lax.div(y, 2)], 4) == half

    @pl.when(here)
    def _():
        out[CHUNK:ROWS, :] = mine[CHUNK:ROWS, :]

    @pl.when(jnp.logical_not(here))
    def _():
        out[CHUNK:ROWS, :] = got[CHUNK:ROWS, :]


def gram_of(core, dense, oriented):
    @pl.when(core == 0)
    def _():
        oriented[...] = dense[...]

    @pl.when(core == 1)
    def _():
        oriented[...] = dense[...].astype(F32).T.astype(BF)

    value = oriented[...]
    return lax.dot_general(value, value, (((1,), (1,)), ((), ())), preferred_element_type=F32)


def newton(current):
    low = current.astype(BF)
    square = (1.0 / 16) * mm(low, low) - (10.0 / 16) * current
    slow = square.astype(BF)
    fourth = (50.0 / 16) * square + mm(slow, slow)
    return (625.0 / 256) * current + mm(fourth, low)


def root_kernel(mine, near, far, out, dense, oriented, packed, stat):
    core, y, _ = place()
    chunk = lax.rem(y, 2)
    dense[rows_at(core, chunk), :] = mine[0:CHUNK, :]
    dense[rows_at(core, 1 - chunk), :] = near[0:CHUNK, :]
    dense[rows_at(1 - core, chunk), :] = far[0]
    dense[rows_at(1 - core, 1 - chunk), :] = far[1]
    packed[rows_at(0, chunk), :] = mine[CHUNK : 2 * CHUNK, :]
    packed[rows_at(0, 1 - chunk), :] = near[CHUNK : 2 * CHUNK, :]
    unpack(packed, mine[2 * CHUNK : ROWS, 0:HALF].astype(F32)[0:1, :], stat)
    gram = gram_of(core, dense, oriented)
    row, col = grid_of(BS)
    shifted = BETA * stat[...] + (1.0 - BETA) * gram + jnp.where(row == col, DAMPING, 0.0)
    frob = jnp.sqrt(jnp.sum(shifted * shifted, keepdims=True))
    m0 = shifted * (1.0 / frob)
    m1 = newton(m0)
    m2 = newton(m1)
    n01 = (-1.25 / 4) * (m0 + m1) + (1.0 / 16) * mm(m0, m1)
    excess = 1.25 * n01 - (1.5625 / 4) * m2 - 0.25 * mm(n01, m2)
    scale = lax.rsqrt(jnp.sqrt(frob))

    @pl.when(core == 0)
    def _():
        block = dense[...]
        out[0:BS, :] = (scale * (1.953125 * block.astype(F32) + mm(excess, block))).astype(BF)
        out[BS : BS + 16, :] = jnp.zeros((16, BS), BF)

    @pl.when(core == 1)
    def _():
        out[0:BS, :] = excess.astype(BF)
        value = jnp.broadcast_to(scale, (16, BS))
        high = value.astype(BF).astype(F32)
        middle = (value - high).astype(BF).astype(F32)
        low = value - high - middle
        line = lax.broadcasted_iota(jnp.int32, (16, BS), 0)
        out[BS : BS + 16, :] = jnp.where(line == 0, high, jnp.where(line == 1, middle, low)).astype(BF)


def product_kernel(mine, other, dense, out, half_rows, left, right):
    core, _, _ = place()

    @pl.when(core == 0)
    def _():
        left[...] = mine[...]
        right[...] = other[...]

    @pl.when(core == 1)
    def _():
        left[...] = other[...]
        right[...] = mine[...]

    tail = right[BS : BS + 16, :].astype(F32)
    scale = tail[0:1, 0:1] + tail[1:2, 0:1] + tail[2:3, 0:1]
    low = left[0:BS, :]
    precond = scale * (1.953125 * low.astype(F32) + mm(low, right[0:BS, :]))
    value = dense[...].astype(F32)
    grad_sq = jnp.sum(value * value, keepdims=True)
    pre_sq = jnp.sum(precond * precond, keepdims=True)
    out[...] = (precond * jnp.sqrt(grad_sq / (pre_sq + 1e-06))).astype(BF)
    half_rows[...] = out[pl.ds(pl.multiple_of(core * HALF, HALF), HALF), :]


def stat_kernel(owner, dense, away, far, stat, out, chosen, oriented):
    core, y, half = place()
    column = lax.axis_index("dp")
    pair = half * 4 + y
    block = lax.div(y, 2)
    same = owner[column, block] == pair
    cross = owner[column, 1 - block] == pair

    @pl.when(same)
    def _():
        chosen[...] = dense[...]

    @pl.when(cross)
    def _():
        chunk = 1 - lax.rem(y, 2)
        chosen[rows_at(core, chunk), :] = away[0]
        chosen[rows_at(core, 1 - chunk), :] = away[1]
        chosen[rows_at(1 - core, chunk), :] = far[0]
        chosen[rows_at(1 - core, 1 - chunk), :] = far[1]

    active = jnp.logical_or(same, cross)

    @pl.when(active)
    def _():
        out[...] = BETA * stat[...] + (1.0 - BETA) * gram_of(core, chosen, oriented)

    @pl.when(jnp.logical_not(active))
    def _():
        out[...] = stat[...]


def last_kernel(mine, away, far, out):
    core, y, _ = place()
    block = lax.div(y, 2)
    out[block] = mine[...]
    out[1 - block, pl.ds(pl.multiple_of(core * HALF, HALF), HALF), :] = away[...]
    out[1 - block, pl.ds(pl.multiple_of((1 - core) * HALF, HALF), HALF), :] = far[...]


def body(grad, stats, owner):
    core = lax.axis_index("group") % 2
    along_y = [[h * 8 + 2 * k + c for k in range(4)] for h in range(2) for c in range(2)]

    def send(value, change):
        return lax.ppermute(value, "group", [(g, change(g)) for g in range(16)])

    def to_core(value):
        return send(value, lambda g: g ^ 1)

    def to_mate(value):
        return send(value, lambda g: g ^ 2)

    def to_mirror(value):
        return send(value, lambda g: g ^ 6)

    def to_half(value):
        return send(value, lambda g: g ^ 8)

    block = grad[0]
    stat = stats[0, 0]
    got = to_core(lax.dynamic_slice_in_dim(block, (1 - core) * HALF, HALF, 1))
    parts = call(first_kernel, array(4, ROWS, BS), [VM, VM, VM])(block, got, stat)
    parts = lax.all_to_all(parts, "group", 0, 0, tiled=True, axis_index_groups=along_y)
    mine = call(second_kernel, array(ROWS, BS), [SM, VM])(owner, parts)
    got = to_half(mine)
    mine = call(third_kernel, array(ROWS, BS), [SM, VM, VM])(owner, mine, got)
    near = to_mate(mine)
    both = jnp.stack([mine[:CHUNK], near[:CHUNK]])
    far = to_core(both)
    away = to_mirror(both)
    payload, dense = call(
        root_kernel,
        (array(BS + 16, BS), array(BS, BS)),
        [VM, VM, VM],
        [SQUARE, pltpu.VMEM((HALF, BS), BF), pltpu.VMEM((BS, BS), F32)],
        flops=10 * 2 * BS**3,
    )(mine, near, far)
    received = to_core(payload)
    away_far = to_core(away)
    tall = pltpu.VMEM((BS + 16, BS), BF)
    result, half_rows = call(
        product_kernel, (array(BS, BS), array(HALF, BS)), [VM, VM, VM], [tall, tall], flops=2 * BS**3
    )(payload, received, dense)
    mirror = to_mirror(half_rows)
    new_stat = call(
        stat_kernel,
        array(BS, BS, dtype=F32),
        [SM, VM, VM, VM, VM],
        [SQUARE, SQUARE],
        flops=2 * BS**3,
        nbytes=3 << 20,
    )(owner, dense, away, away_far, stat)
    update = call(last_kernel, array(2, BS, BS), [VM, VM, VM])(result, mirror, to_core(mirror))
    return (new_stat[None, None], update)


def solution(mesh):
    in_specs = (P("group", "dp", None, None), P("group", "dp", None, None), P())
    out_specs = (P("group", "dp", None, None), P("dp", None, None))
    return jax.shard_map(body, mesh=mesh, in_specs=in_specs, out_specs=out_specs, check_vma=False)
```

time: 589 us -> 112 us (0.19)
  the two profiles are of different devices: /device:TPU:1 before, /device:TPU:37 now
where the time goes in v2:
time: 112 us
  waiting for transfers between devices  54 us (48%)
  starting transfers between devices  42.9 us (38%)
  Pallas kernels  11.6 us (10%)
  local copies, waits for them, and re-layouts  2.51 us (2%)
    ppermute x9, waiting for transfers between devices, send(): return lax.ppermute(value, 'group', [(g, change(g)) for g in range(16)])  38.8 us
    ppermute x9, starting transfers between devices, send(): return lax.ppermute(value, 'group', [(g, change(g)) for g in range(16)])  38.6 us
    all_to_all x1, waiting for transfers between devices, body(): lax.all_to_all(parts, 'group', 0, 0, tiled=True, axis_index_groups=along_y)  15.1 us
    all_to_all x1, starting transfers between devices, body(): lax.all_to_all(parts, 'group', 0, 0, tiled=True, axis_index_groups=along_y)  4.31 us
    pallas_call x1, Pallas kernels, body(): call(root_kernel, (array(BS + 16, BS), array(BS, BS)), [VM, VM, VM], [SQU...  3.96 us
    pallas_call x1, Pallas kernels, body(): call(stat_kernel, array(BS, BS, dtype=F32), [SM, VM, VM, VM, VM], [SQUARE...  2.6 us
  transfers between devices with their start and end apart: 10, of which 7 were waited for; matrix products, arithmetic and copies ran while one was open for 0% of the time, Pallas kernels for 3%

profile of v2, /device:TPU:37, one launch (start us, length us, event | category | flops | bytes accessed | tf_op | source)
XLA Modules:
  0.0 111.8 jit_solution(5923391744184061452)
XLA Ops:
  0.6 0.0 copy-start
  0.7 1.2 %dynamic-slice_bitcast_fusion = bf16[2,256,512]{2,1,0:T(8,128)(2,1)S(1)} fusion(bf16[1,2,512,512]{3,2,1,0:T(8,128)(2,1)} %param.3, s32[]{:T(128)S(6)} %select_n.11), kind=kLoop, calls=%fused_computation | loop fusion | bytes 1048580 | tf_op jit(solution)/shard_map/dynamic_slice | solution.py:257
  1.8 2.6 %collective-permute-start = (bf16[2,256,512]{2,1,0:T(8,128)(2,1)S(1)}, bf16[2,256,512]{2,1,0:T(8,128)(2,1)S(1)}, u32[]{:S(2)}, u32[]{:S(2)}) collective-permute-start(bf16[2,256,512]{2,1,0:T(8,128)(2,1)S(1)} %dynamic-slice_bitcast_fusion), channel_id=1, source_target_pairs={{0,32},{32,0},{64,96},{96,64},{128,160},{160,128},{192,224},{224,1... | collective-permute-start | bytes 1572872 | tf_op jit(solution)/shard_map/ppermute | solution.py:241
  4.4 1.5 %collective-permute-done.got = bf16[2,256,512]{2,1,0:T(8,128)(2,1)S(1)} collective-permute-done((bf16[2,256,512]{2,1,0:T(8,128)(2,1)S(1)}, bf16[2,256,512]{2,1,0:T(8,128)(2,1)S(1)}, u32[]{:S(2)}, u32[]{:S(2)}) %collective-permute-start) | collective-permute-done | bytes 524320 | tf_op jit(solution)/shard_map/ppermute | solution.py:241
  5.9 0.0 copy-done
  5.9 0.0 copy-start.1
  5.9 1.2 %copy-done.1 = bf16[1,2,512,512]{3,2,1,0:T(8,128)(2,1)S(1)} copy-done((bf16[1,2,512,512]{3,2,1,0:T(8,128)(2,1)S(1)}, bf16[1,2,512,512]{3,2,1,0:T(8,128)(2,1)}, u32[]{:S(2)}) %copy-start.1) | copy-done | bytes 1048600
  7.2 1.2 %shard_map.50 = bf16[4,272,512]{2,1,0:T(8,128)(2,1)} custom-call(bf16[2,512,512]{2,1,0:T(8,128)(2,1)S(1)} %bitcast.11, bf16[2,256,512]{2,1,0:T(8,128)(2,1)S(1)} %collective-permute-done.got, f32[512,512]{1,0:T(8,128)S(1)} %bitcast.9), custom_call_target="tpu_custom_call" | custom-call | tf_op jit(solution)/shard_map/pallas_call | solution.py:258
  8.3 0.0 copy-start.2
  8.3 4.3 %all-to-all-start = ((bf16[4,272,512]{2,1,0:T(8,128)(2,1)}), bf16[4,272,512]{2,1,0:T(8,128)(2,1)S(1)}, u32[]{:S(2)}, u32[]{:S(2)}) async-start(bf16[4,272,512]{2,1,0:T(8,128)(2,1)} %shard_map.50), calls=%async_computation | async-start | bytes 2228224 | tf_op jit(solution)/shard_map/all_to_all | solution.py:259
  12.7 0.0 copy-done.2
  12.7 0.1 copy.7.owner
  12.7 15.1 %all-to-all-done.got = bf16[4,272,512]{2,1,0:T(8,128)(2,1)S(1)} async-done(((bf16[4,272,512]{2,1,0:T(8,128)(2,1)}), bf16[4,272,512]{2,1,0:T(8,128)(2,1)S(1)}, u32[]{:S(2)}, u32[]{:S(2)}) %all-to-all-start) | async-done | bytes 1114144 | tf_op jit(solution)/shard_map/all_to_all | solution.py:259
  27.9 0.9 shard_map.51.mine
  28.8 14.5 %collective-permute-start.1 = (bf16[272,512]{1,0:T(8,128)(2,1)S(1)}, bf16[272,512]{1,0:T(8,128)(2,1)S(1)}, u32[]{:S(2)}, u32[]{:S(2)}) collective-permute-start(bf16[272,512]{1,0:T(8,128)(2,1)S(1)} %shard_map.51.mine), channel_id=1, source_target_pairs={{0,256},{32,288},{64,320},{96,352},{128,384},{160,416},{192,448},{... | collective-permute-start | bytes 835592 | tf_op jit(solution)/shard_map/ppermute | solution.py:241
  43.3 24.1 %collective-permute-done.1.got = bf16[272,512]{1,0:T(8,128)(2,1)S(1)} collective-permute-done((bf16[272,512]{1,0:T(8,128)(2,1)S(1)}, bf16[272,512]{1,0:T(8,128)(2,1)S(1)}, u32[]{:S(2)}, u32[]{:S(2)}) %collective-permute-start.1) | collective-permute-done | bytes 278560 | tf_op jit(solution)/shard_map/ppermute | solution.py:241
  67.4 0.8 shard_map.52.mine
  68.2 2.2 %collective-permute-start.2 = (bf16[272,512]{1,0:T(8,128)(2,1)S(1)}, bf16[272,512]{1,0:T(8,128)(2,1)S(1)}, u32[]{:S(2)}, u32[]{:S(2)}) collective-permute-start(bf16[272,512]{1,0:T(8,128)(2,1)S(1)} %shard_map.52.mine), channel_id=1, source_target_pairs={{0,64},{32,96},{64,0},{96,32},{128,192},{160,224},{192,128},{224,1... | collective-permute-start | bytes 835592 | tf_op jit(solution)/shard_map/ppermute | solution.py:241
  70.4 6.2 %collective-permute-done.2.near = bf16[272,512]{1,0:T(8,128)(2,1)S(1)} collective-permute-done((bf16[272,512]{1,0:T(8,128)(2,1)S(1)}, bf16[272,512]{1,0:T(8,128)(2,1)S(1)}, u32[]{:S(2)}, u32[]{:S(2)}) %collective-permute-start.2) | collective-permute-done | bytes 278560 | tf_op jit(solution)/shard_map/ppermute | solution.py:241
  76.7 4.5 %collective-permute-start.3 = (bf16[2,128,512]{2,1,0:T(8,128)(2,1)S(1)}, bf16[2,128,512]{2,1,0:T(8,128)(2,1)S(1)}, u32[]{:S(2)}, u32[]{:S(2)}) collective-permute-start(bf16[2,128,512]{2,1,0:T(8,128)(2,1)S(1)} %pad_maximum_fusion), channel_id=1, source_target_pairs={{0,32},{32,0},{64,96},{96,64},{128,160},{160,128},{192,224},{224,1... | collective-permute-start | bytes 786440 | tf_op jit(solution)/shard_map/ppermute | solution.py:241
  81.2 1.1 %collective-permute-done.3.far = bf16[2,128,512]{2,1,0:T(8,128)(2,1)S(1)} collective-permute-done((bf16[2,128,512]{2,1,0:T(8,128)(2,1)S(1)}, bf16[2,128,512]{2,1,0:T(8,128)(2,1)S(1)}, u32[]{:S(2)}, u32[]{:S(2)}) %collective-permute-start.3) | collective-permute-done | bytes 262176 | tf_op jit(solution)/shard_map/ppermute | solution.py:241
  82.3 4.0 %shard_map.53 = (bf16[528,512]{1,0:T(8,128)(2,1)S(1)}, bf16[512,512]{1,0:T(8,128)(2,1)S(1)}) custom-call(bf16[272,512]{1,0:T(8,128)(2,1)S(1)} %shard_map.52.mine, bf16[272,512]{1,0:T(8,128)(2,1)S(1)} %collective-permute-done.2.near, bf16[2,128,512]{2,1,0:T(8,128)(2,1)S(1)} %collective-permute-done.3.far), custom_call_target="tpu_custom_call" | custom-call | flops 2684354560 | tf_op jit(solution)/shard_map/pallas_call | solution.py:267
  86.3 2.5 %collective-permute-start.6 = (bf16[528,512]{1,0:T(8,128)(2,1)S(1)}, bf16[528,512]{1,0:T(8,128)(2,1)S(1)}, u32[]{:S(2)}, u32[]{:S(2)}) collective-permute-start(bf16[528,512]{1,0:T(8,128)(2,1)S(1)} %get-tuple-element.7.mine), channel_id=1, source_target_pairs={{0,32},{32,0},{64,96},{96,64},{128,160},{160,128},{192,224},{224,1... | collective-permute-start | bytes 1622024 | tf_op jit(solution)/shard_map/ppermute | solution.py:241
  88.8 2.8 %collective-permute-start.4 = (bf16[2,128,512]{2,1,0:T(8,128)(2,1)S(1)}, bf16[2,128,512]{2,1,0:T(8,128)(2,1)S(1)}, u32[]{:S(2)}, u32[]{:S(2)}) collective-permute-start(bf16[2,128,512]{2,1,0:T(8,128)(2,1)S(1)} %pad_maximum_fusion), channel_id=1, source_target_pairs={{0,192},{32,224},{64,128},{96,160},{128,64},{160,96},{192,0},{224,... | collective-permute-start | bytes 786440 | tf_op jit(solution)/shard_map/ppermute | solution.py:241
  91.6 0.0 collective-permute-done.6.other
  91.6 1.1 shard_map.55
  92.7 3.7 %collective-permute-start.7 = (bf16[256,512]{1,0:T(8,128)(2,1)S(1)}, bf16[256,512]{1,0:T(8,128)(2,1)S(1)}, u32[]{:S(2)}, u32[]{:S(2)}) collective-permute-start(bf16[256,512]{1,0:T(8,128)(2,1)S(1)} %get-tuple-element.9), channel_id=1, source_target_pairs={{0,192},{32,224},{64,128},{96,160},{128,64},{160,96},{192,0},{224,... | collective-permute-start | bytes 786440 | tf_op jit(solution)/shard_map/ppermute | solution.py:241
  96.4 3.4 %collective-permute-done.4.away = bf16[2,128,512]{2,1,0:T(8,128)(2,1)S(1)} collective-permute-done((bf16[2,128,512]{2,1,0:T(8,128)(2,1)S(1)}, bf16[2,128,512]{2,1,0:T(8,128)(2,1)S(1)}, u32[]{:S(2)}, u32[]{:S(2)}) %collective-permute-start.4) | collective-permute-done | bytes 262176 | tf_op jit(solution)/shard_map/ppermute | solution.py:241
  99.8 3.1 %collective-permute-start.5 = (bf16[2,128,512]{2,1,0:T(8,128)(2,1)S(1)}, bf16[2,128,512]{2,1,0:T(8,128)(2,1)S(1)}, u32[]{:S(2)}, u32[]{:S(2)}) collective-permute-start(bf16[2,128,512]{2,1,0:T(8,128)(2,1)S(1)} %collective-permute-done.4.away), channel_id=1, source_target_pairs={{0,32},{32,0},{64,96},{96,64},{128,160},{160,128},{192,224},{224,1... | collective-permute-start | bytes 786440 | tf_op jit(solution)/shard_map/ppermute | solution.py:241
  102.9 2.5 %collective-permute-done.7.away = bf16[256,512]{1,0:T(8,128)(2,1)S(1)} collective-permute-done((bf16[256,512]{1,0:T(8,128)(2,1)S(1)}, bf16[256,512]{1,0:T(8,128)(2,1)S(1)}, u32[]{:S(2)}, u32[]{:S(2)}) %collective-permute-start.7) | collective-permute-done | bytes 262176 | tf_op jit(solution)/shard_map/ppermute | solution.py:241
  105.4 2.7 %collective-permute-start.8 = (bf16[256,512]{1,0:T(8,128)(2,1)S(1)}, bf16[256,512]{1,0:T(8,128)(2,1)S(1)}, u32[]{:S(2)}, u32[]{:S(2)}) collective-permute-start(bf16[256,512]{1,0:T(8,128)(2,1)S(1)} %collective-permute-done.7.away), channel_id=1, source_target_pairs={{0,32},{32,0},{64,96},{96,64},{128,160},{160,128},{192,224},{224,1... | collective-permute-start | bytes 786440 | tf_op jit(solution)/shard_map/ppermute | solution.py:241
  108.1 0.0 collective-permute-done.5.far
  108.1 2.6 %shard_map.54 = f32[512,512]{1,0:T(8,128)} custom-call(s32[32,2]{1,0:T(8,128)S(1)} %copy.7.owner, bf16[512,512]{1,0:T(8,128)(2,1)S(1)} %get-tuple-element.6.dense, bf16[2,128,512]{2,1,0:T(8,128)(2,1)S(1)} %collective-permute-done.4.away, bf16[2,128,512]{2,1,0:T(8,128)(2,1)S(1)} %collective-permute-done.5.far, f32[512,512]{1,0:T(8,128)S(1)} %bitcast.10), custom_call_target="tpu_custom_call" | custom-call | flops 268435456 | bytes 3145728 | tf_op jit(solution)/shard_map/pallas_call | solution.py:281
  110.7 0.0 collective-permute-done.8.far
  110.7 1.1 shard_map.56
  (3 shorter events, 0.0 us)
Async XLA Ops:
  0.6 5.3 %copy-start = (f32[1,1,512,512]{3,2,1,0:T(8,128)S(1)}, f32[1,1,512,512]{3,2,1,0:T(8,128)}, u32[]{:S(2)}) copy-start(f32[1,1,512,512]{3,2,1,0:T(8,128)} %param.4) | copy-start | bytes 3145732
  1.8 4.1 %collective-permute-start = (bf16[2,256,512]{2,1,0:T(8,128)(2,1)S(1)}, bf16[2,256,512]{2,1,0:T(8,128)(2,1)S(1)}, u32[]{:S(2)}, u32[]{:S(2)}) collective-permute-start(bf16[2,256,512]{2,1,0:T(8,128)(2,1)S(1)} %dynamic-slice_bitcast_fusion), channel_id=1, source_target_pairs={{0,32},{32,0},{64,96},{96,64},{128,160},{160,128},{192,224},{224,1... | collective-permute-start | bytes 1572872 | tf_op jit(solution)/shard_map/ppermute | solution.py:241
  5.9 1.2 %copy-start.1 = (bf16[1,2,512,512]{3,2,1,0:T(8,128)(2,1)S(1)}, bf16[1,2,512,512]{3,2,1,0:T(8,128)(2,1)}, u32[]{:S(2)}) copy-start(bf16[1,2,512,512]{3,2,1,0:T(8,128)(2,1)} %param.3) | copy-start | bytes 3145732
  8.3 4.3 %copy-start.2 = (s32[32,2]{0,1:T(2,128)S(1)}, s32[32,2]{0,1:T(2,128)}, u32[]{:S(2)}) copy-start(s32[32,2]{0,1:T(2,128)} %param.5) | copy-start | bytes 772
  8.3 19.5 %all-to-all-start = ((bf16[4,272,512]{2,1,0:T(8,128)(2,1)}), bf16[4,272,512]{2,1,0:T(8,128)(2,1)S(1)}, u32[]{:S(2)}, u32[]{:S(2)}) async-start(bf16[4,272,512]{2,1,0:T(8,128)(2,1)} %shard_map.50), calls=%async_computation | async-start | bytes 2228224 | tf_op jit(solution)/shard_map/all_to_all | solution.py:259
  28.8 38.6 %collective-permute-start.1 = (bf16[272,512]{1,0:T(8,128)(2,1)S(1)}, bf16[272,512]{1,0:T(8,128)(2,1)S(1)}, u32[]{:S(2)}, u32[]{:S(2)}) collective-permute-start(bf16[272,512]{1,0:T(8,128)(2,1)S(1)} %shard_map.51.mine), channel_id=1, source_target_pairs={{0,256},{32,288},{64,320},{96,352},{128,384},{160,416},{192,448},{... | collective-permute-start | bytes 835592 | tf_op jit(solution)/shard_map/ppermute | solution.py:241
  68.2 8.4 %collective-permute-start.2 = (bf16[272,512]{1,0:T(8,128)(2,1)S(1)}, bf16[272,512]{1,0:T(8,128)(2,1)S(1)}, u32[]{:S(2)}, u32[]{:S(2)}) collective-permute-start(bf16[272,512]{1,0:T(8,128)(2,1)S(1)} %shard_map.52.mine), channel_id=1, source_target_pairs={{0,64},{32,96},{64,0},{96,32},{128,192},{160,224},{192,128},{224,1... | collective-permute-start | bytes 835592 | tf_op jit(solution)/shard_map/ppermute | solution.py:241
  76.7 5.6 %collective-permute-start.3 = (bf16[2,128,512]{2,1,0:T(8,128)(2,1)S(1)}, bf16[2,128,512]{2,1,0:T(8,128)(2,1)S(1)}, u32[]{:S(2)}, u32[]{:S(2)}) collective-permute-start(bf16[2,128,512]{2,1,0:T(8,128)(2,1)S(1)} %pad_maximum_fusion), channel_id=1, source_target_pairs={{0,32},{32,0},{64,96},{96,64},{128,160},{160,128},{192,224},{224,1... | collective-permute-start | bytes 786440 | tf_op jit(solution)/shard_map/ppermute | solution.py:241
  86.3 5.3 %collective-permute-start.6 = (bf16[528,512]{1,0:T(8,128)(2,1)S(1)}, bf16[528,512]{1,0:T(8,128)(2,1)S(1)}, u32[]{:S(2)}, u32[]{:S(2)}) collective-permute-start(bf16[528,512]{1,0:T(8,128)(2,1)S(1)} %get-tuple-element.7.mine), channel_id=1, source_target_pairs={{0,32},{32,0},{64,96},{96,64},{128,160},{160,128},{192,224},{224,1... | collective-permute-start | bytes 1622024 | tf_op jit(solution)/shard_map/ppermute | solution.py:241
  88.8 11.0 %collective-permute-start.4 = (bf16[2,128,512]{2,1,0:T(8,128)(2,1)S(1)}, bf16[2,128,512]{2,1,0:T(8,128)(2,1)S(1)}, u32[]{:S(2)}, u32[]{:S(2)}) collective-permute-start(bf16[2,128,512]{2,1,0:T(8,128)(2,1)S(1)} %pad_maximum_fusion), channel_id=1, source_target_pairs={{0,192},{32,224},{64,128},{96,160},{128,64},{160,96},{192,0},{224,... | collective-permute-start | bytes 786440 | tf_op jit(solution)/shard_map/ppermute | solution.py:241
  92.7 12.7 %collective-permute-start.7 = (bf16[256,512]{1,0:T(8,128)(2,1)S(1)}, bf16[256,512]{1,0:T(8,128)(2,1)S(1)}, u32[]{:S(2)}, u32[]{:S(2)}) collective-permute-start(bf16[256,512]{1,0:T(8,128)(2,1)S(1)} %get-tuple-element.9), channel_id=1, source_target_pairs={{0,192},{32,224},{64,128},{96,160},{128,64},{160,96},{192,0},{224,... | collective-permute-start | bytes 786440 | tf_op jit(solution)/shard_map/ppermute | solution.py:241
  99.8 8.3 %collective-permute-start.5 = (bf16[2,128,512]{2,1,0:T(8,128)(2,1)S(1)}, bf16[2,128,512]{2,1,0:T(8,128)(2,1)S(1)}, u32[]{:S(2)}, u32[]{:S(2)}) collective-permute-start(bf16[2,128,512]{2,1,0:T(8,128)(2,1)S(1)} %collective-permute-done.4.away), channel_id=1, source_target_pairs={{0,32},{32,0},{64,96},{96,64},{128,160},{160,128},{192,224},{224,1... | collective-permute-start | bytes 786440 | tf_op jit(solution)/shard_map/ppermute | solution.py:241
  105.4 5.3 %collective-permute-start.8 = (bf16[256,512]{1,0:T(8,128)(2,1)S(1)}, bf16[256,512]{1,0:T(8,128)(2,1)S(1)}, u32[]{:S(2)}, u32[]{:S(2)}) collective-permute-start(bf16[256,512]{1,0:T(8,128)(2,1)S(1)} %collective-permute-done.7.away), channel_id=1, source_target_pairs={{0,32},{32,0},{64,96},{96,64},{128,160},{160,128},{192,224},{224,1... | collective-permute-start | bytes 786440 | tf_op jit(solution)/shard_map/ppermute | solution.py:241

commit v3 on v2

--- a/solution.py
+++ b/solution.py
@@ -44,8 +44,8 @@
     return lax.rem(group, 2), lax.rem(lax.div(group, 2), 4), lax.div(group, 8)
 
 
-def rows_at(core, chunk):
-    return pl.ds(pl.multiple_of(core * HALF + chunk * CHUNK, CHUNK), CHUNK)
+def half_at(core):
+    return pl.ds(pl.multiple_of(core * HALF, HALF), HALF)
 
 
 def mm(a, b):
@@ -56,24 +56,26 @@
     return lax.broadcasted_iota(jnp.int32, (n, n), 0), lax.broadcasted_iota(jnp.int32, (n, n), 1)
 
 
-def first_kernel(grad, got, stat, out):
-    core, _, _ = place()
-    for y in range(4):
-        mine = grad[y // 2, rows_at(core, y % 2), :].astype(F32)
-        other = got[y // 2, (y % 2) * CHUNK : (y % 2 + 1) * CHUNK, :].astype(F32)
-        out[y, 0:CHUNK, :] = (mine + other).astype(BF)
+def pack_kernel(stat, out):
     row, col = grid_of(HALF)
     corner = stat[HALF:BS, HALF:BS]
     fold = jnp.where(row <= col, stat[0:HALF, 0:HALF], corner).astype(BF)
     diagonal = jnp.sum(jnp.where(row == col, corner, 0.0), axis=0, keepdims=True)
     diagonal = jnp.broadcast_to(diagonal, (16, HALF)).astype(BF)
     side = stat[0:HALF, HALF:BS].astype(BF)
+    for chunk in range(2):
+        lo = chunk * CHUNK
+        out[chunk, 0:CHUNK, 0:HALF] = fold[lo : lo + CHUNK]
+        out[chunk, 0:CHUNK, HALF:BS] = side[lo : lo + CHUNK]
+        out[chunk, CHUNK:STAT, 0:HALF] = diagonal
+        out[chunk, CHUNK:STAT, HALF:BS] = diagonal
+
+
+def first_kernel(keep, got, packed, out):
     for y in range(4):
-        lo = (y % 2) * CHUNK
-        out[y, CHUNK : 2 * CHUNK, 0:HALF] = fold[lo : lo + CHUNK]
-        out[y, CHUNK : 2 * CHUNK, HALF:BS] = side[lo : lo + CHUNK]
-        out[y, 2 * CHUNK : ROWS, 0:HALF] = diagonal
-        out[y, 2 * CHUNK : ROWS, HALF:BS] = diagonal
+        rows = slice((y % 2) * CHUNK, (y % 2 + 1) * CHUNK)
+        out[y, 0:CHUNK, :] = (keep[y // 2, rows, :].astype(F32) + got[y // 2, rows, :].astype(F32)).astype(BF)
+        out[y, CHUNK:ROWS, :] = packed[y % 2]
 
 
 def unpack(packed, diagonal, stat):
@@ -97,18 +99,11 @@
     out[CHUNK:ROWS, :] = got[lax.rem(pair, 4), CHUNK:ROWS, :]
 
 
-def third_kernel(owner, mine, got, out):
-    _, y, half = place()
-    out[0:CHUNK, :] = (mine[0:CHUNK, :].astype(F32) + got[0:CHUNK, :].astype(F32)).astype(BF)
-    here = lax.div(owner[lax.axis_index("dp"), lax.div(y, 2)], 4) == half
-
-    @pl.when(here)
-    def _():
-        out[CHUNK:ROWS, :] = mine[CHUNK:ROWS, :]
-
-    @pl.when(jnp.logical_not(here))
-    def _():
-        out[CHUNK:ROWS, :] = got[CHUNK:ROWS, :]
+def third_kernel(owner, got, out):
+    _, y, _ = place()
+    out[0:CHUNK, :] = (got[0, 0:CHUNK, :].astype(F32) + got[1, 0:CHUNK, :].astype(F32)).astype(BF)
+    pair = owner[lax.axis_index("dp"), lax.div(y, 2)]
+    out[CHUNK:ROWS, :] = got[lax.div(pair, 4), CHUNK:ROWS, :]
 
 
 def gram_of(core, dense, oriented):
@@ -132,16 +127,11 @@
     return (625.0 / 256) * current + mm(fourth, low)
 
 
-def root_kernel(mine, near, far, out, dense, oriented, packed, stat):
-    core, y, _ = place()
-    chunk = lax.rem(y, 2)
-    dense[rows_at(core, chunk), :] = mine[0:CHUNK, :]
-    dense[rows_at(core, 1 - chunk), :] = near[0:CHUNK, :]
-    dense[rows_at(1 - core, chunk), :] = far[0]
-    dense[rows_at(1 - core, 1 - chunk), :] = far[1]
-    packed[rows_at(0, chunk), :] = mine[CHUNK : 2 * CHUNK, :]
-    packed[rows_at(0, 1 - chunk), :] = near[CHUNK : 2 * CHUNK, :]
-    unpack(packed, mine[2 * CHUNK : ROWS, 0:HALF].astype(F32)[0:1, :], stat)
+def root_kernel(pair, dense, out, oriented, packed, stat):
+    core, _, _ = place()
+    packed[0:CHUNK, :] = pair[0, CHUNK : 2 * CHUNK, :]
+    packed[CHUNK:HALF, :] = pair[1, CHUNK : 2 * CHUNK, :]
+    unpack(packed, pair[0, 2 * CHUNK : ROWS, 0:HALF].astype(F32)[0:1, :], stat)
     gram = gram_of(core, dense, oriented)
     row, col = grid_of(BS)
     shifted = BETA * stat[...] + (1.0 - BETA) * gram + jnp.where(row == col, DAMPING, 0.0)
@@ -191,7 +181,7 @@
     grad_sq = jnp.sum(value * value, keepdims=True)
     pre_sq = jnp.sum(precond * precond, keepdims=True)
     out[...] = (precond * jnp.sqrt(grad_sq / (pre_sq + 1e-06))).astype(BF)
-    half_rows[...] = out[pl.ds(pl.multiple_of(core * HALF, HALF), HALF), :]
+    half_rows[...] = out[half_at(core), :]
 
 
 def stat_kernel(owner, dense, away, far, stat, out, chosen, oriented):
@@ -208,11 +198,8 @@
 
     @pl.when(cross)
     def _():
-        chunk = 1 - lax.rem(y, 2)
-        chosen[rows_at(core, chunk), :] = away[0]
-        chosen[rows_at(core, 1 - chunk), :] = away[1]
-        chosen[rows_at(1 - core, chunk), :] = far[0]
-        chosen[rows_at(1 - core, 1 - chunk), :] = far[1]
+        chosen[half_at(core), :] = away[...]
+        chosen[half_at(1 - core), :] = far[...]
 
     active = jnp.logical_or(same, cross)
 
@@ -225,59 +212,52 @@
         out[...] = stat[...]
 
 
-def last_kernel(mine, away, far, out):
-    core, y, _ = place()
+def last_kernel(mine, other, out):
+    _, y, _ = place()
     block = lax.div(y, 2)
     out[block] = mine[...]
-    out[1 - block, pl.ds(pl.multiple_of(core * HALF, HALF), HALF), :] = away[...]
-    out[1 - block, pl.ds(pl.multiple_of((1 - core) * HALF, HALF), HALF), :] = far[...]
+    out[1 - block, 0:HALF, :] = other[0]
+    out[1 - block, HALF:BS, :] = other[1]
 
 
 def body(grad, stats, owner):
     core = lax.axis_index("group") % 2
     along_y = [[h * 8 + 2 * k + c for k in range(4)] for h in range(2) for c in range(2)]
 
-    def send(value, change):
-        return lax.ppermute(value, "group", [(g, change(g)) for g in range(16)])
-
-    def to_core(value):
-        return send(value, lambda g: g ^ 1)
-
-    def to_mate(value):
-        return send(value, lambda g: g ^ 2)
-
-    def to_mirror(value):
-        return send(value, lambda g: g ^ 6)
-
-    def to_half(value):
-        return send(value, lambda g: g ^ 8)
+    def send(value, bits):
+        return lax.ppermute(value, "group", [(g, g ^ bits) for g in range(16)])
+
+    def gather(value, bits):
+        return lax.all_gather(value, "group", axis_index_groups=[[g, g ^ bits] for g in range(16) if g < g ^ bits])
 
     block = grad[0]
     stat = stats[0, 0]
-    got = to_core(lax.dynamic_slice_in_dim(block, (1 - core) * HALF, HALF, 1))
-    parts = call(first_kernel, array(4, ROWS, BS), [VM, VM, VM])(block, got, stat)
+    got = send(lax.dynamic_slice_in_dim(block, (1 - core) * HALF, HALF, 1), 1)
+    keep = lax.dynamic_slice_in_dim(block, core * HALF, HALF, 1)
+    packed = call(pack_kernel, array(2, STAT, BS), [VM], nbytes=3 << 19)(stat)
+    parts = call(first_kernel, array(4, ROWS, BS), [VM, VM, VM])(keep, got, packed)
     parts = lax.all_to_all(parts, "group", 0, 0, tiled=True, axis_index_groups=along_y)
-    mine = call(second_kernel, array(ROWS, BS), [SM, VM])(owner, parts)
-    got = to_half(mine)
-    mine = call(third_kernel, array(ROWS, BS), [SM, VM, VM])(owner, mine, got)
-    near = to_mate(mine)
-    both = jnp.stack([mine[:CHUNK], near[:CHUNK]])
-    far = to_core(both)
-    away = to_mirror(both)
-    payload, dense = call(
+    partial = call(second_kernel, array(ROWS, BS), [SM, VM])(owner, parts)
+    mine = call(third_kernel, array(ROWS, BS), [SM, VM])(owner, gather(partial, 8))
+    pair = gather(mine, 2)
+    rows = pair[:, :CHUNK].reshape(HALF, BS)
+    away = send(rows, 6)
+    dense = gather(rows, 1).reshape(BS, BS)
+    payload = call(
         root_kernel,
-        (array(BS + 16, BS), array(BS, BS)),
-        [VM, VM, VM],
+        array(BS + 16, BS),
+        [VM, VM],
         [SQUARE, pltpu.VMEM((HALF, BS), BF), pltpu.VMEM((BS, BS), F32)],
         flops=10 * 2 * BS**3,
-    )(mine, near, far)
-    received = to_core(payload)
-    away_far = to_core(away)
+    )(pair, dense)
+    payload, away = lax.optimization_barrier((payload, away))
+    received = send(payload, 1)
+    away_far = send(away, 1)
     tall = pltpu.VMEM((BS + 16, BS), BF)
     result, half_rows = call(
         product_kernel, (array(BS, BS), array(HALF, BS)), [VM, VM, VM], [tall, tall], flops=2 * BS**3
     )(payload, received, dense)
-    mirror = to_mirror(half_rows)
+    mirror = send(half_rows, 6)
     new_stat = call(
         stat_kernel,
         array(BS, BS, dtype=F32),
@@ -286,7 +266,7 @@
         flops=2 * BS**3,
         nbytes=3 << 20,
     )(owner, dense, away, away_far, stat)
-    update = call(last_kernel, array(2, BS, BS), [VM, VM, VM])(result, mirror, to_core(mirror))
+    update = call(last_kernel, array(2, BS, BS), [VM, VM])(result, gather(mirror, 1))
     return (new_stat[None, None], update)
 
 

time: 112 us -> 105 us (0.938)
  the two profiles are of different devices: /device:TPU:37 before, /device:TPU:39 now
where the time goes in v3:
time: 105 us
  blocking collectives  52.4 us (50%)
  waiting for transfers between devices  21.6 us (21%)
  starting transfers between devices  17.8 us (17%)
  Pallas kernels  10.8 us (10%)
  local copies, waits for them, and re-layouts  1.47 us (1%)
    all_gather x4, blocking collectives, gather(): lax.all_gather(value, 'group', axis_index_groups=[[g, g ^ bits] for g in...  52.4 us
    all_to_all x1, waiting for transfers between devices, body(): lax.all_to_all(parts, 'group', 0, 0, tiled=True, axis_index_groups=along_y)  15.1 us
    ppermute x5, starting transfers between devices, send(): return lax.ppermute(value, 'group', [(g, g ^ bits) for g in range(16)])  13.5 us
    ppermute x5, waiting for transfers between devices, send(): return lax.ppermute(value, 'group', [(g, g ^ bits) for g in range(16)])  6.45 us
    all_to_all x1, starting transfers between devices, body(): lax.all_to_all(parts, 'group', 0, 0, tiled=True, axis_index_groups=along_y)  4.31 us
    pallas_call x1, Pallas kernels, body(): call(root_kernel, array(BS + 16, BS), [VM, VM], [SQUARE, pltpu.VMEM((HALF...  3.86 us
  transfers between devices with their start and end apart: 6, of which 3 were waited for; matrix products, arithmetic and copies ran while one was open for 0% of the time, Pallas kernels for 7%

profile of v3, /device:TPU:39, one launch (start us, length us, event | category | flops | bytes accessed | tf_op | source)
XLA Modules:
  0.0 104.8 jit_solution(15721511777374022636)
XLA Ops:
  0.6 0.0 copy-start
  0.7 1.4 %dynamic-slice_bitcast_fusion = (bf16[2,256,512]{2,1,0:T(8,128)(2,1)S(1)}, bf16[2,256,512]{2,1,0:T(8,128)(2,1)S(1)}) fusion(bf16[1,2,512,512]{3,2,1,0:T(8,128)(2,1)} %param.3, s32[]{:T(128)S(6)} %select_n.15, s32[]{:T(128)S(6)} %select_n.14), kind=kLoop, calls=%fused_computation | loop fusion | bytes 2097160 | tf_op jit(solution)/shard_map/dynamic_slice | solution.py:235
  2.0 2.6 %collective-permute-start = (bf16[2,256,512]{2,1,0:T(8,128)(2,1)S(1)}, bf16[2,256,512]{2,1,0:T(8,128)(2,1)S(1)}, u32[]{:S(2)}, u32[]{:S(2)}) collective-permute-start(bf16[2,256,512]{2,1,0:T(8,128)(2,1)S(1)} %get-tuple-element.10), channel_id=1, source_target_pairs={{0,32},{32,0},{64,96},{96,64},{128,160},{160,128},{192,224},{224,1... | collective-permute-start | bytes 1572872 | tf_op jit(solution)/shard_map/ppermute | solution.py:228
  4.6 0.0 copy-done
  4.6 0.1 shard_map.50.packed
  4.7 1.4 %collective-permute-done.got = bf16[2,256,512]{2,1,0:T(8,128)(2,1)S(1)} collective-permute-done((bf16[2,256,512]{2,1,0:T(8,128)(2,1)S(1)}, bf16[2,256,512]{2,1,0:T(8,128)(2,1)S(1)}, u32[]{:S(2)}, u32[]{:S(2)}) %collective-permute-start) | collective-permute-done | bytes 524320 | tf_op jit(solution)/shard_map/ppermute | solution.py:228
  6.1 1.1 %shard_map.51 = bf16[4,272,512]{2,1,0:T(8,128)(2,1)} custom-call(bf16[2,256,512]{2,1,0:T(8,128)(2,1)S(1)} %get-tuple-element.11.keep, bf16[2,256,512]{2,1,0:T(8,128)(2,1)S(1)} %collective-permute-done.got, bf16[2,144,512]{2,1,0:T(8,128)(2,1)S(1)} %shard_map.50.packed), custom_call_target="tpu_custom_call" | custom-call | tf_op jit(solution)/shard_map/pallas_call | solution.py:238
  7.3 0.0 copy-start.1
  7.3 4.3 %all-to-all-start = ((bf16[4,272,512]{2,1,0:T(8,128)(2,1)}), bf16[4,272,512]{2,1,0:T(8,128)(2,1)S(1)}, u32[]{:S(2)}, u32[]{:S(2)}) async-start(bf16[4,272,512]{2,1,0:T(8,128)(2,1)} %shard_map.51), calls=%async_computation | async-start | bytes 2228224 | tf_op jit(solution)/shard_map/all_to_all | solution.py:239
  11.6 0.0 copy-done.1
  11.6 0.1 copy.10.owner
  11.7 15.1 %all-to-all-done.got = bf16[4,272,512]{2,1,0:T(8,128)(2,1)S(1)} async-done(((bf16[4,272,512]{2,1,0:T(8,128)(2,1)}), bf16[4,272,512]{2,1,0:T(8,128)(2,1)S(1)}, u32[]{:S(2)}, u32[]{:S(2)}) %all-to-all-start) | async-done | bytes 1114144 | tf_op jit(solution)/shard_map/all_to_all | solution.py:239
  26.8 0.9 shard_map.52
  27.7 37.4 %all-gather = bf16[544,512]{1,0:T(8,128)(2,1)S(1)} all-gather(bf16[272,512]{1,0:T(8,128)(2,1)S(1)} %shard_map.52), channel_id=2, replica_groups={{0,256},{32,288},{64,320},{96,352},{128,384},{160,416},{192,448},{224,4..., dimensions={0}, use_global_device_ids=true | all-gather | bytes 835584 | tf_op jit(solution)/shard_map/all_gather | solution.py:231
  65.1 0.8 shard_map.53
  65.9 7.2 %all-gather.1 = bf16[544,512]{1,0:T(8,128)(2,1)S(1)} all-gather(bf16[272,512]{1,0:T(8,128)(2,1)S(1)} %shard_map.53), channel_id=3, replica_groups={{0,64},{32,96},{128,192},{160,224},{256,320},{288,352},{384,448},{416,4..., dimensions={0}, use_global_device_ids=true | all-gather | bytes 835584 | tf_op jit(solution)/shard_map/all_gather | solution.py:231
  73.1 2.8 %collective-permute-start.1 = (bf16[256,512]{1,0:T(8,128)(2,1)S(1)}, bf16[256,512]{1,0:T(8,128)(2,1)S(1)}, u32[]{:S(2)}, u32[]{:S(2)}) collective-permute-start(bf16[256,512]{1,0:T(8,128)(2,1)S(1)} %bitcast.22), channel_id=1, source_target_pairs={{0,192},{32,224},{64,128},{96,160},{128,64},{160,96},{192,0},{224,... | collective-permute-start | bytes 786440 | tf_op jit(solution)/shard_map/ppermute | solution.py:228
  75.9 4.7 %all_gather.25 = bf16[2,256,512]{2,1,0:T(8,128)(2,1)S(1)} all-gather(bf16[1,256,512]{2,1,0:T(8,128)(2,1)S(1)} %bitcast.23), channel_id=1, replica_groups={{0,32},{64,96},{128,160},{192,224},{256,288},{320,352},{384,416},{448,4..., dimensions={0}, use_global_device_ids=true | all-gather | bytes 786432 | tf_op jit(solution)/shard_map/all_gather | solution.py:231
  80.6 3.9 %shard_map.54.mine = bf16[528,512]{1,0:T(8,128)(2,1)S(1)} custom-call(bf16[2,272,512]{2,1,0:T(8,128)(2,1)S(1)} %bitcast.20, bf16[512,512]{1,0:T(8,128)(2,1)S(1)} %bitcast.12), custom_call_target="tpu_custom_call" | custom-call | flops 2684354560 | tf_op jit(solution)/shard_map/pallas_call | solution.py:246
  84.4 0.0 collective-permute-done.1.away
  84.4 2.6 %collective-permute-start.3 = (bf16[528,512]{1,0:T(8,128)(2,1)S(1)}, bf16[528,512]{1,0:T(8,128)(2,1)S(1)}, u32[]{:S(2)}, u32[]{:S(2)}) collective-permute-start(bf16[528,512]{1,0:T(8,128)(2,1)S(1)} %shard_map.54.mine), channel_id=1, source_target_pairs={{0,32},{32,0},{64,96},{96,64},{128,160},{160,128},{192,224},{224,1... | collective-permute-start | bytes 1622024 | tf_op jit(solution)/shard_map/ppermute | solution.py:228
  87.1 1.9 %collective-permute-start.2 = (bf16[256,512]{1,0:T(8,128)(2,1)S(1)}, bf16[256,512]{1,0:T(8,128)(2,1)S(1)}, u32[]{:S(2)}, u32[]{:S(2)}) collective-permute-start(bf16[256,512]{1,0:T(8,128)(2,1)S(1)} %collective-permute-done.1.away), channel_id=1, source_target_pairs={{0,32},{32,0},{64,96},{96,64},{128,160},{160,128},{192,224},{224,1... | collective-permute-start | bytes 786440 | tf_op jit(solution)/shard_map/ppermute | solution.py:228
  89.0 0.0 collective-permute-done.3.other
  89.0 1.1 %shard_map.56 = (bf16[512,512]{1,0:T(8,128)(2,1)S(1)}, bf16[256,512]{1,0:T(8,128)(2,1)S(1)}) custom-call(bf16[528,512]{1,0:T(8,128)(2,1)S(1)} %shard_map.54.mine, bf16[528,512]{1,0:T(8,128)(2,1)S(1)} %collective-permute-done.3.other, bf16[512,512]{1,0:T(8,128)(2,1)S(1)} %bitcast.13), custom_call_target="tpu_custom_call" | custom-call | flops 268435456 | tf_op jit(solution)/shard_map/pallas_call | solution.py:257
  90.1 3.6 %collective-permute-start.4 = (bf16[256,512]{1,0:T(8,128)(2,1)S(1)}, bf16[256,512]{1,0:T(8,128)(2,1)S(1)}, u32[]{:S(2)}, u32[]{:S(2)}) collective-permute-start(bf16[256,512]{1,0:T(8,128)(2,1)S(1)} %get-tuple-element.9), channel_id=1, source_target_pairs={{0,192},{32,224},{64,128},{96,160},{128,64},{160,96},{192,0},{224,... | collective-permute-start | bytes 786440 | tf_op jit(solution)/shard_map/ppermute | solution.py:228
  93.7 0.0 collective-permute-done.2.far
  93.7 1.9 %shard_map.55 = f32[512,512]{1,0:T(8,128)} custom-call(s32[32,2]{1,0:T(8,128)S(1)} %copy.10.owner, bf16[512,512]{1,0:T(8,128)(2,1)S(1)} %bitcast.14, bf16[256,512]{1,0:T(8,128)(2,1)S(1)} %collective-permute-done.1.away, bf16[256,512]{1,0:T(8,128)(2,1)S(1)} %collective-permute-done.2.far, f32[512,512]{1,0:T(8,128)S(1)} %bitcast.16), custom_call_target="tpu_custom_call" | custom-call | flops 268435456 | bytes 3145728 | tf_op jit(solution)/shard_map/pallas_call | solution.py:261
  95.6 5.0 %collective-permute-done.4 = bf16[256,512]{1,0:T(8,128)(2,1)S(1)} collective-permute-done((bf16[256,512]{1,0:T(8,128)(2,1)S(1)}, bf16[256,512]{1,0:T(8,128)(2,1)S(1)}, u32[]{:S(2)}, u32[]{:S(2)}) %collective-permute-start.4) | collective-permute-done | bytes 262176 | tf_op jit(solution)/shard_map/ppermute | solution.py:228
  100.6 3.1 %all-gather.2 = bf16[512,512]{1,0:T(8,128)(2,1)S(1)} all-gather(bf16[256,512]{1,0:T(8,128)(2,1)S(1)} %collective-permute-done.4), channel_id=4, replica_groups={{0,32},{64,96},{128,160},{192,224},{256,288},{320,352},{384,416},{448,4..., dimensions={0}, use_global_device_ids=true | all-gather | bytes 786432 | tf_op jit(solution)/shard_map/all_gather | solution.py:231
  103.7 1.1 %shard_map.57 = bf16[2,512,512]{2,1,0:T(8,128)(2,1)} custom-call(bf16[512,512]{1,0:T(8,128)(2,1)S(1)} %get-tuple-element.8.mine, bf16[2,256,512]{2,1,0:T(8,128)(2,1)S(1)} %bitcast.18), custom_call_target="tpu_custom_call" | custom-call | tf_op jit(solution)/shard_map/pallas_call | solution.py:269
  (1 shorter events, 0.0 us)
Async XLA Ops:
  0.6 4.0 %copy-start = (f32[1,1,512,512]{3,2,1,0:T(8,128)S(1)}, f32[1,1,512,512]{3,2,1,0:T(8,128)}, u32[]{:S(2)}) copy-start(f32[1,1,512,512]{3,2,1,0:T(8,128)} %param.4) | copy-start | bytes 3145732
  2.0 4.1 %collective-permute-start = (bf16[2,256,512]{2,1,0:T(8,128)(2,1)S(1)}, bf16[2,256,512]{2,1,0:T(8,128)(2,1)S(1)}, u32[]{:S(2)}, u32[]{:S(2)}) collective-permute-start(bf16[2,256,512]{2,1,0:T(8,128)(2,1)S(1)} %get-tuple-element.10), channel_id=1, source_target_pairs={{0,32},{32,0},{64,96},{96,64},{128,160},{160,128},{192,224},{224,1... | collective-permute-start | bytes 1572872 | tf_op jit(solution)/shard_map/ppermute | solution.py:228
  7.3 4.3 %copy-start.1 = (s32[32,2]{0,1:T(2,128)S(1)}, s32[32,2]{0,1:T(2,128)}, u32[]{:S(2)}) copy-start(s32[32,2]{0,1:T(2,128)} %param.5) | copy-start | bytes 772
  7.3 19.5 %all-to-all-start = ((bf16[4,272,512]{2,1,0:T(8,128)(2,1)}), bf16[4,272,512]{2,1,0:T(8,128)(2,1)S(1)}, u32[]{:S(2)}, u32[]{:S(2)}) async-start(bf16[4,272,512]{2,1,0:T(8,128)(2,1)} %shard_map.51), calls=%async_computation | async-start | bytes 2228224 | tf_op jit(solution)/shard_map/all_to_all | solution.py:239
  73.1 11.3 %collective-permute-start.1 = (bf16[256,512]{1,0:T(8,128)(2,1)S(1)}, bf16[256,512]{1,0:T(8,128)(2,1)S(1)}, u32[]{:S(2)}, u32[]{:S(2)}) collective-permute-start(bf16[256,512]{1,0:T(8,128)(2,1)S(1)} %bitcast.22), channel_id=1, source_target_pairs={{0,192},{32,224},{64,128},{96,160},{128,64},{160,96},{192,0},{224,... | collective-permute-start | bytes 786440 | tf_op jit(solution)/shard_map/ppermute | solution.py:228
  84.4 4.5 %collective-permute-start.3 = (bf16[528,512]{1,0:T(8,128)(2,1)S(1)}, bf16[528,512]{1,0:T(8,128)(2,1)S(1)}, u32[]{:S(2)}, u32[]{:S(2)}) collective-permute-start(bf16[528,512]{1,0:T(8,128)(2,1)S(1)} %shard_map.54.mine), channel_id=1, source_target_pairs={{0,32},{32,0},{64,96},{96,64},{128,160},{160,128},{192,224},{224,1... | collective-permute-start | bytes 1622024 | tf_op jit(solution)/shard_map/ppermute | solution.py:228
  87.1 6.6 %collective-permute-start.2 = (bf16[256,512]{1,0:T(8,128)(2,1)S(1)}, bf16[256,512]{1,0:T(8,128)(2,1)S(1)}, u32[]{:S(2)}, u32[]{:S(2)}) collective-permute-start(bf16[256,512]{1,0:T(8,128)(2,1)S(1)} %collective-permute-done.1.away), channel_id=1, source_target_pairs={{0,32},{32,0},{64,96},{96,64},{128,160},{160,128},{192,224},{224,1... | collective-permute-start | bytes 786440 | tf_op jit(solution)/shard_map/ppermute | solution.py:228
  90.1 10.5 %collective-permute-start.4 = (bf16[256,512]{1,0:T(8,128)(2,1)S(1)}, bf16[256,512]{1,0:T(8,128)(2,1)S(1)}, u32[]{:S(2)}, u32[]{:S(2)}) collective-permute-start(bf16[256,512]{1,0:T(8,128)(2,1)S(1)} %get-tuple-element.9), channel_id=1, source_target_pairs={{0,192},{32,224},{64,128},{96,160},{128,64},{160,96},{192,0},{224,... | collective-permute-start | bytes 786440 | tf_op jit(solution)/shard_map/ppermute | solution.py:228

commit v4 on v3

--- a/solution.py
+++ b/solution.py
@@ -63,19 +63,18 @@
     diagonal = jnp.sum(jnp.where(row == col, corner, 0.0), axis=0, keepdims=True)
     diagonal = jnp.broadcast_to(diagonal, (16, HALF)).astype(BF)
     side = stat[0:HALF, HALF:BS].astype(BF)
-    for chunk in range(2):
-        lo = chunk * CHUNK
-        out[chunk, 0:CHUNK, 0:HALF] = fold[lo : lo + CHUNK]
-        out[chunk, 0:CHUNK, HALF:BS] = side[lo : lo + CHUNK]
-        out[chunk, CHUNK:STAT, 0:HALF] = diagonal
-        out[chunk, CHUNK:STAT, HALF:BS] = diagonal
-
-
-def first_kernel(keep, got, packed, out):
+    for y in range(4):
+        lo = (y % 2) * CHUNK
+        out[y, 0:CHUNK, 0:HALF] = fold[lo : lo + CHUNK]
+        out[y, 0:CHUNK, HALF:BS] = side[lo : lo + CHUNK]
+        out[y, CHUNK:STAT, 0:HALF] = diagonal
+        out[y, CHUNK:STAT, HALF:BS] = diagonal
+
+
+def first_kernel(keep, got, out):
     for y in range(4):
         rows = slice((y % 2) * CHUNK, (y % 2 + 1) * CHUNK)
-        out[y, 0:CHUNK, :] = (keep[y // 2, rows, :].astype(F32) + got[y // 2, rows, :].astype(F32)).astype(BF)
-        out[y, CHUNK:ROWS, :] = packed[y % 2]
+        out[y] = (keep[y // 2, rows, :].astype(F32) + got[y // 2, rows, :].astype(F32)).astype(BF)
 
 
 def unpack(packed, diagonal, stat):
@@ -89,21 +88,30 @@
     stat[HALF:BS, 0:HALF] = side.T
 
 
-def second_kernel(owner, got, out):
+def choose_kernel(owner, got, out):
     _, y, _ = place()
-    total = got[0, 0:CHUNK, :].astype(F32)
+    out[...] = got[lax.rem(owner[lax.axis_index("dp"), lax.div(y, 2)], 4)]
+
+
+def second_kernel(got, out):
+    total = got[0].astype(F32)
     for source in range(1, 4):
-        total += got[source, 0:CHUNK, :].astype(F32)
-    out[0:CHUNK, :] = total.astype(BF)
-    pair = owner[lax.axis_index("dp"), lax.div(y, 2)]
-    out[CHUNK:ROWS, :] = got[lax.rem(pair, 4), CHUNK:ROWS, :]
-
-
-def third_kernel(owner, got, out):
-    _, y, _ = place()
-    out[0:CHUNK, :] = (got[0, 0:CHUNK, :].astype(F32) + got[1, 0:CHUNK, :].astype(F32)).astype(BF)
-    pair = owner[lax.axis_index("dp"), lax.div(y, 2)]
-    out[CHUNK:ROWS, :] = got[lax.div(pair, 4), CHUNK:ROWS, :]
+        total += got[source].astype(F32)
+    out[...] = total.astype(BF)
+
+
+def third_kernel(owner, sums, stat, other, out):
+    _, y, half = place()
+    out[0:CHUNK, :] = (sums[0].astype(F32) + sums[1].astype(F32)).astype(BF)
+    here = lax.div(owner[lax.axis_index("dp"), lax.div(y, 2)], 4) == half
+
+    @pl.when(here)
+    def _():
+        out[CHUNK:ROWS, :] = stat[...]
+
+    @pl.when(jnp.logical_not(here))
+    def _():
+        out[CHUNK:ROWS, :] = other[...]
 
 
 def gram_of(core, dense, oriented):
@@ -230,15 +238,20 @@
     def gather(value, bits):
         return lax.all_gather(value, "group", axis_index_groups=[[g, g ^ bits] for g in range(16) if g < g ^ bits])
 
+    def exchange(value):
+        return lax.all_to_all(value, "group", 0, 0, tiled=True, axis_index_groups=along_y)
+
     block = grad[0]
     stat = stats[0, 0]
     got = send(lax.dynamic_slice_in_dim(block, (1 - core) * HALF, HALF, 1), 1)
     keep = lax.dynamic_slice_in_dim(block, core * HALF, HALF, 1)
-    packed = call(pack_kernel, array(2, STAT, BS), [VM], nbytes=3 << 19)(stat)
-    parts = call(first_kernel, array(4, ROWS, BS), [VM, VM, VM])(keep, got, packed)
-    parts = lax.all_to_all(parts, "group", 0, 0, tiled=True, axis_index_groups=along_y)
-    partial = call(second_kernel, array(ROWS, BS), [SM, VM])(owner, parts)
-    mine = call(third_kernel, array(ROWS, BS), [SM, VM])(owner, gather(partial, 8))
+    packed = call(pack_kernel, array(4, STAT, BS), [VM], nbytes=3 << 19)(stat)
+    chosen = call(choose_kernel, array(STAT, BS), [SM, VM])(owner, exchange(packed))
+    parts = exchange(call(first_kernel, array(4, CHUNK, BS), [VM, VM])(keep, got))
+    partial = call(second_kernel, array(CHUNK, BS), [VM])(parts)
+    across = send(chosen, 8)
+    sums = gather(partial, 8)
+    mine = call(third_kernel, array(ROWS, BS), [SM, VM, VM, VM])(owner, sums, chosen, across)
     pair = gather(mine, 2)
     rows = pair[:, :CHUNK].reshape(HALF, BS)
     away = send(rows, 6)

time: 105 us -> 104 us (level)
  the two profiles are of different devices: /device:TPU:39 before, /device:TPU:5 now
where the time goes in v4:
time: 104 us
  starting transfers between devices  37.6 us (36%)
  blocking collectives  37.6 us (36%)
  waiting for transfers between devices  13.9 us (13%)
  Pallas kernels  12.1 us (12%)
  local copies, waits for them, and re-layouts  1.48 us (1%)
    all_gather x4, blocking collectives, gather(): lax.all_gather(value, 'group', axis_index_groups=[[g, g ^ bits] for g in...  37.6 us
    ppermute x6, starting transfers between devices, send(): return lax.ppermute(value, 'group', [(g, g ^ bits) for g in range(16)])  30 us
    all_to_all x2, waiting for transfers between devices, exchange(): lax.all_to_all(value, 'group', 0, 0, tiled=True, axis_index_groups=along_y)  9.1 us
    all_to_all x2, starting transfers between devices, exchange(): lax.all_to_all(value, 'group', 0, 0, tiled=True, axis_index_groups=along_y)  7.66 us
    ppermute x6, waiting for transfers between devices, send(): return lax.ppermute(value, 'group', [(g, g ^ bits) for g in range(16)])  4.84 us
    pallas_call x1, Pallas kernels, body(): call(root_kernel, array(BS + 16, BS), [VM, VM], [SQUARE, pltpu.VMEM((HALF...  3.85 us
    pallas_call x1, Pallas kernels, body(): call(stat_kernel, array(BS, BS, dtype=F32), [SM, VM, VM, VM, VM], [SQUARE...  2.6 us
  transfers between devices with their start and end apart: 8, of which 2 were waited for; matrix products, arithmetic and copies ran while one was open for 0% of the time, Pallas kernels for 10%

profile of v4, /device:TPU:5, one launch (start us, length us, event | category | flops | bytes accessed | tf_op | source)
XLA Modules:
  0.0 103.6 jit_solution(303843712275051633)
XLA Ops:
  0.6 0.0 copy-start
  0.7 1.4 %dynamic-slice_bitcast_fusion = (bf16[2,256,512]{2,1,0:T(8,128)(2,1)S(1)}, bf16[2,256,512]{2,1,0:T(8,128)(2,1)S(1)}) fusion(bf16[1,2,512,512]{3,2,1,0:T(8,128)(2,1)} %param.3, s32[]{:T(128)S(6)} %select_n.15, s32[]{:T(128)S(6)} %select_n.14), kind=kLoop, calls=%fused_computation | loop fusion | bytes 2097160 | tf_op jit(solution)/shard_map/dynamic_slice | solution.py:246
  2.0 2.6 %collective-permute-start = (bf16[2,256,512]{2,1,0:T(8,128)(2,1)S(1)}, bf16[2,256,512]{2,1,0:T(8,128)(2,1)S(1)}, u32[]{:S(2)}, u32[]{:S(2)}) collective-permute-start(bf16[2,256,512]{2,1,0:T(8,128)(2,1)S(1)} %get-tuple-element.10), channel_id=1, source_target_pairs={{0,32},{32,0},{64,96},{96,64},{128,160},{160,128},{192,224},{224,1... | collective-permute-start | bytes 1572872 | tf_op jit(solution)/shard_map/ppermute | solution.py:236
  4.6 0.0 copy-done
  4.6 0.9 shard_map.52
  5.5 4.2 %all-to-all-start.1 = ((bf16[4,144,512]{2,1,0:T(8,128)(2,1)}), bf16[4,144,512]{2,1,0:T(8,128)(2,1)S(1)}, u32[]{:S(2)}, u32[]{:S(2)}) async-start(bf16[4,144,512]{2,1,0:T(8,128)(2,1)} %shard_map.52), calls=%async_computation.1 | async-start | bytes 1179648 | tf_op jit(solution)/shard_map/all_to_all | solution.py:242
  9.7 0.0 collective-permute-done.got
  9.7 0.9 shard_map.50
  10.6 0.0 copy-start.1
  10.6 9.1 %all-to-all-done.1.got = bf16[4,144,512]{2,1,0:T(8,128)(2,1)S(1)} async-done(((bf16[4,144,512]{2,1,0:T(8,128)(2,1)}), bf16[4,144,512]{2,1,0:T(8,128)(2,1)S(1)}, u32[]{:S(2)}, u32[]{:S(2)}) %all-to-all-start.1) | async-done | bytes 589856 | tf_op jit(solution)/shard_map/all_to_all | solution.py:242
  19.7 3.5 %all-to-all-start = ((bf16[4,128,512]{2,1,0:T(8,128)(2,1)}), bf16[4,128,512]{2,1,0:T(8,128)(2,1)S(1)}, u32[]{:S(2)}, u32[]{:S(2)}) async-start(bf16[4,128,512]{2,1,0:T(8,128)(2,1)} %shard_map.50), calls=%async_computation | async-start | bytes 1048576 | tf_op jit(solution)/shard_map/all_to_all | solution.py:242
  23.2 0.0 copy-done.1
  23.2 0.1 copy.10.owner
  23.3 0.8 shard_map.53.stat
  24.1 15.4 %collective-permute-start.1 = (bf16[144,512]{1,0:T(8,128)(2,1)S(1)}, bf16[144,512]{1,0:T(8,128)(2,1)S(1)}, u32[]{:S(2)}, u32[]{:S(2)}) collective-permute-start(bf16[144,512]{1,0:T(8,128)(2,1)S(1)} %shard_map.53.stat), channel_id=1, source_target_pairs={{0,256},{32,288},{64,320},{96,352},{128,384},{160,416},{192,448},{... | collective-permute-start | bytes 442376 | tf_op jit(solution)/shard_map/ppermute | solution.py:236
  39.6 0.0 all-to-all-done.got
  39.6 0.1 shard_map.51
  39.7 22.1 %all-gather = bf16[256,512]{1,0:T(8,128)(2,1)S(1)} all-gather(bf16[128,512]{1,0:T(8,128)(2,1)S(1)} %shard_map.51), channel_id=2, replica_groups={{0,256},{32,288},{64,320},{96,352},{128,384},{160,416},{192,448},{224,4..., dimensions={0}, use_global_device_ids=true | all-gather | bytes 393216 | tf_op jit(solution)/shard_map/all_gather | solution.py:239
  61.7 0.0 collective-permute-done.1.other
  61.7 0.8 shard_map.54
  62.6 8.1 %all-gather.1 = bf16[544,512]{1,0:T(8,128)(2,1)S(1)} all-gather(bf16[272,512]{1,0:T(8,128)(2,1)S(1)} %shard_map.54), channel_id=3, replica_groups={{0,64},{32,96},{128,192},{160,224},{256,320},{288,352},{384,448},{416,4..., dimensions={0}, use_global_device_ids=true | all-gather | bytes 835584 | tf_op jit(solution)/shard_map/all_gather | solution.py:239
  70.8 4.5 %collective-permute-start.2 = (bf16[256,512]{1,0:T(8,128)(2,1)S(1)}, bf16[256,512]{1,0:T(8,128)(2,1)S(1)}, u32[]{:S(2)}, u32[]{:S(2)}) collective-permute-start(bf16[256,512]{1,0:T(8,128)(2,1)S(1)} %bitcast.22), channel_id=1, source_target_pairs={{0,192},{32,224},{64,128},{96,160},{128,64},{160,96},{192,0},{224,... | collective-permute-start | bytes 786440 | tf_op jit(solution)/shard_map/ppermute | solution.py:236
  75.2 4.3 %all_gather.25 = bf16[2,256,512]{2,1,0:T(8,128)(2,1)S(1)} all-gather(bf16[1,256,512]{2,1,0:T(8,128)(2,1)S(1)} %bitcast.23), channel_id=1, replica_groups={{0,32},{64,96},{128,160},{192,224},{256,288},{320,352},{384,416},{448,4..., dimensions={0}, use_global_device_ids=true | all-gather | bytes 786432 | tf_op jit(solution)/shard_map/all_gather | solution.py:239
  79.5 3.9 %shard_map.55.mine = bf16[528,512]{1,0:T(8,128)(2,1)S(1)} custom-call(bf16[2,272,512]{2,1,0:T(8,128)(2,1)S(1)} %bitcast.19, bf16[512,512]{1,0:T(8,128)(2,1)S(1)} %bitcast.12), custom_call_target="tpu_custom_call" | custom-call | flops 2684354560 | tf_op jit(solution)/shard_map/pallas_call | solution.py:259
  83.4 0.0 collective-permute-done.2.away
  83.4 2.5 %collective-permute-start.4 = (bf16[528,512]{1,0:T(8,128)(2,1)S(1)}, bf16[528,512]{1,0:T(8,128)(2,1)S(1)}, u32[]{:S(2)}, u32[]{:S(2)}) collective-permute-start(bf16[528,512]{1,0:T(8,128)(2,1)S(1)} %shard_map.55.mine), channel_id=1, source_target_pairs={{0,32},{32,0},{64,96},{96,64},{128,160},{160,128},{192,224},{224,1... | collective-permute-start | bytes 1622024 | tf_op jit(solution)/shard_map/ppermute | solution.py:236
  85.9 1.9 %collective-permute-start.3 = (bf16[256,512]{1,0:T(8,128)(2,1)S(1)}, bf16[256,512]{1,0:T(8,128)(2,1)S(1)}, u32[]{:S(2)}, u32[]{:S(2)}) collective-permute-start(bf16[256,512]{1,0:T(8,128)(2,1)S(1)} %collective-permute-done.2.away), channel_id=1, source_target_pairs={{0,32},{32,0},{64,96},{96,64},{128,160},{160,128},{192,224},{224,1... | collective-permute-start | bytes 786440 | tf_op jit(solution)/shard_map/ppermute | solution.py:236
  87.8 0.0 collective-permute-done.4.other
  87.8 1.1 %shard_map.57 = (bf16[512,512]{1,0:T(8,128)(2,1)S(1)}, bf16[256,512]{1,0:T(8,128)(2,1)S(1)}) custom-call(bf16[528,512]{1,0:T(8,128)(2,1)S(1)} %shard_map.55.mine, bf16[528,512]{1,0:T(8,128)(2,1)S(1)} %collective-permute-done.4.other, bf16[512,512]{1,0:T(8,128)(2,1)S(1)} %bitcast.13), custom_call_target="tpu_custom_call" | custom-call | flops 268435456 | tf_op jit(solution)/shard_map/pallas_call | solution.py:270
  88.9 3.0 %collective-permute-start.5 = (bf16[256,512]{1,0:T(8,128)(2,1)S(1)}, bf16[256,512]{1,0:T(8,128)(2,1)S(1)}, u32[]{:S(2)}, u32[]{:S(2)}) collective-permute-start(bf16[256,512]{1,0:T(8,128)(2,1)S(1)} %get-tuple-element.9), channel_id=1, source_target_pairs={{0,192},{32,224},{64,128},{96,160},{128,64},{160,96},{192,0},{224,... | collective-permute-start | bytes 786440 | tf_op jit(solution)/shard_map/ppermute | solution.py:236
  92.0 0.0 collective-permute-done.3.far
  92.0 2.6 %shard_map.56 = f32[512,512]{1,0:T(8,128)} custom-call(s32[32,2]{1,0:T(8,128)S(1)} %copy.10.owner, bf16[512,512]{1,0:T(8,128)(2,1)S(1)} %bitcast.14, bf16[256,512]{1,0:T(8,128)(2,1)S(1)} %collective-permute-done.2.away, bf16[256,512]{1,0:T(8,128)(2,1)S(1)} %collective-permute-done.3.far, f32[512,512]{1,0:T(8,128)S(1)} %bitcast.16), custom_call_target="tpu_custom_call" | custom-call | flops 268435456 | bytes 3145728 | tf_op jit(solution)/shard_map/pallas_call | solution.py:274
  94.6 4.8 %collective-permute-done.5 = bf16[256,512]{1,0:T(8,128)(2,1)S(1)} collective-permute-done((bf16[256,512]{1,0:T(8,128)(2,1)S(1)}, bf16[256,512]{1,0:T(8,128)(2,1)S(1)}, u32[]{:S(2)}, u32[]{:S(2)}) %collective-permute-start.5) | collective-permute-done | bytes 262176 | tf_op jit(solution)/shard_map/ppermute | solution.py:236
  99.4 3.1 %all-gather.2 = bf16[512,512]{1,0:T(8,128)(2,1)S(1)} all-gather(bf16[256,512]{1,0:T(8,128)(2,1)S(1)} %collective-permute-done.5), channel_id=4, replica_groups={{0,32},{64,96},{128,160},{192,224},{256,288},{320,352},{384,416},{448,4..., dimensions={0}, use_global_device_ids=true | all-gather | bytes 786432 | tf_op jit(solution)/shard_map/all_gather | solution.py:239
  102.6 1.1 %shard_map.58 = bf16[2,512,512]{2,1,0:T(8,128)(2,1)} custom-call(bf16[512,512]{1,0:T(8,128)(2,1)S(1)} %get-tuple-element.8.mine, bf16[2,256,512]{2,1,0:T(8,128)(2,1)S(1)} %bitcast.17), custom_call_target="tpu_custom_call" | custom-call | tf_op jit(solution)/shard_map/pallas_call | solution.py:282
  (1 shorter events, 0.0 us)
Async XLA Ops:
  0.6 4.0 %copy-start = (f32[1,1,512,512]{3,2,1,0:T(8,128)S(1)}, f32[1,1,512,512]{3,2,1,0:T(8,128)}, u32[]{:S(2)}) copy-start(f32[1,1,512,512]{3,2,1,0:T(8,128)} %param.4) | copy-start | bytes 3145732
  2.0 7.7 %collective-permute-start = (bf16[2,256,512]{2,1,0:T(8,128)(2,1)S(1)}, bf16[2,256,512]{2,1,0:T(8,128)(2,1)S(1)}, u32[]{:S(2)}, u32[]{:S(2)}) collective-permute-start(bf16[2,256,512]{2,1,0:T(8,128)(2,1)S(1)} %get-tuple-element.10), channel_id=1, source_target_pairs={{0,32},{32,0},{64,96},{96,64},{128,160},{160,128},{192,224},{224,1... | collective-permute-start | bytes 1572872 | tf_op jit(solution)/shard_map/ppermute | solution.py:236
  5.5 14.2 %all-to-all-start.1 = ((bf16[4,144,512]{2,1,0:T(8,128)(2,1)}), bf16[4,144,512]{2,1,0:T(8,128)(2,1)S(1)}, u32[]{:S(2)}, u32[]{:S(2)}) async-start(bf16[4,144,512]{2,1,0:T(8,128)(2,1)} %shard_map.52), calls=%async_computation.1 | async-start | bytes 1179648 | tf_op jit(solution)/shard_map/all_to_all | solution.py:242
  10.6 12.6 %copy-start.1 = (s32[32,2]{0,1:T(2,128)S(1)}, s32[32,2]{0,1:T(2,128)}, u32[]{:S(2)}) copy-start(s32[32,2]{0,1:T(2,128)} %param.5) | copy-start | bytes 772
  19.7 19.9 %all-to-all-start = ((bf16[4,128,512]{2,1,0:T(8,128)(2,1)}), bf16[4,128,512]{2,1,0:T(8,128)(2,1)S(1)}, u32[]{:S(2)}, u32[]{:S(2)}) async-start(bf16[4,128,512]{2,1,0:T(8,128)(2,1)} %shard_map.50), calls=%async_computation | async-start | bytes 1048576 | tf_op jit(solution)/shard_map/all_to_all | solution.py:242
  24.1 37.6 %collective-permute-start.1 = (bf16[144,512]{1,0:T(8,128)(2,1)S(1)}, bf16[144,512]{1,0:T(8,128)(2,1)S(1)}, u32[]{:S(2)}, u32[]{:S(2)}) collective-permute-start(bf16[144,512]{1,0:T(8,128)(2,1)S(1)} %shard_map.53.stat), channel_id=1, source_target_pairs={{0,256},{32,288},{64,320},{96,352},{128,384},{160,416},{192,448},{... | collective-permute-start | bytes 442376 | tf_op jit(solution)/shard_map/ppermute | solution.py:236
  70.8 12.6 %collective-permute-start.2 = (bf16[256,512]{1,0:T(8,128)(2,1)S(1)}, bf16[256,512]{1,0:T(8,128)(2,1)S(1)}, u32[]{:S(2)}, u32[]{:S(2)}) collective-permute-start(bf16[256,512]{1,0:T(8,128)(2,1)S(1)} %bitcast.22), channel_id=1, source_target_pairs={{0,192},{32,224},{64,128},{96,160},{128,64},{160,96},{192,0},{224,... | collective-permute-start | bytes 786440 | tf_op jit(solution)/shard_map/ppermute | solution.py:236
  83.4 4.4 %collective-permute-start.4 = (bf16[528,512]{1,0:T(8,128)(2,1)S(1)}, bf16[528,512]{1,0:T(8,128)(2,1)S(1)}, u32[]{:S(2)}, u32[]{:S(2)}) collective-permute-start(bf16[528,512]{1,0:T(8,128)(2,1)S(1)} %shard_map.55.mine), channel_id=1, source_target_pairs={{0,32},{32,0},{64,96},{96,64},{128,160},{160,128},{192,224},{224,1... | collective-permute-start | bytes 1622024 | tf_op jit(solution)/shard_map/ppermute | solution.py:236
  85.9 6.1 %collective-permute-start.3 = (bf16[256,512]{1,0:T(8,128)(2,1)S(1)}, bf16[256,512]{1,0:T(8,128)(2,1)S(1)}, u32[]{:S(2)}, u32[]{:S(2)}) collective-permute-start(bf16[256,512]{1,0:T(8,128)(2,1)S(1)} %collective-permute-done.2.away), channel_id=1, source_target_pairs={{0,32},{32,0},{64,96},{96,64},{128,160},{160,128},{192,224},{224,1... | collective-permute-start | bytes 786440 | tf_op jit(solution)/shard_map/ppermute | solution.py:236
  88.9 10.5 %collective-permute-start.5 = (bf16[256,512]{1,0:T(8,128)(2,1)S(1)}, bf16[256,512]{1,0:T(8,128)(2,1)S(1)}, u32[]{:S(2)}, u32[]{:S(2)}) collective-permute-start(bf16[256,512]{1,0:T(8,128)(2,1)S(1)} %get-tuple-element.9), channel_id=1, source_target_pairs={{0,192},{32,224},{64,128},{96,160},{128,64},{160,96},{192,0},{224,... | collective-permute-start | bytes 786440 | tf_op jit(solution)/shard_map/ppermute | solution.py:236

commit v5 on v3

--- a/solution.py
+++ b/solution.py
@@ -18,20 +18,21 @@
 F32 = jnp.float32
 
 VM = pl.BlockSpec(memory_space=pltpu.VMEM)
-SM = pl.BlockSpec(memory_space=pltpu.SMEM)
+HBM = pl.BlockSpec(memory_space=pl.ANY)
 SQUARE = pltpu.VMEM((BS, BS), BF)
 
 
-def call(kernel, shapes, specs, scratch=(), flops=0, nbytes=0):
+def call(kernel, shapes, specs, scratch=(), flops=0, nbytes=0, out_spec=VM, **more):
     many = isinstance(shapes, tuple)
     return pl.pallas_call(
         kernel,
         out_shape=shapes,
         in_specs=specs,
-        out_specs=(VM,) * len(shapes) if many else VM,
+        out_specs=(out_spec,) * len(shapes) if many else out_spec,
         scratch_shapes=list(scratch),
         compiler_params=pltpu.CompilerParams(vmem_limit_bytes=LIMIT),
         cost_estimate=pl.CostEstimate(flops=flops, bytes_accessed=nbytes, transcendentals=0),
+        **more,
     )
 
 
@@ -44,6 +45,12 @@
     return lax.rem(group, 2), lax.rem(lax.div(group, 2), 4), lax.div(group, 8)
 
 
+def owner_of(owner, block):
+    row = lax.broadcasted_iota(jnp.int32, owner.shape, 0) == lax.axis_index("dp")
+    col = lax.broadcasted_iota(jnp.int32, owner.shape, 1) == block
+    return jnp.sum(jnp.where(row & col, owner[...], 0))
+
+
 def half_at(core):
     return pl.ds(pl.multiple_of(core * HALF, HALF), HALF)
 
@@ -54,6 +61,19 @@
 
 def grid_of(n):
     return lax.broadcasted_iota(jnp.int32, (n, n), 0), lax.broadcasted_iota(jnp.int32, (n, n), 1)
+
+
+def take(other):
+    def kernel(grad, out, sems):
+        core, _, _ = place()
+        rows = half_at(1 - core if other else core)
+        copies = [pltpu.make_async_copy(grad.at[b, rows, :], out.at[b], sems.at[b]) for b in range(2)]
+        for copy in copies:
+            copy.start()
+        for copy in copies:
+            copy.wait()
+
+    return kernel
 
 
 def pack_kernel(stat, out):
@@ -71,7 +91,8 @@
         out[chunk, CHUNK:STAT, HALF:BS] = diagonal
 
 
-def first_kernel(keep, got, packed, out):
+def first_kernel(keep, got, packed, owner, out):
+    del owner
     for y in range(4):
         rows = slice((y % 2) * CHUNK, (y % 2 + 1) * CHUNK)
         out[y, 0:CHUNK, :] = (keep[y // 2, rows, :].astype(F32) + got[y // 2, rows, :].astype(F32)).astype(BF)
@@ -95,14 +116,14 @@
     for source in range(1, 4):
         total += got[source, 0:CHUNK, :].astype(F32)
     out[0:CHUNK, :] = total.astype(BF)
-    pair = owner[lax.axis_index("dp"), lax.div(y, 2)]
+    pair = owner_of(owner, lax.div(y, 2))
     out[CHUNK:ROWS, :] = got[lax.rem(pair, 4), CHUNK:ROWS, :]
 
 
 def third_kernel(owner, got, out):
     _, y, _ = place()
     out[0:CHUNK, :] = (got[0, 0:CHUNK, :].astype(F32) + got[1, 0:CHUNK, :].astype(F32)).astype(BF)
-    pair = owner[lax.axis_index("dp"), lax.div(y, 2)]
+    pair = owner_of(owner, lax.div(y, 2))
     out[CHUNK:ROWS, :] = got[lax.div(pair, 4), CHUNK:ROWS, :]
 
 
@@ -186,11 +207,10 @@
 
 def stat_kernel(owner, dense, away, far, stat, out, chosen, oriented):
     core, y, half = place()
-    column = lax.axis_index("dp")
     pair = half * 4 + y
     block = lax.div(y, 2)
-    same = owner[column, block] == pair
-    cross = owner[column, 1 - block] == pair
+    same = owner_of(owner, block) == pair
+    cross = owner_of(owner, 1 - block) == pair
 
     @pl.when(same)
     def _():
@@ -212,16 +232,22 @@
         out[...] = stat[...]
 
 
-def last_kernel(mine, other, out):
+def own_kernel(mine, out, sem):
     _, y, _ = place()
-    block = lax.div(y, 2)
-    out[block] = mine[...]
-    out[1 - block, 0:HALF, :] = other[0]
-    out[1 - block, HALF:BS, :] = other[1]
+    copy = pltpu.make_async_copy(mine, out.at[lax.div(y, 2)], sem)
+    copy.start()
+    copy.wait()
+
+
+def last_kernel(other, begun, out, sem):
+    del begun
+    _, y, _ = place()
+    copy = pltpu.make_async_copy(other, out.at[1 - lax.div(y, 2)], sem)
+    copy.start()
+    copy.wait()
 
 
 def body(grad, stats, owner):
-    core = lax.axis_index("group") % 2
     along_y = [[h * 8 + 2 * k + c for k in range(4)] for h in range(2) for c in range(2)]
 
     def send(value, bits):
@@ -232,13 +258,14 @@
 
     block = grad[0]
     stat = stats[0, 0]
-    got = send(lax.dynamic_slice_in_dim(block, (1 - core) * HALF, HALF, 1), 1)
-    keep = lax.dynamic_slice_in_dim(block, core * HALF, HALF, 1)
+    pieces = [call(take(other), array(2, HALF, BS), [HBM], [pltpu.SemaphoreType.DMA((2,))]) for other in (True, False)]
+    got = send(pieces[0](block), 1)
+    keep = pieces[1](block)
     packed = call(pack_kernel, array(2, STAT, BS), [VM], nbytes=3 << 19)(stat)
-    parts = call(first_kernel, array(4, ROWS, BS), [VM, VM, VM])(keep, got, packed)
+    parts = call(first_kernel, array(4, ROWS, BS), [VM, VM, VM, VM])(keep, got, packed, owner)
     parts = lax.all_to_all(parts, "group", 0, 0, tiled=True, axis_index_groups=along_y)
-    partial = call(second_kernel, array(ROWS, BS), [SM, VM])(owner, parts)
-    mine = call(third_kernel, array(ROWS, BS), [SM, VM])(owner, gather(partial, 8))
+    partial = call(second_kernel, array(ROWS, BS), [VM, VM])(owner, parts)
+    mine = call(third_kernel, array(ROWS, BS), [VM, VM])(owner, gather(partial, 8))
     pair = gather(mine, 2)
     rows = pair[:, :CHUNK].reshape(HALF, BS)
     away = send(rows, 6)
@@ -261,12 +288,15 @@
     new_stat = call(
         stat_kernel,
         array(BS, BS, dtype=F32),
-        [SM, VM, VM, VM, VM],
+        [VM, VM, VM, VM, VM],
         [SQUARE, SQUARE],
         flops=2 * BS**3,
         nbytes=3 << 20,
     )(owner, dense, away, away_far, stat)
-    update = call(last_kernel, array(2, BS, BS), [VM, VM])(result, gather(mirror, 1))
+    sem = [pltpu.SemaphoreType.DMA]
+    begun = call(own_kernel, array(2, BS, BS), [VM], sem, out_spec=HBM)(result)
+    other = gather(mirror, 1).reshape(BS, BS)
+    update = call(last_kernel, array(2, BS, BS), [VM, HBM], sem, out_spec=HBM, input_output_aliases={1: 0})(other, begun)
     return (new_stat[None, None], update)
 
 

time: 105 us -> 102 us (0.971)
  blocking collectives: 52.4 us -> 71.6 us
  waiting for transfers between devices: 21.6 us -> 5.45 us
  starting transfers between devices: 17.8 us -> 13.6 us
  Pallas kernels: 10.8 us -> 9.09 us
    all_to_all x0 -> x1, blocking collectives: none -> 19.2 us  [body(): lax.all_to_all(parts, 'group', 0, 0, tiled=True, axis_index_groups=along_y)]
    all_to_all x1 -> x0, waiting for transfers between devices: 15.1 us -> none  [body(): lax.all_to_all(parts, 'group', 0, 0, tiled=True, axis_index_groups=along_y)]
    all_to_all x1 -> x0, starting transfers between devices: 4.31 us -> none  [body(): lax.all_to_all(parts, 'group', 0, 0, tiled=True, axis_index_groups=along_y)]
    pallas_call x5 -> x8, Pallas kernels: 5.77 us -> 4.07 us  [the longest x1 1.91 us: body(): call(stat_kernel, array(BS, BS, dtype=F32), [VM, VM, VM, VM, VM], [SQUARE...]
    dynamic_slice x1 -> x0, local copies, waits for them, and re-layouts: 1.36 us -> none  [body(): got = send(lax.dynamic_slice_in_dim(block, (1 - core) * HALF, HALF, 1), 1)]
    unnamed x5 -> x7, local copies, waits for them, and re-layouts: 0.09 us -> 1.32 us
  transfers between devices with their start and end apart: 6 -> 5, of which waited for: 3 -> 2; matrix products, arithmetic and copies ran while one was open for 0% -> 0% of each run, Pallas kernels for 7% -> 8%
where the time goes in v5:
time: 102 us
  blocking collectives  71.6 us (70%)
  starting transfers between devices  13.6 us (13%)
  Pallas kernels  9.09 us (9%)
  waiting for transfers between devices  5.45 us (5%)
  local copies, waits for them, and re-layouts  1.34 us (1%)
    all_gather x4, blocking collectives, gather(): lax.all_gather(value, 'group', axis_index_groups=[[g, g ^ bits] for g in...  52.4 us
    all_to_all x1, blocking collectives, body(): lax.all_to_all(parts, 'group', 0, 0, tiled=True, axis_index_groups=along_y)  19.2 us
    ppermute x5, starting transfers between devices, send(): return lax.ppermute(value, 'group', [(g, g ^ bits) for g in range(16)])  13.6 us
    ppermute x5, waiting for transfers between devices, send(): return lax.ppermute(value, 'group', [(g, g ^ bits) for g in range(16)])  5.45 us
    pallas_call x1, Pallas kernels, body(): call(root_kernel, array(BS + 16, BS), [VM, VM], [SQUARE, pltpu.VMEM((HALF...  3.87 us
  transfers between devices with their start and end apart: 5, of which 2 were waited for; matrix products, arithmetic and copies ran while one was open for 0% of the time, Pallas kernels for 8%

profile of v5, /device:TPU:39, one launch (start us, length us, event | category | flops | bytes accessed | tf_op | source)
XLA Modules:
  0.0 101.8 jit_solution(7987298067472389600)
XLA Ops:
  0.6 0.0 copy-start.1
  0.6 1.2 %copy-done.1 = bf16[1,2,512,512]{3,2,1,0:T(8,128)(2,1)S(1)} copy-done((bf16[1,2,512,512]{3,2,1,0:T(8,128)(2,1)S(1)}, bf16[1,2,512,512]{3,2,1,0:T(8,128)(2,1)}, u32[]{:S(2)}) %copy-start.1) | copy-done | bytes 1048600
  1.9 0.1 shard_map.51
  1.9 0.0 copy-start.2
  1.9 0.0 copy-start
  1.9 2.7 %collective-permute-start = (bf16[2,256,512]{2,1,0:T(8,128)(2,1)S(1)}, bf16[2,256,512]{2,1,0:T(8,128)(2,1)S(1)}, u32[]{:S(2)}, u32[]{:S(2)}) collective-permute-start(bf16[2,256,512]{2,1,0:T(8,128)(2,1)S(1)} %shard_map.51), channel_id=1, source_target_pairs={{0,32},{32,0},{64,96},{96,64},{128,160},{160,128},{192,224},{224,1... | collective-permute-start | bytes 1572872 | tf_op jit(solution)/shard_map/ppermute | solution.py:254
  4.7 0.1 shard_map.50.keep
  4.7 0.0 copy-done.2
  4.8 0.1 copy.13.owner
  4.8 0.0 copy-done
  4.8 0.1 shard_map.52.packed
  4.9 1.3 %collective-permute-done.got = bf16[2,256,512]{2,1,0:T(8,128)(2,1)S(1)} collective-permute-done((bf16[2,256,512]{2,1,0:T(8,128)(2,1)S(1)}, bf16[2,256,512]{2,1,0:T(8,128)(2,1)S(1)}, u32[]{:S(2)}, u32[]{:S(2)}) %collective-permute-start) | collective-permute-done | bytes 524320 | tf_op jit(solution)/shard_map/ppermute | solution.py:254
  6.2 0.1 shard_map.53
  6.3 19.2 %all_to_all.5.got = bf16[4,272,512]{2,1,0:T(8,128)(2,1)S(1)} all-to-all(bf16[4,272,512]{2,1,0:T(8,128)(2,1)S(1)} %shard_map.53), channel_id=1, replica_groups={{0,64,128,192},{32,96,160,224},{256,320,384,448},{288,352,416,480},{1,6..., dimensions={0} | all-to-all | bytes 2228224 | tf_op jit(solution)/shard_map/all_to_all | solution.py:266
  25.5 0.2 shard_map.54
  25.7 37.4 %all-gather = bf16[544,512]{1,0:T(8,128)(2,1)S(1)} all-gather(bf16[272,512]{1,0:T(8,128)(2,1)S(1)} %shard_map.54), channel_id=2, replica_groups={{0,256},{32,288},{64,320},{96,352},{128,384},{160,416},{192,448},{224,4..., dimensions={0}, use_global_device_ids=true | all-gather | bytes 835584 | tf_op jit(solution)/shard_map/all_gather | solution.py:257
  63.1 0.2 shard_map.55
  63.2 7.2 %all-gather.1 = bf16[544,512]{1,0:T(8,128)(2,1)S(1)} all-gather(bf16[272,512]{1,0:T(8,128)(2,1)S(1)} %shard_map.55), channel_id=3, replica_groups={{0,64},{32,96},{128,192},{160,224},{256,320},{288,352},{384,448},{416,4..., dimensions={0}, use_global_device_ids=true | all-gather | bytes 835584 | tf_op jit(solution)/shard_map/all_gather | solution.py:257
  70.4 2.8 %collective-permute-start.1 = (bf16[256,512]{1,0:T(8,128)(2,1)S(1)}, bf16[256,512]{1,0:T(8,128)(2,1)S(1)}, u32[]{:S(2)}, u32[]{:S(2)}) collective-permute-start(bf16[256,512]{1,0:T(8,128)(2,1)S(1)} %bitcast.19), channel_id=1, source_target_pairs={{0,192},{32,224},{64,128},{96,160},{128,64},{160,96},{192,0},{224,... | collective-permute-start | bytes 786440 | tf_op jit(solution)/shard_map/ppermute | solution.py:254
  73.2 4.7 %all_gather.25 = bf16[2,256,512]{2,1,0:T(8,128)(2,1)S(1)} all-gather(bf16[1,256,512]{2,1,0:T(8,128)(2,1)S(1)} %bitcast.20), channel_id=1, replica_groups={{0,32},{64,96},{128,160},{192,224},{256,288},{320,352},{384,416},{448,4..., dimensions={0}, use_global_device_ids=true | all-gather | bytes 786432 | tf_op jit(solution)/shard_map/all_gather | solution.py:257
  77.9 3.9 %shard_map.56.mine = bf16[528,512]{1,0:T(8,128)(2,1)S(1)} custom-call(bf16[2,272,512]{2,1,0:T(8,128)(2,1)S(1)} %bitcast.17, bf16[512,512]{1,0:T(8,128)(2,1)S(1)} %bitcast.8), custom_call_target="tpu_custom_call" | custom-call | flops 2684354560 | tf_op jit(solution)/shard_map/pallas_call | solution.py:273
  81.8 0.0 collective-permute-done.1.away
  81.8 2.6 %collective-permute-start.3 = (bf16[528,512]{1,0:T(8,128)(2,1)S(1)}, bf16[528,512]{1,0:T(8,128)(2,1)S(1)}, u32[]{:S(2)}, u32[]{:S(2)}) collective-permute-start(bf16[528,512]{1,0:T(8,128)(2,1)S(1)} %shard_map.56.mine), channel_id=1, source_target_pairs={{0,32},{32,0},{64,96},{96,64},{128,160},{160,128},{192,224},{224,1... | collective-permute-start | bytes 1622024 | tf_op jit(solution)/shard_map/ppermute | solution.py:254
  84.4 1.9 %collective-permute-start.2 = (bf16[256,512]{1,0:T(8,128)(2,1)S(1)}, bf16[256,512]{1,0:T(8,128)(2,1)S(1)}, u32[]{:S(2)}, u32[]{:S(2)}) collective-permute-start(bf16[256,512]{1,0:T(8,128)(2,1)S(1)} %collective-permute-done.1.away), channel_id=1, source_target_pairs={{0,32},{32,0},{64,96},{96,64},{128,160},{160,128},{192,224},{224,1... | collective-permute-start | bytes 786440 | tf_op jit(solution)/shard_map/ppermute | solution.py:254
  86.3 0.0 collective-permute-done.3.other
  86.3 1.1 %shard_map.58 = (bf16[512,512]{1,0:T(8,128)(2,1)S(1)}, bf16[256,512]{1,0:T(8,128)(2,1)S(1)}) custom-call(bf16[528,512]{1,0:T(8,128)(2,1)S(1)} %shard_map.56.mine, bf16[528,512]{1,0:T(8,128)(2,1)S(1)} %collective-permute-done.3.other, bf16[512,512]{1,0:T(8,128)(2,1)S(1)} %bitcast.9), custom_call_target="tpu_custom_call" | custom-call | flops 268435456 | tf_op jit(solution)/shard_map/pallas_call | solution.py:284
  87.4 3.6 %collective-permute-start.4 = (bf16[256,512]{1,0:T(8,128)(2,1)S(1)}, bf16[256,512]{1,0:T(8,128)(2,1)S(1)}, u32[]{:S(2)}, u32[]{:S(2)}) collective-permute-start(bf16[256,512]{1,0:T(8,128)(2,1)S(1)} %get-tuple-element.8), channel_id=1, source_target_pairs={{0,192},{32,224},{64,128},{96,160},{128,64},{160,96},{192,0},{224,... | collective-permute-start | bytes 786440 | tf_op jit(solution)/shard_map/ppermute | solution.py:254
  91.0 0.0 collective-permute-done.2.far
  91.0 1.9 %shard_map.57 = f32[512,512]{1,0:T(8,128)} custom-call(s32[32,2]{1,0:T(8,128)S(1)} %copy.13.owner, bf16[512,512]{1,0:T(8,128)(2,1)S(1)} %bitcast.10, bf16[256,512]{1,0:T(8,128)(2,1)S(1)} %collective-permute-done.1.away, bf16[256,512]{1,0:T(8,128)(2,1)S(1)} %collective-permute-done.2.far, f32[512,512]{1,0:T(8,128)S(1)} %bitcast.12), custom_call_target="tpu_custom_call" | custom-call | flops 268435456 | bytes 3145728 | tf_op jit(solution)/shard_map/pallas_call | solution.py:288
  92.9 0.8 shard_map.59.begun
  93.7 4.2 %collective-permute-done.4 = bf16[256,512]{1,0:T(8,128)(2,1)S(1)} collective-permute-done((bf16[256,512]{1,0:T(8,128)(2,1)S(1)}, bf16[256,512]{1,0:T(8,128)(2,1)S(1)}, u32[]{:S(2)}, u32[]{:S(2)}) %collective-permute-start.4) | collective-permute-done | bytes 262176 | tf_op jit(solution)/shard_map/ppermute | solution.py:254
  97.9 3.1 %all-gather.2.other = bf16[512,512]{1,0:T(8,128)(2,1)S(1)} all-gather(bf16[256,512]{1,0:T(8,128)(2,1)S(1)} %collective-permute-done.4), channel_id=4, replica_groups={{0,32},{64,96},{128,160},{192,224},{256,288},{320,352},{384,416},{448,4..., dimensions={0}, use_global_device_ids=true | all-gather | bytes 786432 | tf_op jit(solution)/shard_map/all_gather | solution.py:257
  101.0 0.8 shard_map.60
  (1 shorter events, 0.0 us)
Async XLA Ops:
  0.6 1.2 %copy-start.1 = (bf16[1,2,512,512]{3,2,1,0:T(8,128)(2,1)S(1)}, bf16[1,2,512,512]{3,2,1,0:T(8,128)(2,1)}, u32[]{:S(2)}) copy-start(bf16[1,2,512,512]{3,2,1,0:T(8,128)(2,1)} %param.3) | copy-start | bytes 3145732
  1.9 2.8 %copy-start.2 = (s32[32,2]{0,1:T(2,128)S(1)}, s32[32,2]{0,1:T(2,128)}, u32[]{:S(2)}) copy-start(s32[32,2]{0,1:T(2,128)} %param.5) | copy-start | bytes 772
  1.9 2.9 %copy-start = (f32[1,1,512,512]{3,2,1,0:T(8,128)S(1)}, f32[1,1,512,512]{3,2,1,0:T(8,128)}, u32[]{:S(2)}) copy-start(f32[1,1,512,512]{3,2,1,0:T(8,128)} %param.4) | copy-start | bytes 3145732
  1.9 4.2 %collective-permute-start = (bf16[2,256,512]{2,1,0:T(8,128)(2,1)S(1)}, bf16[2,256,512]{2,1,0:T(8,128)(2,1)S(1)}, u32[]{:S(2)}, u32[]{:S(2)}) collective-permute-start(bf16[2,256,512]{2,1,0:T(8,128)(2,1)S(1)} %shard_map.51), channel_id=1, source_target_pairs={{0,32},{32,0},{64,96},{96,64},{128,160},{160,128},{192,224},{224,1... | collective-permute-start | bytes 1572872 | tf_op jit(solution)/shard_map/ppermute | solution.py:254
  70.4 11.3 %collective-permute-start.1 = (bf16[256,512]{1,0:T(8,128)(2,1)S(1)}, bf16[256,512]{1,0:T(8,128)(2,1)S(1)}, u32[]{:S(2)}, u32[]{:S(2)}) collective-permute-start(bf16[256,512]{1,0:T(8,128)(2,1)S(1)} %bitcast.19), channel_id=1, source_target_pairs={{0,192},{32,224},{64,128},{96,160},{128,64},{160,96},{192,0},{224,... | collective-permute-start | bytes 786440 | tf_op jit(solution)/shard_map/ppermute | solution.py:254
  81.8 4.5 %collective-permute-start.3 = (bf16[528,512]{1,0:T(8,128)(2,1)S(1)}, bf16[528,512]{1,0:T(8,128)(2,1)S(1)}, u32[]{:S(2)}, u32[]{:S(2)}) collective-permute-start(bf16[528,512]{1,0:T(8,128)(2,1)S(1)} %shard_map.56.mine), channel_id=1, source_target_pairs={{0,32},{32,0},{64,96},{96,64},{128,160},{160,128},{192,224},{224,1... | collective-permute-start | bytes 1622024 | tf_op jit(solution)/shard_map/ppermute | solution.py:254
  84.4 6.6 %collective-permute-start.2 = (bf16[256,512]{1,0:T(8,128)(2,1)S(1)}, bf16[256,512]{1,0:T(8,128)(2,1)S(1)}, u32[]{:S(2)}, u32[]{:S(2)}) collective-permute-start(bf16[256,512]{1,0:T(8,128)(2,1)S(1)} %collective-permute-done.1.away), channel_id=1, source_target_pairs={{0,32},{32,0},{64,96},{96,64},{128,160},{160,128},{192,224},{224,1... | collective-permute-start | bytes 786440 | tf_op jit(solution)/shard_map/ppermute | solution.py:254
  87.4 10.5 %collective-permute-start.4 = (bf16[256,512]{1,0:T(8,128)(2,1)S(1)}, bf16[256,512]{1,0:T(8,128)(2,1)S(1)}, u32[]{:S(2)}, u32[]{:S(2)}) collective-permute-start(bf16[256,512]{1,0:T(8,128)(2,1)S(1)} %get-tuple-element.8), channel_id=1, source_target_pairs={{0,192},{32,224},{64,128},{96,160},{128,64},{160,96},{192,0},{224,... | collective-permute-start | bytes 786440 | tf_op jit(solution)/shard_map/ppermute | solution.py:254

commit v6 on v5

v6 whole, which is shorter than its diff:
```python
import jax
import jax.numpy as jnp
from jax import lax
from jax.experimental import pallas as pl
from jax.experimental.pallas import tpu as pltpu
from jax.sharding import PartitionSpec as P

BETA = 0.9
DAMPING = 0.0001
BS = 512
HALF = 256
CHUNK = 64
TILE = 16
STAT = CHUNK + TILE
PART = 2 * CHUNK + STAT
ROWS = 4 * CHUNK + TILE
LIMIT = 40 * 1024 * 1024

BF = jnp.bfloat16
F32 = jnp.float32

VM = pl.BlockSpec(memory_space=pltpu.VMEM)
HBM = pl.BlockSpec(memory_space=pl.ANY)
BLOCKS = range(2)


def call(kernel, shapes, specs, scratch=(), flops=0, nbytes=0, out_spec=VM, **more):
    many = isinstance(shapes, tuple)
    return pl.pallas_call(
        kernel,
        out_shape=shapes,
        in_specs=specs,
        out_specs=(out_spec,) * len(shapes) if many else out_spec,
        scratch_shapes=list(scratch),
        compiler_params=pltpu.CompilerParams(vmem_limit_bytes=LIMIT),
        cost_estimate=pl.CostEstimate(flops=flops, bytes_accessed=nbytes, transcendentals=0),
        **more,
    )


def array(*shape, dtype=BF):
    return jax.ShapeDtypeStruct(shape, dtype)


def place():
    group = lax.axis_index("group")
    return lax.rem(group, 2), lax.rem(lax.div(group, 2), 4), lax.div(group, 8)


def owner_of(owner, block):
    row = lax.broadcasted_iota(jnp.int32, owner.shape, 0) == lax.axis_index("dp")
    col = lax.broadcasted_iota(jnp.int32, owner.shape, 1) == block
    return jnp.sum(jnp.where(row & col, owner[...], 0))


def half_at(core):
    return pl.ds(pl.multiple_of(core * HALF, HALF), HALF)


def mm(a, b):
    return jnp.dot(a.astype(BF), b.astype(BF), preferred_element_type=F32)


def grid_of(n):
    return lax.broadcasted_iota(jnp.int32, (n, n), 0), lax.broadcasted_iota(jnp.int32, (n, n), 1)


def take(other):
    def kernel(grad, out, sems):
        core, _, _ = place()
        rows = half_at(1 - core if other else core)
        copies = [pltpu.make_async_copy(grad.at[b, rows, :], out.at[b], sems.at[b]) for b in range(2)]
        for copy in copies:
            copy.start()
        for copy in copies:
            copy.wait()

    return kernel


def pack_kernel(stat, out):
    row, col = grid_of(HALF)
    corner = stat[HALF:BS, HALF:BS]
    fold = jnp.where(row <= col, stat[0:HALF, 0:HALF], corner).astype(BF)
    diagonal = jnp.sum(jnp.where(row == col, corner, 0.0), axis=0, keepdims=True)
    diagonal = jnp.broadcast_to(diagonal, (TILE, HALF)).astype(BF)
    side = stat[0:HALF, HALF:BS].astype(BF)
    for y in range(4):
        lo = y * CHUNK
        out[y, 0:CHUNK, 0:HALF] = fold[lo : lo + CHUNK]
        out[y, 0:CHUNK, HALF:BS] = side[lo : lo + CHUNK]
        out[y, CHUNK:STAT, 0:HALF] = diagonal
        out[y, CHUNK:STAT, HALF:BS] = diagonal


def first_kernel(keep, got, packed, owner, out):
    del owner
    for y in range(4):
        rows = slice(y * CHUNK, (y + 1) * CHUNK)
        for b in BLOCKS:
            total = (keep[b, rows, :].astype(F32) + got[b, rows, :].astype(F32)).astype(BF)
            out[y, b * CHUNK : (b + 1) * CHUNK, :] = total
        out[y, 2 * CHUNK : PART, :] = packed[y]


def join(first, second):
    row = lax.broadcasted_iota(jnp.int32, (TILE, BS), 0)
    return jnp.where(row < TILE // 2, first.astype(F32), second.astype(F32)).astype(BF)


def second_kernel(owner, got, out):
    total = got[0, 0 : 2 * CHUNK, :].astype(F32)
    for source in range(1, 4):
        total += got[source, 0 : 2 * CHUNK, :].astype(F32)
    out[0 : 2 * CHUNK, :] = total.astype(BF)
    source = [lax.rem(owner_of(owner, b), 4) for b in BLOCKS]
    for b in BLOCKS:
        out[(2 + b) * CHUNK : (3 + b) * CHUNK, :] = got[source[b], 2 * CHUNK : 3 * CHUNK, :]
    out[4 * CHUNK : ROWS, :] = join(*(got[source[b], 3 * CHUNK : PART, :] for b in BLOCKS))


def third_kernel(owner, got, out):
    total = (got[0, 0 : 2 * CHUNK, :].astype(F32) + got[1, 0 : 2 * CHUNK, :].astype(F32)).astype(BF)
    half = [lax.div(owner_of(owner, b), 4) for b in BLOCKS]
    stats = [got[half[b], (2 + b) * CHUNK : (3 + b) * CHUNK, :] for b in BLOCKS]
    diagonals = join(*(got[half[b], 4 * CHUNK : ROWS, :] for b in BLOCKS))
    for y in range(4):
        out[y, 0 : 2 * CHUNK, :] = total
        for b in BLOCKS:
            out[y, (2 + b) * CHUNK : (3 + b) * CHUNK, :] = stats[b]
        out[y, 4 * CHUNK : ROWS, :] = diagonals


def unpack_kernel(got, out):
    row, col = grid_of(HALF)
    damping = jnp.where(row == col, DAMPING, 0.0)
    tile = got[0, 4 * CHUNK : ROWS, 0:HALF].astype(F32)
    for b in BLOCKS:
        rows = slice((2 + b) * CHUNK, (3 + b) * CHUNK)
        packed = BETA * jnp.concatenate([got[y, rows, :] for y in range(4)], axis=0).astype(F32)
        fold = packed[:, 0:HALF]
        turned = fold.T
        at = b * (TILE // 2)
        diagonal = BETA * tile[at : at + 1, :]
        out[b, 0:HALF, 0:HALF] = jnp.where(row <= col, fold, turned) + damping
        out[b, HALF:BS, HALF:BS] = jnp.where(row > col, fold, jnp.where(row < col, turned, diagonal)) + damping
        side = packed[:, HALF:BS]
        out[b, 0:HALF, HALF:BS] = side
        out[b, HALF:BS, 0:HALF] = side.T


def gram_of(core, dense, oriented):
    @pl.when(core == 0)
    def _():
        oriented[...] = dense[...]

    @pl.when(core == 1)
    def _():
        oriented[...] = dense[...].astype(F32).T.astype(BF)

    value = oriented[...]
    return lax.dot_general(value, value, (((1,), (1,)), ((), ())), preferred_element_type=F32)


def newton(currents):
    lows = [m.astype(BF) for m in currents]
    squares = [(1.0 / 16) * mm(low, low) - (10.0 / 16) * m for low, m in zip(lows, currents)]
    slows = [square.astype(BF) for square in squares]
    fourths = [(50.0 / 16) * square + mm(slow, slow) for square, slow in zip(squares, slows)]
    return [(625.0 / 256) * m + mm(fourth, low) for fourth, low, m in zip(fourths, lows, currents)]


def root_kernel(got, far, stat, out, dense, oriented):
    core, _, _ = place()
    for b in BLOCKS:
        rows = slice(b * CHUNK, (b + 1) * CHUNK)
        for y in range(4):
            for where, source in ((core, got), (1 - core, far)):
                at = pl.multiple_of(where * HALF + y * CHUNK, CHUNK)
                dense[b, pl.ds(at, CHUNK), :] = source[y, rows, :]
    shifted = [stat[b] + (1.0 - BETA) * gram_of(core, dense.at[b], oriented.at[b]) for b in BLOCKS]
    frobs = [jnp.sqrt(jnp.sum(m * m, keepdims=True)) for m in shifted]
    m0 = [m * (1.0 / frob) for m, frob in zip(shifted, frobs)]
    m1 = newton(m0)
    m2 = newton(m1)
    n01 = [(-1.25 / 4) * (p + q) + (1.0 / 16) * mm(p, q) for p, q in zip(m0, m1)]
    excess = [1.25 * n - (1.5625 / 4) * m - 0.25 * mm(n, m) for n, m in zip(n01, m2)]
    scales = [lax.rsqrt(jnp.sqrt(frob)) for frob in frobs]

    @pl.when(core == 0)
    def _():
        for b in BLOCKS:
            block = dense[b]
            value = scales[b] * (1.953125 * block.astype(F32) + mm(excess[b], block))
            out[b * BS : (b + 1) * BS, :] = value.astype(BF)
        out[2 * BS : 2 * BS + TILE, :] = jnp.zeros((TILE, BS), BF)

    @pl.when(core == 1)
    def _():
        line = lax.broadcasted_iota(jnp.int32, (TILE, BS), 0)
        tail = jnp.zeros((TILE, BS), F32)
        for b in BLOCKS:
            out[b * BS : (b + 1) * BS, :] = excess[b].astype(BF)
            value = jnp.broadcast_to(scales[b], (TILE, BS))
            for term in range(3):
                high = value.astype(BF).astype(F32)
                tail = jnp.where(line == b * (TILE // 2) + term, high, tail)
                value = value - high
        out[2 * BS : 2 * BS + TILE, :] = tail.astype(BF)


def stat_kernel(owner, dense, stat, out, oriented):
    core, y, half = place()
    pair = half * 4 + y
    owned = [owner_of(owner, b) == pair for b in BLOCKS]
    for b in BLOCKS:

        @pl.when(owned[b])
        def _():
            out[...] = BETA * stat[...] + (1.0 - BETA) * gram_of(core, dense.at[b], oriented)

    @pl.when(jnp.logical_not(jnp.logical_or(*owned)))
    def _():
        out[...] = stat[...]


def product_kernel(mine, other, dense, out, done, sems):
    core, _, _ = place()

    def products(left, right):
        tail = right[2 * BS : 2 * BS + TILE, :].astype(F32)
        for b in BLOCKS:
            at = b * (TILE // 2)
            scale = tail[at : at + 1, 0:1] + tail[at + 1 : at + 2, 0:1] + tail[at + 2 : at + 3, 0:1]
            rows = slice(b * BS, (b + 1) * BS)
            low = left[rows, :]
            precond = scale * (1.953125 * low.astype(F32) + mm(low, right[rows, :]))
            value = dense[b].astype(F32)
            grad_sq = jnp.sum(value * value, keepdims=True)
            pre_sq = jnp.sum(precond * precond, keepdims=True)
            done[b] = (precond * jnp.sqrt(grad_sq / (pre_sq + 1e-06))).astype(BF)
            pltpu.make_async_copy(done.at[b], out.at[b], sems.at[b]).start()

    @pl.when(core == 0)
    def _():
        products(mine, other)

    @pl.when(core == 1)
    def _():
        products(other, mine)

    for b in BLOCKS:
        pltpu.make_async_copy(done.at[b], out.at[b], sems.at[b]).wait()


def body(grad, stats, owner):
    along_y = [[h * 8 + 2 * k + c for k in range(4)] for h in range(2) for c in range(2)]

    def send(value, bits):
        return lax.ppermute(value, "group", [(g, g ^ bits) for g in range(16)])

    def gather(value, bits):
        return lax.all_gather(value, "group", axis_index_groups=[[g, g ^ bits] for g in range(16) if g < g ^ bits])

    def exchange(value):
        return lax.all_to_all(value, "group", 0, 0, tiled=True, axis_index_groups=along_y)

    block = grad[0]
    stat = stats[0, 0]
    pieces = [call(take(other), array(2, HALF, BS), [HBM], [pltpu.SemaphoreType.DMA((2,))]) for other in (True, False)]
    got = send(pieces[0](block), 1)
    keep = pieces[1](block)
    packed = call(pack_kernel, array(4, STAT, BS), [VM], nbytes=3 << 19)(stat)
    parts = exchange(call(first_kernel, array(4, PART, BS), [VM, VM, VM, VM])(keep, got, packed, owner))
    partial = call(second_kernel, array(ROWS, BS), [VM, VM])(owner, parts)
    parts = exchange(call(third_kernel, array(4, ROWS, BS), [VM, VM])(owner, gather(partial, 8)))
    far = send(parts[:, : 2 * CHUNK], 1)
    shifted = call(unpack_kernel, array(2, BS, BS, dtype=F32), [VM], nbytes=5 << 19)(parts)
    pair = pltpu.VMEM((2, BS, BS), BF)
    payload, dense = call(
        root_kernel, (array(2 * BS + TILE, BS), array(2, BS, BS)), [VM, VM, VM], [pair], flops=20 * 2 * BS**3
    )(parts, far, shifted)
    received = send(payload, 1)
    new_stat = call(
        stat_kernel, array(BS, BS, dtype=F32), [VM, VM, VM], [pltpu.VMEM((BS, BS), BF)], flops=2 * BS**3, nbytes=3 << 20
    )(owner, dense, stat)
    update = call(
        product_kernel,
        array(2, BS, BS),
        [VM, VM, VM],
        [pair, pltpu.SemaphoreType.DMA((2,))],
        flops=4 * BS**3,
        out_spec=HBM,
    )(payload, received, dense)
    return (new_stat[None, None], update)


def solution(mesh):
    in_specs = (P("group", "dp", None, None), P("group", "dp", None, None), P())
    out_specs = (P("group", "dp", None, None), P("dp", None, None))
    return jax.shard_map(body, mesh=mesh, in_specs=in_specs, out_specs=out_specs, check_vma=False)
```

time: 102 us -> 97.4 us (0.955)
  the two profiles are of different devices: /device:TPU:39 before, /device:TPU:33 now
where the time goes in v6:
time: 97.4 us; the launch traced here: 97.1 us
  blocking collectives  70.1 us (72%)
  Pallas kernels  11.3 us (12%)
  starting transfers between devices  10.1 us (10%)
  waiting for transfers between devices  3.53 us (4%)
  local copies, waits for them, and re-layouts  1.35 us (1%)
    all_gather x1, blocking collectives, gather(): lax.all_gather(value, 'group', axis_index_groups=[[g, g ^ bits] for g in...  37.4 us
    all_to_all x2, blocking collectives, exchange(): lax.all_to_all(value, 'group', 0, 0, tiled=True, axis_index_groups=along_y)  32.7 us
    ppermute x3, starting transfers between devices, send(): return lax.ppermute(value, 'group', [(g, g ^ bits) for g in range(16)])  10.1 us
    pallas_call x1, Pallas kernels, body(): call(root_kernel, (array(2 * BS + TILE, BS), array(2, BS, BS)), [VM, VM,...  6.72 us
    ppermute x3, waiting for transfers between devices, send(): return lax.ppermute(value, 'group', [(g, g ^ bits) for g in range(16)])  3.53 us
    pallas_call x1, Pallas kernels, body(): call(product_kernel, array(2, BS, BS), [VM, VM, VM], [pair, pltpu.Semapho...  2.45 us
  transfers between devices with their start and end apart: 3, of which 3 were waited for; matrix products, arithmetic and copies ran while one was open for 0% of the time, Pallas kernels for 2%

profile of v6, /device:TPU:33, one launch (start us, length us, event | category | flops | bytes accessed | tf_op | source)
XLA Modules:
  0.0 97.1 jit_solution(16929608696742720276)
XLA Ops:
  0.6 0.0 copy-start.1
  0.6 1.2 %copy-done.1 = bf16[1,2,512,512]{3,2,1,0:T(8,128)(2,1)S(1)} copy-done((bf16[1,2,512,512]{3,2,1,0:T(8,128)(2,1)S(1)}, bf16[1,2,512,512]{3,2,1,0:T(8,128)(2,1)}, u32[]{:S(2)}) %copy-start.1) | copy-done | bytes 1048600
  1.9 0.1 shard_map.51
  1.9 0.0 copy-start.2
  1.9 0.0 copy-start
  1.9 2.7 %collective-permute-start = (bf16[2,256,512]{2,1,0:T(8,128)(2,1)S(1)}, bf16[2,256,512]{2,1,0:T(8,128)(2,1)S(1)}, u32[]{:S(2)}, u32[]{:S(2)}) collective-permute-start(bf16[2,256,512]{2,1,0:T(8,128)(2,1)S(1)} %shard_map.51), channel_id=1, source_target_pairs={{0,32},{32,0},{64,96},{96,64},{128,160},{160,128},{192,224},{224,1... | collective-permute-start | bytes 1572872 | tf_op jit(solution)/shard_map/ppermute | solution.py:260
  4.7 0.1 shard_map.50.keep
  4.7 0.0 copy-done.2
  4.8 0.1 copy.8.owner
  4.8 0.0 copy-done
  4.8 0.1 shard_map.52.packed
  4.9 1.3 %collective-permute-done.got = bf16[2,256,512]{2,1,0:T(8,128)(2,1)S(1)} collective-permute-done((bf16[2,256,512]{2,1,0:T(8,128)(2,1)S(1)}, bf16[2,256,512]{2,1,0:T(8,128)(2,1)S(1)}, u32[]{:S(2)}, u32[]{:S(2)}) %collective-permute-start) | collective-permute-done | bytes 524320 | tf_op jit(solution)/shard_map/ppermute | solution.py:260
  6.2 0.1 shard_map.53
  6.3 16.4 %all_to_all.10.got = bf16[4,208,512]{2,1,0:T(8,128)(2,1)S(1)} all-to-all(bf16[4,208,512]{2,1,0:T(8,128)(2,1)S(1)} %shard_map.53), channel_id=1, replica_groups={{0,64,128,192},{32,96,160,224},{256,320,384,448},{288,352,416,480},{1,6..., dimensions={0} | all-to-all | bytes 1703936 | tf_op jit(solution)/shard_map/all_to_all | solution.py:266
  22.7 0.1 shard_map.54
  22.9 37.4 %all-gather = bf16[544,512]{1,0:T(8,128)(2,1)S(1)} all-gather(bf16[272,512]{1,0:T(8,128)(2,1)S(1)} %shard_map.54), channel_id=2, replica_groups={{0,256},{32,288},{64,320},{96,352},{128,384},{160,416},{192,448},{224,4..., dimensions={0}, use_global_device_ids=true | all-gather | bytes 835584 | tf_op jit(solution)/shard_map/all_gather | solution.py:263
  60.2 0.2 shard_map.55
  60.4 16.3 %all_to_all.11.got = bf16[4,272,512]{2,1,0:T(8,128)(2,1)S(1)} all-to-all(bf16[4,272,512]{2,1,0:T(8,128)(2,1)S(1)} %shard_map.55), channel_id=1, replica_groups={{0,64,128,192},{32,96,160,224},{256,320,384,448},{288,352,416,480},{1,6..., dimensions={0} | all-to-all | bytes 2228224 | tf_op jit(solution)/shard_map/all_to_all | solution.py:266
  76.8 4.8 %collective-permute-start.1 = (bf16[4,128,512]{2,1,0:T(8,128)(2,1)S(1)}, bf16[4,128,512]{2,1,0:T(8,128)(2,1)S(1)}, u32[]{:S(2)}, u32[]{:S(2)}) collective-permute-start(bf16[4,128,512]{2,1,0:T(8,128)(2,1)S(1)} %slice.4), channel_id=1, source_target_pairs={{0,32},{32,0},{64,96},{96,64},{128,160},{160,128},{192,224},{224,1... | collective-permute-start | bytes 1572872 | tf_op jit(solution)/shard_map/ppermute | solution.py:260
  81.5 0.4 shard_map.56.stat
  81.9 1.2 %collective-permute-done.1.far = bf16[4,128,512]{2,1,0:T(8,128)(2,1)S(1)} collective-permute-done((bf16[4,128,512]{2,1,0:T(8,128)(2,1)S(1)}, bf16[4,128,512]{2,1,0:T(8,128)(2,1)S(1)}, u32[]{:S(2)}, u32[]{:S(2)}) %collective-permute-start.1) | collective-permute-done | bytes 524320 | tf_op jit(solution)/shard_map/ppermute | solution.py:260
  83.1 6.7 %shard_map.57 = (bf16[1040,512]{1,0:T(8,128)(2,1)S(1)}, bf16[2,512,512]{2,1,0:T(8,128)(2,1)S(1)}) custom-call(bf16[4,272,512]{2,1,0:T(8,128)(2,1)S(1)} %all_to_all.11.got, bf16[4,128,512]{2,1,0:T(8,128)(2,1)S(1)} %collective-permute-done.1.far, f32[2,512,512]{2,1,0:T(8,128)S(1)} %shard_map.56.stat), custom_call_target="tpu_custom_call" | custom-call | flops 5368709120 | tf_op jit(solution)/shard_map/pallas_call | solution.py:280
  89.8 2.6 %collective-permute-start.2 = (bf16[1040,512]{1,0:T(8,128)(2,1)S(1)}, bf16[1040,512]{1,0:T(8,128)(2,1)S(1)}, u32[]{:S(2)}, u32[]{:S(2)}) collective-permute-start(bf16[1040,512]{1,0:T(8,128)(2,1)S(1)} %get-tuple-element.5.mine), channel_id=1, source_target_pairs={{0,32},{32,0},{64,96},{96,64},{128,160},{160,128},{192,224},{224,1... | collective-permute-start | bytes 3194888 | tf_op jit(solution)/shard_map/ppermute | solution.py:260
  92.4 1.2 %shard_map.58 = f32[512,512]{1,0:T(8,128)} custom-call(s32[32,2]{1,0:T(8,128)S(1)} %copy.8.owner, bf16[2,512,512]{2,1,0:T(8,128)(2,1)S(1)} %get-tuple-element.4.dense, f32[512,512]{1,0:T(8,128)S(1)} %bitcast.5), custom_call_target="tpu_custom_call" | custom-call | flops 268435456 | bytes 3145728 | tf_op jit(solution)/shard_map/pallas_call | solution.py:284
  93.5 1.1 %collective-permute-done.2.other = bf16[1040,512]{1,0:T(8,128)(2,1)S(1)} collective-permute-done((bf16[1040,512]{1,0:T(8,128)(2,1)S(1)}, bf16[1040,512]{1,0:T(8,128)(2,1)S(1)}, u32[]{:S(2)}, u32[]{:S(2)}) %collective-permute-start.2) | collective-permute-done | bytes 1064992 | tf_op jit(solution)/shard_map/ppermute | solution.py:260
  94.7 2.5 %shard_map.59 = bf16[2,512,512]{2,1,0:T(8,128)(2,1)} custom-call(bf16[1040,512]{1,0:T(8,128)(2,1)S(1)} %get-tuple-element.5.mine, bf16[1040,512]{1,0:T(8,128)(2,1)S(1)} %collective-permute-done.2.other, bf16[2,512,512]{2,1,0:T(8,128)(2,1)S(1)} %get-tuple-element.4.dense), custom_call_target="tpu_custom_call" | custom-call | flops 536870912 | tf_op jit(solution)/shard_map/pallas_call | solution.py:287
  (1 shorter events, 0.0 us)
Async XLA Ops:
  0.6 1.2 %copy-start.1 = (bf16[1,2,512,512]{3,2,1,0:T(8,128)(2,1)S(1)}, bf16[1,2,512,512]{3,2,1,0:T(8,128)(2,1)}, u32[]{:S(2)}) copy-start(bf16[1,2,512,512]{3,2,1,0:T(8,128)(2,1)} %param.3) | copy-start | bytes 3145732
  1.9 2.8 %copy-start.2 = (s32[32,2]{0,1:T(2,128)S(1)}, s32[32,2]{0,1:T(2,128)}, u32[]{:S(2)}) copy-start(s32[32,2]{0,1:T(2,128)} %param.5) | copy-start | bytes 772
  1.9 2.9 %copy-start = (f32[1,1,512,512]{3,2,1,0:T(8,128)S(1)}, f32[1,1,512,512]{3,2,1,0:T(8,128)}, u32[]{:S(2)}) copy-start(f32[1,1,512,512]{3,2,1,0:T(8,128)} %param.4) | copy-start | bytes 3145732
  1.9 4.2 %collective-permute-start = (bf16[2,256,512]{2,1,0:T(8,128)(2,1)S(1)}, bf16[2,256,512]{2,1,0:T(8,128)(2,1)S(1)}, u32[]{:S(2)}, u32[]{:S(2)}) collective-permute-start(bf16[2,256,512]{2,1,0:T(8,128)(2,1)S(1)} %shard_map.51), channel_id=1, source_target_pairs={{0,32},{32,0},{64,96},{96,64},{128,160},{160,128},{192,224},{224,1... | collective-permute-start | bytes 1572872 | tf_op jit(solution)/shard_map/ppermute | solution.py:260
  76.8 6.3 %collective-permute-start.1 = (bf16[4,128,512]{2,1,0:T(8,128)(2,1)S(1)}, bf16[4,128,512]{2,1,0:T(8,128)(2,1)S(1)}, u32[]{:S(2)}, u32[]{:S(2)}) collective-permute-start(bf16[4,128,512]{2,1,0:T(8,128)(2,1)S(1)} %slice.4), channel_id=1, source_target_pairs={{0,32},{32,0},{64,96},{96,64},{128,160},{160,128},{192,224},{224,1... | collective-permute-start | bytes 1572872 | tf_op jit(solution)/shard_map/ppermute | solution.py:260
  89.8 4.9 %collective-permute-start.2 = (bf16[1040,512]{1,0:T(8,128)(2,1)S(1)}, bf16[1040,512]{1,0:T(8,128)(2,1)S(1)}, u32[]{:S(2)}, u32[]{:S(2)}) collective-permute-start(bf16[1040,512]{1,0:T(8,128)(2,1)S(1)} %get-tuple-element.5.mine), channel_id=1, source_target_pairs={{0,32},{32,0},{64,96},{96,64},{128,160},{160,128},{192,224},{224,1... | collective-permute-start | bytes 3194888 | tf_op jit(solution)/shard_map/ppermute | solution.py:260

commit v7 on v6

--- a/solution.py
+++ b/solution.py
@@ -10,10 +10,11 @@
 BS = 512
 HALF = 256
 CHUNK = 64
-TILE = 16
+TILE = 8
 STAT = CHUNK + TILE
 PART = 2 * CHUNK + STAT
 ROWS = 4 * CHUNK + TILE
+TAIL = 16
 LIMIT = 40 * 1024 * 1024
 
 BF = jnp.bfloat16
@@ -142,32 +143,57 @@
         turned = fold.T
         at = b * (TILE // 2)
         diagonal = BETA * tile[at : at + 1, :]
-        out[b, 0:HALF, 0:HALF] = jnp.where(row <= col, fold, turned) + damping
-        out[b, HALF:BS, HALF:BS] = jnp.where(row > col, fold, jnp.where(row < col, turned, diagonal)) + damping
-        side = packed[:, HALF:BS]
-        out[b, 0:HALF, HALF:BS] = side
-        out[b, HALF:BS, 0:HALF] = side.T
-
-
-def gram_of(core, dense, oriented):
+        out[b, 0] = jnp.where(row <= col, fold, turned) + damping
+        out[b, 1] = packed[:, HALF:BS]
+        out[b, 2] = jnp.where(row > col, fold, jnp.where(row < col, turned, diagonal)) + damping
+
+
+def whole(corners):
+    first, side, last = (corner.astype(BF) for corner in corners)
+    top = jnp.concatenate([first, side], axis=1)
+    return jnp.concatenate([top, jnp.concatenate([side.T, last], axis=1)], axis=0)
+
+
+def corners_of(left, right, contract):
+    numbers = (((1,), (contract,)), ((), ()))
+    top = lax.dot_general(left[0:HALF], right, numbers, preferred_element_type=F32)
+    tail = right[:, HALF:BS] if contract == 0 else right[HALF:BS]
+    last = lax.dot_general(left[HALF:BS], tail, numbers, preferred_element_type=F32)
+    return top[:, 0:HALF], top[:, HALF:BS], last
+
+
+def mix(*terms):
+    mixed = []
+    for corner in range(3):
+        total = None
+        for factor, corners in terms:
+            value = corners[corner] if factor == 1 else factor * corners[corner]
+            total = value if total is None else total + value
+        mixed.append(total)
+    return tuple(mixed)
+
+
+def newton(currents):
+    lows = [whole(m) for m in currents]
+    parts = [mix((1, corners_of(low, low, 0)), (-2.5, m)) for low, m in zip(lows, currents)]
+    slows = [whole(part) for part in parts]
+    fourths = [whole(mix((1, corners_of(slow, slow, 0)), (3.125, part))) for slow, part in zip(slows, parts)]
+    later = [mix((1, corners_of(four, low, 0)), (2.44140625, m)) for four, low, m in zip(fourths, lows, currents)]
+    return later, lows
+
+
+def squares(matrix):
+    return jnp.sum(matrix * matrix, keepdims=True)
+
+
+def oriented_into(core, dense, oriented):
     @pl.when(core == 0)
     def _():
         oriented[...] = dense[...]
 
     @pl.when(core == 1)
     def _():
-        oriented[...] = dense[...].astype(F32).T.astype(BF)
-
-    value = oriented[...]
-    return lax.dot_general(value, value, (((1,), (1,)), ((), ())), preferred_element_type=F32)
-
-
-def newton(currents):
-    lows = [m.astype(BF) for m in currents]
-    squares = [(1.0 / 16) * mm(low, low) - (10.0 / 16) * m for low, m in zip(lows, currents)]
-    slows = [square.astype(BF) for square in squares]
-    fourths = [(50.0 / 16) * square + mm(slow, slow) for square, slow in zip(squares, slows)]
-    return [(625.0 / 256) * m + mm(fourth, low) for fourth, low, m in zip(fourths, lows, currents)]
+        oriented[...] = dense[...].T
 
 
 def root_kernel(got, far, stat, out, dense, oriented):
@@ -178,13 +204,17 @@
             for where, source in ((core, got), (1 - core, far)):
                 at = pl.multiple_of(where * HALF + y * CHUNK, CHUNK)
                 dense[b, pl.ds(at, CHUNK), :] = source[y, rows, :]
-    shifted = [stat[b] + (1.0 - BETA) * gram_of(core, dense.at[b], oriented.at[b]) for b in BLOCKS]
-    frobs = [jnp.sqrt(jnp.sum(m * m, keepdims=True)) for m in shifted]
-    m0 = [m * (1.0 / frob) for m, frob in zip(shifted, frobs)]
-    m1 = newton(m0)
-    m2 = newton(m1)
-    n01 = [(-1.25 / 4) * (p + q) + (1.0 / 16) * mm(p, q) for p, q in zip(m0, m1)]
-    excess = [1.25 * n - (1.5625 / 4) * m - 0.25 * mm(n, m) for n, m in zip(n01, m2)]
+        oriented_into(core, dense.at[b], oriented.at[b])
+    sides = [oriented[b] for b in BLOCKS]
+    grams = [corners_of(side, side, 1) for side in sides]
+    shifted = [mix((1, tuple(stat[b, k] for k in range(3))), (1.0 - BETA, grams[b])) for b in BLOCKS]
+    frobs = [jnp.sqrt(squares(m[0]) + 2.0 * squares(m[1]) + squares(m[2])) for m in shifted]
+    b0 = [tuple(corner * (0.25 / frob) for corner in m) for m, frob in zip(shifted, frobs)]
+    b1, low0 = newton(b0)
+    b2, low1 = newton(b1)
+    n01 = [mix((1, corners_of(p, q, 0)), (-1.25, u), (-1.25, v)) for p, q, u, v in zip(low0, low1, b0, b1)]
+    ends = [corners_of(whole(n), whole(m), 0) for n, m in zip(n01, b2)]
+    excess = [whole(mix((1.25, n), (-1.5625, m), (-1.0, end))) for n, m, end in zip(n01, b2, ends)]
     scales = [lax.rsqrt(jnp.sqrt(frob)) for frob in frobs]
 
     @pl.when(core == 0)
@@ -193,52 +223,54 @@
             block = dense[b]
             value = scales[b] * (1.953125 * block.astype(F32) + mm(excess[b], block))
             out[b * BS : (b + 1) * BS, :] = value.astype(BF)
-        out[2 * BS : 2 * BS + TILE, :] = jnp.zeros((TILE, BS), BF)
+        out[2 * BS : 2 * BS + TAIL, :] = jnp.zeros((TAIL, BS), BF)
 
     @pl.when(core == 1)
     def _():
-        line = lax.broadcasted_iota(jnp.int32, (TILE, BS), 0)
-        tail = jnp.zeros((TILE, BS), F32)
-        for b in BLOCKS:
-            out[b * BS : (b + 1) * BS, :] = excess[b].astype(BF)
-            value = jnp.broadcast_to(scales[b], (TILE, BS))
+        line = lax.broadcasted_iota(jnp.int32, (TAIL, BS), 0)
+        tail = jnp.zeros((TAIL, BS), F32)
+        for b in BLOCKS:
+            out[b * BS : (b + 1) * BS, :] = excess[b]
+            value = jnp.broadcast_to(scales[b], (TAIL, BS))
             for term in range(3):
                 high = value.astype(BF).astype(F32)
-                tail = jnp.where(line == b * (TILE // 2) + term, high, tail)
+                tail = jnp.where(line == b * 8 + term, high, tail)
                 value = value - high
-        out[2 * BS : 2 * BS + TILE, :] = tail.astype(BF)
-
-
-def stat_kernel(owner, dense, stat, out, oriented):
+        out[2 * BS : 2 * BS + TAIL, :] = tail.astype(BF)
+
+
+def stat_kernel(owner, dense, stat, out, sums, oriented):
     core, y, half = place()
     pair = half * 4 + y
     owned = [owner_of(owner, b) == pair for b in BLOCKS]
     for b in BLOCKS:
+        sums[b] = jnp.broadcast_to(squares(dense[b].astype(F32)), (8, 128))
 
         @pl.when(owned[b])
         def _():
-            out[...] = BETA * stat[...] + (1.0 - BETA) * gram_of(core, dense.at[b], oriented)
+            oriented_into(core, dense.at[b], oriented)
+            side = oriented[...]
+            gram = lax.dot_general(side, side, (((1,), (1,)), ((), ())), preferred_element_type=F32)
+            out[...] = BETA * stat[...] + (1.0 - BETA) * gram
 
     @pl.when(jnp.logical_not(jnp.logical_or(*owned)))
     def _():
         out[...] = stat[...]
 
 
-def product_kernel(mine, other, dense, out, done, sems):
+def product_kernel(mine, other, sums, out, done, sems):
     core, _, _ = place()
 
     def products(left, right):
-        tail = right[2 * BS : 2 * BS + TILE, :].astype(F32)
-        for b in BLOCKS:
-            at = b * (TILE // 2)
+        tail = right[2 * BS : 2 * BS + TAIL, :].astype(F32)
+        for b in BLOCKS:
+            at = b * 8
             scale = tail[at : at + 1, 0:1] + tail[at + 1 : at + 2, 0:1] + tail[at + 2 : at + 3, 0:1]
             rows = slice(b * BS, (b + 1) * BS)
             low = left[rows, :]
             precond = scale * (1.953125 * low.astype(F32) + mm(low, right[rows, :]))
-            value = dense[b].astype(F32)
-            grad_sq = jnp.sum(value * value, keepdims=True)
-            pre_sq = jnp.sum(precond * precond, keepdims=True)
-            done[b] = (precond * jnp.sqrt(grad_sq / (pre_sq + 1e-06))).astype(BF)
+            ratio = jnp.sqrt(sums[b, 0:1, 0:1] / (squares(precond) + 1e-06))
+            done[b] = (precond * ratio).astype(BF)
             pltpu.make_async_copy(done.at[b], out.at[b], sems.at[b]).start()
 
     @pl.when(core == 0)
@@ -275,14 +307,19 @@
     partial = call(second_kernel, array(ROWS, BS), [VM, VM])(owner, parts)
     parts = exchange(call(third_kernel, array(4, ROWS, BS), [VM, VM])(owner, gather(partial, 8)))
     far = send(parts[:, : 2 * CHUNK], 1)
-    shifted = call(unpack_kernel, array(2, BS, BS, dtype=F32), [VM], nbytes=5 << 19)(parts)
+    shifted = call(unpack_kernel, array(2, 3, HALF, HALF, dtype=F32), [VM], nbytes=5 << 19)(parts)
     pair = pltpu.VMEM((2, BS, BS), BF)
     payload, dense = call(
-        root_kernel, (array(2 * BS + TILE, BS), array(2, BS, BS)), [VM, VM, VM], [pair], flops=20 * 2 * BS**3
+        root_kernel, (array(2 * BS + TAIL, BS), array(2, BS, BS)), [VM, VM, VM], [pair], flops=20 * 2 * BS**3
     )(parts, far, shifted)
     received = send(payload, 1)
-    new_stat = call(
-        stat_kernel, array(BS, BS, dtype=F32), [VM, VM, VM], [pltpu.VMEM((BS, BS), BF)], flops=2 * BS**3, nbytes=3 << 20
+    new_stat, sums = call(
+        stat_kernel,
+        (array(BS, BS, dtype=F32), array(2, 8, 128, dtype=F32)),
+        [VM, VM, VM],
+        [pltpu.VMEM((BS, BS), BF)],
+        flops=2 * BS**3,
+        nbytes=3 << 20,
     )(owner, dense, stat)
     update = call(
         product_kernel,
@@ -291,7 +328,7 @@
         [pair, pltpu.SemaphoreType.DMA((2,))],
         flops=4 * BS**3,
         out_spec=HBM,
-    )(payload, received, dense)
+    )(payload, received, sums)
     return (new_stat[None, None], update)
 
 

time: 97.4 us -> 94.2 us (0.967)
  blocking collectives: 70.1 us -> 68.8 us
    ppermute x3, waiting for transfers between devices: 3.53 us -> 2.56 us  [send(): return lax.ppermute(value, 'group', [(g, g ^ bits) for g in range(16)])]
  transfers between devices with their start and end apart: 3 -> 3, of which waited for: 3 -> 2; matrix products, arithmetic and copies ran while one was open for 0% -> 0% of each run, Pallas kernels for 2% -> 3%
where the time goes in v7:
time: 94.2 us; the launch traced here: 93.9 us
  blocking collectives  68.8 us (73%)
  Pallas kernels  10.5 us (11%)
  starting transfers between devices  9.98 us (11%)
  waiting for transfers between devices  2.56 us (3%)
  local copies, waits for them, and re-layouts  1.36 us (1%)
    all_gather x1, blocking collectives, gather(): lax.all_gather(value, 'group', axis_index_groups=[[g, g ^ bits] for g in...  36.7 us
    all_to_all x2, blocking collectives, exchange(): lax.all_to_all(value, 'group', 0, 0, tiled=True, axis_index_groups=along_y)  32.1 us
    ppermute x3, starting transfers between devices, send(): return lax.ppermute(value, 'group', [(g, g ^ bits) for g in range(16)])  9.98 us
    pallas_call x1, Pallas kernels, body(): call(root_kernel, (array(2 * BS + TAIL, BS), array(2, BS, BS)), [VM, VM,...  4.9 us
    ppermute x3, waiting for transfers between devices, send(): return lax.ppermute(value, 'group', [(g, g ^ bits) for g in range(16)])  2.56 us
    pallas_call x1, Pallas kernels, body(): call(stat_kernel, (array(BS, BS, dtype=F32), array(2, 8, 128, dtype=F32))...  2.43 us
    pallas_call x1, Pallas kernels, body(): call(product_kernel, array(2, BS, BS), [VM, VM, VM], [pair, pltpu.Semapho...  2.35 us
  transfers between devices with their start and end apart: 3, of which 2 were waited for; matrix products, arithmetic and copies ran while one was open for 0% of the time, Pallas kernels for 3%

profile of v7, /device:TPU:33, one launch (start us, length us, event | category | flops | bytes accessed | tf_op | source)
XLA Modules:
  0.0 93.9 jit_solution(12059400816108115041)
XLA Ops:
  0.6 0.0 copy-start
  0.6 1.2 %copy-done = bf16[1,2,512,512]{3,2,1,0:T(8,128)(2,1)S(1)} copy-done((bf16[1,2,512,512]{3,2,1,0:T(8,128)(2,1)S(1)}, bf16[1,2,512,512]{3,2,1,0:T(8,128)(2,1)}, u32[]{:S(2)}) %copy-start) | copy-done | bytes 1048600
  1.9 0.1 shard_map.51
  1.9 0.0 copy-start.2
  1.9 0.0 copy-start.1
  1.9 2.7 %collective-permute-start = (bf16[2,256,512]{2,1,0:T(8,128)(2,1)S(1)}, bf16[2,256,512]{2,1,0:T(8,128)(2,1)S(1)}, u32[]{:S(2)}, u32[]{:S(2)}) collective-permute-start(bf16[2,256,512]{2,1,0:T(8,128)(2,1)S(1)} %shard_map.51), channel_id=1, source_target_pairs={{0,32},{32,0},{64,96},{96,64},{128,160},{160,128},{192,224},{224,1... | collective-permute-start | bytes 1572872 | tf_op jit(solution)/shard_map/ppermute | solution.py:292
  4.7 0.1 shard_map.50.keep
  4.7 0.0 copy-done.2
  4.8 0.1 copy.8.owner
  4.8 0.0 copy-done.1
  4.8 0.1 shard_map.52.packed
  4.9 1.3 %collective-permute-done.got = bf16[2,256,512]{2,1,0:T(8,128)(2,1)S(1)} collective-permute-done((bf16[2,256,512]{2,1,0:T(8,128)(2,1)S(1)}, bf16[2,256,512]{2,1,0:T(8,128)(2,1)S(1)}, u32[]{:S(2)}, u32[]{:S(2)}) %collective-permute-start) | collective-permute-done | bytes 524320 | tf_op jit(solution)/shard_map/ppermute | solution.py:292
  6.2 0.1 shard_map.53
  6.3 16.1 %all_to_all.10.got = bf16[4,200,512]{2,1,0:T(8,128)(2,1)S(1)} all-to-all(bf16[4,200,512]{2,1,0:T(8,128)(2,1)S(1)} %shard_map.53), channel_id=1, replica_groups={{0,64,128,192},{32,96,160,224},{256,320,384,448},{288,352,416,480},{1,6..., dimensions={0} | all-to-all | bytes 1638400 | tf_op jit(solution)/shard_map/all_to_all | solution.py:298
  22.4 0.2 shard_map.54
  22.5 36.7 %all-gather = bf16[528,512]{1,0:T(8,128)(2,1)S(1)} all-gather(bf16[264,512]{1,0:T(8,128)(2,1)S(1)} %shard_map.54), channel_id=2, replica_groups={{0,256},{32,288},{64,320},{96,352},{128,384},{160,416},{192,448},{224,4..., dimensions={0}, use_global_device_ids=true | all-gather | bytes 811008 | tf_op jit(solution)/shard_map/all_gather | solution.py:295
  59.2 0.2 shard_map.55
  59.4 16.0 %all_to_all.11.got = bf16[4,264,512]{2,1,0:T(8,128)(2,1)S(1)} all-to-all(bf16[4,264,512]{2,1,0:T(8,128)(2,1)S(1)} %shard_map.55), channel_id=1, replica_groups={{0,64,128,192},{32,96,160,224},{256,320,384,448},{288,352,416,480},{1,6..., dimensions={0} | all-to-all | bytes 2162688 | tf_op jit(solution)/shard_map/all_to_all | solution.py:298
  75.5 4.7 %collective-permute-start.1 = (bf16[4,128,512]{2,1,0:T(8,128)(2,1)S(1)}, bf16[4,128,512]{2,1,0:T(8,128)(2,1)S(1)}, u32[]{:S(2)}, u32[]{:S(2)}) collective-permute-start(bf16[4,128,512]{2,1,0:T(8,128)(2,1)S(1)} %slice.4), channel_id=1, source_target_pairs={{0,32},{32,0},{64,96},{96,64},{128,160},{160,128},{192,224},{224,1... | collective-permute-start | bytes 1572872 | tf_op jit(solution)/shard_map/ppermute | solution.py:292
  80.1 0.2 shard_map.56.stat
  80.4 1.3 %collective-permute-done.1.far = bf16[4,128,512]{2,1,0:T(8,128)(2,1)S(1)} collective-permute-done((bf16[4,128,512]{2,1,0:T(8,128)(2,1)S(1)}, bf16[4,128,512]{2,1,0:T(8,128)(2,1)S(1)}, u32[]{:S(2)}, u32[]{:S(2)}) %collective-permute-start.1) | collective-permute-done | bytes 524320 | tf_op jit(solution)/shard_map/ppermute | solution.py:292
  81.6 4.9 %shard_map.57 = (bf16[1040,512]{1,0:T(8,128)(2,1)S(1)}, bf16[2,512,512]{2,1,0:T(8,128)(2,1)S(1)}) custom-call(bf16[4,264,512]{2,1,0:T(8,128)(2,1)S(1)} %all_to_all.11.got, bf16[4,128,512]{2,1,0:T(8,128)(2,1)S(1)} %collective-permute-done.1.far, f32[2,3,256,256]{3,2,1,0:T(8,128)S(1)} %shard_map.56.stat), custom_call_target="tpu_custom_call" | custom-call | flops 5368709120 | tf_op jit(solution)/shard_map/pallas_call | solution.py:312
  86.5 2.6 %collective-permute-start.2 = (bf16[1040,512]{1,0:T(8,128)(2,1)S(1)}, bf16[1040,512]{1,0:T(8,128)(2,1)S(1)}, u32[]{:S(2)}, u32[]{:S(2)}) collective-permute-start(bf16[1040,512]{1,0:T(8,128)(2,1)S(1)} %get-tuple-element.8.mine), channel_id=1, source_target_pairs={{0,32},{32,0},{64,96},{96,64},{128,160},{160,128},{192,224},{224,1... | collective-permute-start | bytes 3194888 | tf_op jit(solution)/shard_map/ppermute | solution.py:292
  89.2 2.4 %shard_map.58 = (f32[512,512]{1,0:T(8,128)}, f32[2,8,128]{2,1,0:T(8,128)S(1)}) custom-call(s32[32,2]{1,0:T(8,128)S(1)} %copy.8.owner, bf16[2,512,512]{2,1,0:T(8,128)(2,1)S(1)} %get-tuple-element.6.dense, f32[512,512]{1,0:T(8,128)S(1)} %bitcast.7), custom_call_target="tpu_custom_call" | custom-call | flops 268435456 | bytes 3145728 | tf_op jit(solution)/shard_map/pallas_call | solution.py:316
  91.6 0.0 collective-permute-done.2.other
  91.6 2.3 %shard_map.59 = bf16[2,512,512]{2,1,0:T(8,128)(2,1)} custom-call(bf16[1040,512]{1,0:T(8,128)(2,1)S(1)} %get-tuple-element.8.mine, bf16[1040,512]{1,0:T(8,128)(2,1)S(1)} %collective-permute-done.2.other, f32[2,8,128]{2,1,0:T(8,128)S(1)} %get-tuple-element.9.sums), custom_call_target="tpu_custom_call" | custom-call | flops 536870912 | tf_op jit(solution)/shard_map/pallas_call | solution.py:324
  (1 shorter events, 0.0 us)
Async XLA Ops:
  0.6 1.2 %copy-start = (bf16[1,2,512,512]{3,2,1,0:T(8,128)(2,1)S(1)}, bf16[1,2,512,512]{3,2,1,0:T(8,128)(2,1)}, u32[]{:S(2)}) copy-start(bf16[1,2,512,512]{3,2,1,0:T(8,128)(2,1)} %param.3) | copy-start | bytes 3145732
  1.9 2.8 %copy-start.2 = (s32[32,2]{0,1:T(2,128)S(1)}, s32[32,2]{0,1:T(2,128)}, u32[]{:S(2)}) copy-start(s32[32,2]{0,1:T(2,128)} %param.5) | copy-start | bytes 772
  1.9 2.9 %copy-start.1 = (f32[1,1,512,512]{3,2,1,0:T(8,128)S(1)}, f32[1,1,512,512]{3,2,1,0:T(8,128)}, u32[]{:S(2)}) copy-start(f32[1,1,512,512]{3,2,1,0:T(8,128)} %param.4) | copy-start | bytes 3145732
  1.9 4.2 %collective-permute-start = (bf16[2,256,512]{2,1,0:T(8,128)(2,1)S(1)}, bf16[2,256,512]{2,1,0:T(8,128)(2,1)S(1)}, u32[]{:S(2)}, u32[]{:S(2)}) collective-permute-start(bf16[2,256,512]{2,1,0:T(8,128)(2,1)S(1)} %shard_map.51), channel_id=1, source_target_pairs={{0,32},{32,0},{64,96},{96,64},{128,160},{160,128},{192,224},{224,1... | collective-permute-start | bytes 1572872 | tf_op jit(solution)/shard_map/ppermute | solution.py:292
  75.5 6.2 %collective-permute-start.1 = (bf16[4,128,512]{2,1,0:T(8,128)(2,1)S(1)}, bf16[4,128,512]{2,1,0:T(8,128)(2,1)S(1)}, u32[]{:S(2)}, u32[]{:S(2)}) collective-permute-start(bf16[4,128,512]{2,1,0:T(8,128)(2,1)S(1)} %slice.4), channel_id=1, source_target_pairs={{0,32},{32,0},{64,96},{96,64},{128,160},{160,128},{192,224},{224,1... | collective-permute-start | bytes 1572872 | tf_op jit(solution)/shard_map/ppermute | solution.py:292
  86.5 5.0 %collective-permute-start.2 = (bf16[1040,512]{1,0:T(8,128)(2,1)S(1)}, bf16[1040,512]{1,0:T(8,128)(2,1)S(1)}, u32[]{:S(2)}, u32[]{:S(2)}) collective-permute-start(bf16[1040,512]{1,0:T(8,128)(2,1)S(1)} %get-tuple-element.8.mine), channel_id=1, source_target_pairs={{0,32},{32,0},{64,96},{96,64},{128,160},{160,128},{192,224},{224,1... | collective-permute-start | bytes 3194888 | tf_op jit(solution)/shard_map/ppermute | solution.py:292

commit v8 on v7

--- a/solution.py
+++ b/solution.py
@@ -15,6 +15,7 @@
 PART = 2 * CHUNK + STAT
 ROWS = 4 * CHUNK + TILE
 TAIL = 16
+PIECES = 4
 LIMIT = 40 * 1024 * 1024
 
 BF = jnp.bfloat16
@@ -64,19 +65,6 @@
 
 def grid_of(n):
     return lax.broadcasted_iota(jnp.int32, (n, n), 0), lax.broadcasted_iota(jnp.int32, (n, n), 1)
-
-
-def take(other):
-    def kernel(grad, out, sems):
-        core, _, _ = place()
-        rows = half_at(1 - core if other else core)
-        copies = [pltpu.make_async_copy(grad.at[b, rows, :], out.at[b], sems.at[b]) for b in range(2)]
-        for copy in copies:
-            copy.start()
-        for copy in copies:
-            copy.wait()
-
-    return kernel
 
 
 def pack_kernel(stat, out):
@@ -94,12 +82,13 @@
         out[y, CHUNK:STAT, HALF:BS] = diagonal
 
 
-def first_kernel(keep, got, packed, owner, out):
+def first_kernel(grad, got, packed, owner, out):
     del owner
+    core, _, _ = place()
     for y in range(4):
-        rows = slice(y * CHUNK, (y + 1) * CHUNK)
-        for b in BLOCKS:
-            total = (keep[b, rows, :].astype(F32) + got[b, rows, :].astype(F32)).astype(BF)
+        rows = pl.ds(pl.multiple_of(core * HALF + y * CHUNK, CHUNK), CHUNK)
+        for b in BLOCKS:
+            total = (grad[b, rows, :].astype(F32) + got[b, rows, :].astype(F32)).astype(BF)
             out[y, b * CHUNK : (b + 1) * CHUNK, :] = total
         out[y, 2 * CHUNK : PART, :] = packed[y]
 
@@ -270,8 +259,10 @@
             low = left[rows, :]
             precond = scale * (1.953125 * low.astype(F32) + mm(low, right[rows, :]))
             ratio = jnp.sqrt(sums[b, 0:1, 0:1] / (squares(precond) + 1e-06))
-            done[b] = (precond * ratio).astype(BF)
-            pltpu.make_async_copy(done.at[b], out.at[b], sems.at[b]).start()
+            for piece in range(PIECES):
+                some = slice(piece * BS // PIECES, (piece + 1) * BS // PIECES)
+                done[b, some, :] = (precond[some] * ratio).astype(BF)
+                pltpu.make_async_copy(done.at[b, some, :], out.at[b, some, :], sems.at[b, piece]).start()
 
     @pl.when(core == 0)
     def _():
@@ -282,7 +273,9 @@
         products(other, mine)
 
     for b in BLOCKS:
-        pltpu.make_async_copy(done.at[b], out.at[b], sems.at[b]).wait()
+        for piece in range(PIECES):
+            some = slice(piece * BS // PIECES, (piece + 1) * BS // PIECES)
+            pltpu.make_async_copy(done.at[b, some, :], out.at[b, some, :], sems.at[b, piece]).wait()
 
 
 def body(grad, stats, owner):
@@ -299,11 +292,9 @@
 
     block = grad[0]
     stat = stats[0, 0]
-    pieces = [call(take(other), array(2, HALF, BS), [HBM], [pltpu.SemaphoreType.DMA((2,))]) for other in (True, False)]
-    got = send(pieces[0](block), 1)
-    keep = pieces[1](block)
+    got = send(block, 1)
     packed = call(pack_kernel, array(4, STAT, BS), [VM], nbytes=3 << 19)(stat)
-    parts = exchange(call(first_kernel, array(4, PART, BS), [VM, VM, VM, VM])(keep, got, packed, owner))
+    parts = exchange(call(first_kernel, array(4, PART, BS), [VM, VM, VM, VM])(block, got, packed, owner))
     partial = call(second_kernel, array(ROWS, BS), [VM, VM])(owner, parts)
     parts = exchange(call(third_kernel, array(4, ROWS, BS), [VM, VM])(owner, gather(partial, 8)))
     far = send(parts[:, : 2 * CHUNK], 1)
@@ -325,7 +316,7 @@
         product_kernel,
         array(2, BS, BS),
         [VM, VM, VM],
-        [pair, pltpu.SemaphoreType.DMA((2,))],
+        [pair, pltpu.SemaphoreType.DMA((2, PIECES))],
         flops=4 * BS**3,
         out_spec=HBM,
     )(payload, received, sums)

time: 94.2 us -> 94.5 us (level)
  the two profiles are of different devices: /device:TPU:33 before, /device:TPU:39 now
where the time goes in v8:
time: 94.5 us; the launch traced here: 94.2 us
  blocking collectives  68.9 us (73%)
  starting transfers between devices  9.85 us (10%)
  Pallas kernels  9.82 us (10%)
  local copies, waits for them, and re-layouts  2.77 us (3%)
  waiting for transfers between devices  2.14 us (2%)
    all_gather x1, blocking collectives, gather(): lax.all_gather(value, 'group', axis_index_groups=[[g, g ^ bits] for g in...  36.7 us
    all_to_all x2, blocking collectives, exchange(): lax.all_to_all(value, 'group', 0, 0, tiled=True, axis_index_groups=along_y)  32.2 us
    ppermute x3, starting transfers between devices, send(): return lax.ppermute(value, 'group', [(g, g ^ bits) for g in range(16)])  9.85 us
    pallas_call x1, Pallas kernels, body(): call(root_kernel, (array(2 * BS + TAIL, BS), array(2, BS, BS)), [VM, VM,...  4.9 us
    unnamed x7, local copies, waits for them, and re-layouts  2.73 us
    pallas_call x1, Pallas kernels, body(): call(product_kernel, array(2, BS, BS), [VM, VM, VM], [pair, pltpu.Semapho...  2.35 us
    ppermute x3, waiting for transfers between devices, send(): return lax.ppermute(value, 'group', [(g, g ^ bits) for g in range(16)])  2.14 us
  transfers between devices with their start and end apart: 3, of which 3 were waited for; matrix products, arithmetic and copies ran while one was open for 1% of the time, Pallas kernels for 2%

profile of v8, /device:TPU:39, one launch (start us, length us, event | category | flops | bytes accessed | tf_op | source)
XLA Modules:
  0.0 94.2 jit_solution(2833315287067016913)
XLA Ops:
  0.6 2.6 %collective-permute-start = (bf16[2,512,512]{2,1,0:T(8,128)(2,1)}, bf16[2,512,512]{2,1,0:T(8,128)(2,1)S(1)}, u32[]{:S(2)}, u32[]{:S(2)}) collective-permute-start(bf16[2,512,512]{2,1,0:T(8,128)(2,1)} %bitcast.7), channel_id=1, source_target_pairs={{0,32},{32,0},{64,96},{96,64},{128,160},{160,128},{192,224},{224,1... | collective-permute-start | bytes 3145736 | tf_op jit(solution)/shard_map/ppermute | solution.py:285
  3.2 0.8 copy.8.owner
  4.0 0.0 copy-start
  4.0 1.2 %copy-done = f32[1,1,512,512]{3,2,1,0:T(8,128)S(1)} copy-done((f32[1,1,512,512]{3,2,1,0:T(8,128)S(1)}, f32[1,1,512,512]{3,2,1,0:T(8,128)}, u32[]{:S(2)}) %copy-start) | copy-done | bytes 1048600
  5.2 0.0 copy-start.2
  5.2 0.1 shard_map.50.packed
  5.3 0.4 collective-permute-done.got
  5.7 0.7 copy-done.2
  6.4 0.1 shard_map.51
  6.6 16.2 %all_to_all.10.got = bf16[4,200,512]{2,1,0:T(8,128)(2,1)S(1)} all-to-all(bf16[4,200,512]{2,1,0:T(8,128)(2,1)S(1)} %shard_map.51), channel_id=1, replica_groups={{0,64,128,192},{32,96,160,224},{256,320,384,448},{288,352,416,480},{1,6..., dimensions={0} | all-to-all | bytes 1638400 | tf_op jit(solution)/shard_map/all_to_all | solution.py:291
  22.7 0.2 shard_map.52
  22.9 36.7 %all-gather = bf16[528,512]{1,0:T(8,128)(2,1)S(1)} all-gather(bf16[264,512]{1,0:T(8,128)(2,1)S(1)} %shard_map.52), channel_id=2, replica_groups={{0,256},{32,288},{64,320},{96,352},{128,384},{160,416},{192,448},{224,4..., dimensions={0}, use_global_device_ids=true | all-gather | bytes 811008 | tf_op jit(solution)/shard_map/all_gather | solution.py:288
  59.6 0.2 shard_map.53
  59.8 16.0 %all_to_all.11.got = bf16[4,264,512]{2,1,0:T(8,128)(2,1)S(1)} all-to-all(bf16[4,264,512]{2,1,0:T(8,128)(2,1)S(1)} %shard_map.53), channel_id=1, replica_groups={{0,64,128,192},{32,96,160,224},{256,320,384,448},{288,352,416,480},{1,6..., dimensions={0} | all-to-all | bytes 2162688 | tf_op jit(solution)/shard_map/all_to_all | solution.py:291
  75.8 4.7 %collective-permute-start.1 = (bf16[4,128,512]{2,1,0:T(8,128)(2,1)S(1)}, bf16[4,128,512]{2,1,0:T(8,128)(2,1)S(1)}, u32[]{:S(2)}, u32[]{:S(2)}) collective-permute-start(bf16[4,128,512]{2,1,0:T(8,128)(2,1)S(1)} %slice.4), channel_id=1, source_target_pairs={{0,32},{32,0},{64,96},{96,64},{128,160},{160,128},{192,224},{224,1... | collective-permute-start | bytes 1572872 | tf_op jit(solution)/shard_map/ppermute | solution.py:285
  80.5 0.2 shard_map.54.stat
  80.8 0.0 copy-start.1
  80.8 1.3 %collective-permute-done.1.far = bf16[4,128,512]{2,1,0:T(8,128)(2,1)S(1)} collective-permute-done((bf16[4,128,512]{2,1,0:T(8,128)(2,1)S(1)}, bf16[4,128,512]{2,1,0:T(8,128)(2,1)S(1)}, u32[]{:S(2)}, u32[]{:S(2)}) %collective-permute-start.1) | collective-permute-done | bytes 524320 | tf_op jit(solution)/shard_map/ppermute | solution.py:285
  82.0 4.9 %shard_map.55 = (bf16[1040,512]{1,0:T(8,128)(2,1)S(1)}, bf16[2,512,512]{2,1,0:T(8,128)(2,1)S(1)}) custom-call(bf16[4,264,512]{2,1,0:T(8,128)(2,1)S(1)} %all_to_all.11.got, bf16[4,128,512]{2,1,0:T(8,128)(2,1)S(1)} %collective-permute-done.1.far, f32[2,3,256,256]{3,2,1,0:T(8,128)S(1)} %shard_map.54.stat), custom_call_target="tpu_custom_call" | custom-call | flops 5368709120 | tf_op jit(solution)/shard_map/pallas_call | solution.py:303
  86.9 2.6 %collective-permute-start.2 = (bf16[1040,512]{1,0:T(8,128)(2,1)S(1)}, bf16[1040,512]{1,0:T(8,128)(2,1)S(1)}, u32[]{:S(2)}, u32[]{:S(2)}) collective-permute-start(bf16[1040,512]{1,0:T(8,128)(2,1)S(1)} %get-tuple-element.8.mine), channel_id=1, source_target_pairs={{0,32},{32,0},{64,96},{96,64},{128,160},{160,128},{192,224},{224,1... | collective-permute-start | bytes 3194888 | tf_op jit(solution)/shard_map/ppermute | solution.py:285
  89.5 0.0 copy-done.1
  89.5 1.8 %shard_map.56 = (f32[512,512]{1,0:T(8,128)}, f32[2,8,128]{2,1,0:T(8,128)S(1)}) custom-call(s32[32,2]{1,0:T(8,128)S(1)} %copy.8.owner, bf16[2,512,512]{2,1,0:T(8,128)(2,1)S(1)} %get-tuple-element.6.dense, f32[512,512]{1,0:T(8,128)S(1)} %bitcast.5), custom_call_target="tpu_custom_call" | custom-call | flops 268435456 | bytes 3145728 | tf_op jit(solution)/shard_map/pallas_call | solution.py:307
  91.4 0.4 collective-permute-done.2.other
  91.8 2.4 %shard_map.57 = bf16[2,512,512]{2,1,0:T(8,128)(2,1)} custom-call(bf16[1040,512]{1,0:T(8,128)(2,1)S(1)} %get-tuple-element.8.mine, bf16[1040,512]{1,0:T(8,128)(2,1)S(1)} %collective-permute-done.2.other, f32[2,8,128]{2,1,0:T(8,128)S(1)} %get-tuple-element.9.sums), custom_call_target="tpu_custom_call" | custom-call | flops 536870912 | tf_op jit(solution)/shard_map/pallas_call | solution.py:315
  (1 shorter events, 0.0 us)
Async XLA Ops:
  0.6 5.1 %collective-permute-start = (bf16[2,512,512]{2,1,0:T(8,128)(2,1)}, bf16[2,512,512]{2,1,0:T(8,128)(2,1)S(1)}, u32[]{:S(2)}, u32[]{:S(2)}) collective-permute-start(bf16[2,512,512]{2,1,0:T(8,128)(2,1)} %bitcast.7), channel_id=1, source_target_pairs={{0,32},{32,0},{64,96},{96,64},{128,160},{160,128},{192,224},{224,1... | collective-permute-start | bytes 3145736 | tf_op jit(solution)/shard_map/ppermute | solution.py:285
  4.0 1.2 %copy-start = (f32[1,1,512,512]{3,2,1,0:T(8,128)S(1)}, f32[1,1,512,512]{3,2,1,0:T(8,128)}, u32[]{:S(2)}) copy-start(f32[1,1,512,512]{3,2,1,0:T(8,128)} %param.4) | copy-start | bytes 3145732
  5.2 1.2 %copy-start.2 = (bf16[1,2,512,512]{3,2,1,0:T(8,128)(2,1)S(1)}, bf16[1,2,512,512]{3,2,1,0:T(8,128)(2,1)}, u32[]{:S(2)}) copy-start(bf16[1,2,512,512]{3,2,1,0:T(8,128)(2,1)} %param.3) | copy-start | bytes 3145732
  75.8 6.2 %collective-permute-start.1 = (bf16[4,128,512]{2,1,0:T(8,128)(2,1)S(1)}, bf16[4,128,512]{2,1,0:T(8,128)(2,1)S(1)}, u32[]{:S(2)}, u32[]{:S(2)}) collective-permute-start(bf16[4,128,512]{2,1,0:T(8,128)(2,1)S(1)} %slice.4), channel_id=1, source_target_pairs={{0,32},{32,0},{64,96},{96,64},{128,160},{160,128},{192,224},{224,1... | collective-permute-start | bytes 1572872 | tf_op jit(solution)/shard_map/ppermute | solution.py:285
  80.8 8.8 %copy-start.1 = (f32[1,1,512,512]{3,2,1,0:T(8,128)S(1)}, f32[1,1,512,512]{3,2,1,0:T(8,128)}, u32[]{:S(2)}) copy-start(f32[1,1,512,512]{3,2,1,0:T(8,128)} %param.4) | copy-start | bytes 3145732
  86.9 4.9 %collective-permute-start.2 = (bf16[1040,512]{1,0:T(8,128)(2,1)S(1)}, bf16[1040,512]{1,0:T(8,128)(2,1)S(1)}, u32[]{:S(2)}, u32[]{:S(2)}) collective-permute-start(bf16[1040,512]{1,0:T(8,128)(2,1)S(1)} %get-tuple-element.8.mine), channel_id=1, source_target_pairs={{0,32},{32,0},{64,96},{96,64},{128,160},{160,128},{192,224},{224,1... | collective-permute-start | bytes 3194888 | tf_op jit(solution)/shard_map/ppermute | solution.py:285

commit v9 on v8

v9 whole, which is shorter than its diff:
```python
import jax
import jax.numpy as jnp
from jax import lax
from jax.experimental import pallas as pl
from jax.experimental.pallas import tpu as pltpu
from jax.sharding import PartitionSpec as P

BETA = 0.9
DAMPING = 0.0001
BS = 512
HALF = 256
CHUNK = 128
FOLD = 64
TILE = 8
STAT = FOLD + TILE
PART = CHUNK + STAT
ROWS = CHUNK + 2 * FOLD + TILE
TAIL = 16
LIMIT = 40 * 1024 * 1024

BF = jnp.bfloat16
F32 = jnp.float32

VM = pl.BlockSpec(memory_space=pltpu.VMEM)
HBM = pl.BlockSpec(memory_space=pl.ANY)
BLOCKS = range(2)


def call(kernel, shapes, specs, scratch=(), flops=0, nbytes=0, out_spec=VM, **more):
    many = isinstance(shapes, tuple)
    return pl.pallas_call(
        kernel,
        out_shape=shapes,
        in_specs=specs,
        out_specs=(out_spec,) * len(shapes) if many and not isinstance(out_spec, tuple) else out_spec,
        scratch_shapes=list(scratch),
        compiler_params=pltpu.CompilerParams(vmem_limit_bytes=LIMIT),
        cost_estimate=pl.CostEstimate(flops=flops, bytes_accessed=nbytes, transcendentals=0),
        **more,
    )


def array(*shape, dtype=BF):
    return jax.ShapeDtypeStruct(shape, dtype)


def place():
    group = lax.axis_index("group")
    return lax.rem(group, 2), lax.rem(lax.div(group, 2), 4), lax.div(group, 8)


def owner_of(owner, block):
    row = lax.broadcasted_iota(jnp.int32, owner.shape, 0) == lax.axis_index("dp")
    col = lax.broadcasted_iota(jnp.int32, owner.shape, 1) == block
    return jnp.sum(jnp.where(row & col, owner[...], 0))


def mm(a, b):
    return jnp.dot(a.astype(BF), b.astype(BF), preferred_element_type=F32)


def grid_of(n):
    return lax.broadcasted_iota(jnp.int32, (n, n), 0), lax.broadcasted_iota(jnp.int32, (n, n), 1)


def pack_kernel(stat, out):
    row, col = grid_of(HALF)
    corner = stat[HALF:BS, HALF:BS]
    fold = jnp.where(row <= col, stat[0:HALF, 0:HALF], corner).astype(BF)
    diagonal = jnp.sum(jnp.where(row == col, corner, 0.0), axis=0, keepdims=True)
    diagonal = jnp.broadcast_to(diagonal, (TILE, HALF)).astype(BF)
    side = stat[0:HALF, HALF:BS].astype(BF)
    for y in range(4):
        lo = y * FOLD
        out[y, 0:FOLD, 0:HALF] = fold[lo : lo + FOLD]
        out[y, 0:FOLD, HALF:BS] = side[lo : lo + FOLD]
        out[y, FOLD:STAT, 0:HALF] = diagonal
        out[y, FOLD:STAT, HALF:BS] = diagonal


def first_kernel(grad, got, packed, owner, out):
    del owner
    core, _, _ = place()
    for y in range(4):
        rows = slice(y * CHUNK, (y + 1) * CHUNK)
        out[y, 0:CHUNK, :] = (grad[core, rows, :].astype(F32) + got[core, rows, :].astype(F32)).astype(BF)
        out[y, CHUNK:PART, :] = packed[y]


def join(first, second):
    row = lax.broadcasted_iota(jnp.int32, (TILE, BS), 0)
    return jnp.where(row < TILE // 2, first.astype(F32), second.astype(F32)).astype(BF)


def second_kernel(owner, got, out):
    total = got[0, 0:CHUNK, :].astype(F32)
    for source in range(1, 4):
        total += got[source, 0:CHUNK, :].astype(F32)
    out[0:CHUNK, :] = total.astype(BF)
    source = [lax.rem(owner_of(owner, b), 4) for b in BLOCKS]
    for b in BLOCKS:
        out[CHUNK + b * FOLD : CHUNK + (b + 1) * FOLD, :] = got[source[b], CHUNK : CHUNK + FOLD, :]
    out[CHUNK + 2 * FOLD : ROWS, :] = join(*(got[source[b], CHUNK + FOLD : PART, :] for b in BLOCKS))


def third_kernel(owner, got, out):
    total = (got[0, 0:CHUNK, :].astype(F32) + got[1, 0:CHUNK, :].astype(F32)).astype(BF)
    half = [lax.div(owner_of(owner, b), 4) for b in BLOCKS]
    stats = [got[half[b], CHUNK + b * FOLD : CHUNK + (b + 1) * FOLD, :] for b in BLOCKS]
    diagonals = join(*(got[half[b], CHUNK + 2 * FOLD : ROWS, :] for b in BLOCKS))
    for y in range(4):
        out[y, 0:CHUNK, :] = total
        for b in BLOCKS:
            out[y, CHUNK + b * FOLD : CHUNK + (b + 1) * FOLD, :] = stats[b]
        out[y, CHUNK + 2 * FOLD : ROWS, :] = diagonals


def folded(got, block, y):
    return got[y, pl.ds(pl.multiple_of(CHUNK + block * FOLD, FOLD), FOLD), :]


def diagonal_of(got, block):
    tile = got[0, CHUNK + 2 * FOLD : ROWS, :].astype(F32)
    return jnp.where(block == 0, tile[0:1, :], tile[TILE // 2 : TILE // 2 + 1, :])


def swap_kernel(got, out):
    core, _, _ = place()
    for y in range(4):
        out[y * CHUNK : (y + 1) * CHUNK, :] = got[y, 0:CHUNK, :]
        out[BS + y * FOLD : BS + (y + 1) * FOLD, :] = folded(got, 1 - core, y)
    out[BS + 4 * FOLD : BS + 4 * FOLD + TAIL, :] = jnp.broadcast_to(diagonal_of(got, 1 - core), (TAIL, BS)).astype(BF)


def unpacked(packed, diagonal):
    row, col = grid_of(HALF)
    packed = BETA * packed.astype(F32)
    fold = packed[:, 0:HALF]
    turned = fold.T
    first = jnp.where(row <= col, fold, turned)
    last = jnp.where(row > col, fold, jnp.where(row < col, turned, BETA * diagonal[:, 0:HALF]))
    return first, packed[:, HALF:BS], last


def whole(corners):
    first, side, last = (corner.astype(BF) for corner in corners)
    top = jnp.concatenate([first, side], axis=1)
    return jnp.concatenate([top, jnp.concatenate([side.T, last], axis=1)], axis=0)


def corners_of(left, right, contract):
    numbers = (((1,), (contract,)), ((), ()))
    top = lax.dot_general(left[0:HALF], right, numbers, preferred_element_type=F32)
    tail = right[:, HALF:BS] if contract == 0 else right[HALF:BS]
    last = lax.dot_general(left[HALF:BS], tail, numbers, preferred_element_type=F32)
    return top[:, 0:HALF], top[:, HALF:BS], last


def mix(*terms):
    mixed = []
    for corner in range(3):
        total = None
        for factor, corners in terms:
            value = corners[corner] if factor == 1 else factor * corners[corner]
            total = value if total is None else total + value
        mixed.append(total)
    return tuple(mixed)


def newton(currents):
    lows = [whole(m) for m in currents]
    parts = [mix((1, corners_of(low, low, 0)), (-2.5, m)) for low, m in zip(lows, currents)]
    slows = [whole(part) for part in parts]
    fourths = [whole(mix((1, corners_of(slow, slow, 0)), (3.125, part))) for slow, part in zip(slows, parts)]
    later = [mix((1, corners_of(four, low, 0)), (2.44140625, m)) for four, low, m in zip(fourths, lows, currents)]
    return later, lows


def squares(matrix):
    return jnp.sum(matrix * matrix, keepdims=True)


def early_kernel(got, shifted, dense, sums):
    core, _, _ = place()
    for y in range(4):
        dense[y * CHUNK : (y + 1) * CHUNK, :] = got[y, 0:CHUNK, :]
    total = dense[...]
    sums[...] = jnp.broadcast_to(squares(total.astype(F32)), (8, 128))
    row, col = grid_of(HALF)
    damping = jnp.where(row == col, DAMPING, 0.0)
    for k, side in enumerate((total, total.T)):
        gram = corners_of(side, side, 1)
        shifted[k, 0] = (1.0 - BETA) * gram[0] + damping
        shifted[k, 1] = (1.0 - BETA) * gram[1]
        shifted[k, 2] = (1.0 - BETA) * gram[2] + damping
    packed = jnp.concatenate([folded(got, core, y) for y in range(4)], axis=0)
    for corner, value in enumerate(unpacked(packed, diagonal_of(got, core))):
        shifted[core, corner] += value


def root_kernel(early, far, dense, sums, out, shifted):
    core, _, _ = place()
    shifted[...] = early[...]
    diagonal = far[BS + 4 * FOLD : BS + 4 * FOLD + TAIL, :].astype(F32)[0:1, :]
    for corner, value in enumerate(unpacked(far[BS : BS + 4 * FOLD, :], diagonal)):
        shifted[1 - core, corner] += value
    sides = [tuple(shifted[k, corner] for corner in range(3)) for k in range(2)]
    frobs = [jnp.sqrt(squares(m[0]) + 2.0 * squares(m[1]) + squares(m[2])) for m in sides]
    b0 = [tuple(corner * (0.25 / frob) for corner in m) for m, frob in zip(sides, frobs)]
    b1, low0 = newton(b0)
    b2, low1 = newton(b1)
    n01 = [mix((1, corners_of(p, q, 0)), (-1.25, u), (-1.25, v)) for p, q, u, v in zip(low0, low1, b0, b1)]
    ends = [corners_of(whole(n), whole(m), 0) for n, m in zip(n01, b2)]
    left, right = [whole(mix((1.25, n), (-1.5625, m), (-1.0, end))) for n, m, end in zip(n01, b2, ends)]
    scale = lax.rsqrt(jnp.sqrt(frobs[0])) * lax.rsqrt(jnp.sqrt(frobs[1]))
    block = dense[...]
    part = 1.953125 * block.astype(F32) + mm(left, block)
    precond = 1.953125 * part + mm(part, right)
    ratio = scale * jnp.sqrt(sums[0:1, 0:1] / (scale * scale * squares(precond) + 1e-06))
    out[...] = (precond * ratio).astype(BF)


def stat_kernel(owner, dense, far, stat, mine, out, update, oriented, sem):
    core, y, half = place()
    copy = pltpu.make_async_copy(mine, update.at[core], sem)
    copy.start()
    pair = half * 4 + y
    own = owner_of(owner, core) == pair
    other = owner_of(owner, 1 - core) == pair

    @pl.when(own)
    def _():
        oriented[...] = dense[...]

    @pl.when(other)
    def _():
        oriented[...] = far[0:BS, :]

    @pl.when(core == 1)
    def _():
        oriented[...] = oriented[...].T

    active = jnp.logical_or(own, other)

    @pl.when(active)
    def _():
        side = oriented[...]
        gram = lax.dot_general(side, side, (((1,), (1,)), ((), ())), preferred_element_type=F32)
        out[...] = BETA * stat[...] + (1.0 - BETA) * gram

    @pl.when(jnp.logical_not(active))
    def _():
        out[...] = stat[...]

    copy.wait()


def last_kernel(other, begun, out, sem):
    del begun
    core, _, _ = place()
    copy = pltpu.make_async_copy(other, out.at[1 - core], sem)
    copy.start()
    copy.wait()


def body(grad, stats, owner):
    along_y = [[h * 8 + 2 * k + c for k in range(4)] for h in range(2) for c in range(2)]

    def send(value, bits):
        return lax.ppermute(value, "group", [(g, g ^ bits) for g in range(16)])

    def gather(value, bits):
        return lax.all_gather(value, "group", axis_index_groups=[[g, g ^ bits] for g in range(16) if g < g ^ bits])

    def exchange(value):
        return lax.all_to_all(value, "group", 0, 0, tiled=True, axis_index_groups=along_y)

    block = grad[0]
    stat = stats[0, 0]
    got = send(block, 1)
    packed = call(pack_kernel, array(4, STAT, BS), [VM], nbytes=3 << 19)(stat)
    parts = exchange(call(first_kernel, array(4, PART, BS), [VM, VM, VM, VM])(block, got, packed, owner))
    partial = call(second_kernel, array(ROWS, BS), [VM, VM])(owner, parts)
    parts = exchange(call(third_kernel, array(4, ROWS, BS), [VM, VM])(owner, gather(partial, 8)))
    far = send(call(swap_kernel, array(BS + 4 * FOLD + TAIL, BS), [VM])(parts), 1)
    corners = array(2, 3, HALF, HALF, dtype=F32)
    early, dense, sums = call(early_kernel, (corners, array(BS, BS), array(8, 128, dtype=F32)), [VM], flops=4 * BS**3)(parts)
    mine = call(
        root_kernel, array(BS, BS), [VM, VM, VM, VM], [pltpu.VMEM((2, 3, HALF, HALF), F32)], flops=20 * 2 * BS**3
    )(early, far, dense, sums)
    other = send(mine, 1)
    new_stat, begun = call(
        stat_kernel,
        (array(BS, BS, dtype=F32), array(2, BS, BS)),
        [VM, VM, VM, VM, VM],
        [pltpu.VMEM((BS, BS), BF), pltpu.SemaphoreType.DMA],
        flops=2 * BS**3,
        nbytes=3 << 20,
        out_spec=(VM, HBM),
    )(owner, dense, far, stat, mine)
    update = call(
        last_kernel,
        array(2, BS, BS),
        [VM, HBM],
        [pltpu.SemaphoreType.DMA],
        out_spec=HBM,
        input_output_aliases={1: 0},
    )(other, begun)
    return (new_stat[None, None], update)


def solution(mesh):
    in_specs = (P("group", "dp", None, None), P("group", "dp", None, None), P())
    out_specs = (P("group", "dp", None, None), P("dp", None, None))
    return jax.shard_map(body, mesh=mesh, in_specs=in_specs, out_specs=out_specs, check_vma=False)
```

time: 94.5 us -> 93 us (0.984)
    pallas_call x4 -> x5, Pallas kernels: 9.31 us -> 8.82 us  [the longest x1 5.26 us: body(): call(root_kernel, array(BS, BS), [VM, VM, VM, VM], [pltpu.VMEM((2, 3, HAL...]
  transfers between devices with their start and end apart: 3 -> 3, of which waited for: 3 -> 2; matrix products, arithmetic and copies ran while one was open for 1% -> 1% of each run, Pallas kernels for 2% -> 3%
where the time goes in v9:
time: 93 us; the launch traced here: 92.7 us
  blocking collectives  68.9 us (74%)
  starting transfers between devices  9.54 us (10%)
  Pallas kernels  9.32 us (10%)
  local copies, waits for them, and re-layouts  2.73 us (3%)
  waiting for transfers between devices  1.49 us (2%)
    all_gather x1, blocking collectives, gather(): lax.all_gather(value, 'group', axis_index_groups=[[g, g ^ bits] for g in...  36.7 us
    all_to_all x2, blocking collectives, exchange(): lax.all_to_all(value, 'group', 0, 0, tiled=True, axis_index_groups=along_y)  32.2 us
    ppermute x3, starting transfers between devices, send(): return lax.ppermute(value, 'group', [(g, g ^ bits) for g in range(16)])  9.54 us
    pallas_call x1, Pallas kernels, body(): call(root_kernel, array(BS, BS), [VM, VM, VM, VM], [pltpu.VMEM((2, 3, HAL...  5.26 us
    unnamed x7, local copies, waits for them, and re-layouts  2.73 us
  transfers between devices with their start and end apart: 3, of which 2 were waited for; matrix products, arithmetic and copies ran while one was open for 1% of the time, Pallas kernels for 3%

profile of v9, /device:TPU:39, one launch (start us, length us, event | category | flops | bytes accessed | tf_op | source)
XLA Modules:
  0.0 92.7 jit_solution(12175379280136279849)
XLA Ops:
  0.6 2.6 %collective-permute-start = (bf16[2,512,512]{2,1,0:T(8,128)(2,1)}, bf16[2,512,512]{2,1,0:T(8,128)(2,1)S(1)}, u32[]{:S(2)}, u32[]{:S(2)}) collective-permute-start(bf16[2,512,512]{2,1,0:T(8,128)(2,1)} %bitcast.7), channel_id=1, source_target_pairs={{0,32},{32,0},{64,96},{96,64},{128,160},{160,128},{192,224},{224,1... | collective-permute-start | bytes 3145736 | tf_op jit(solution)/shard_map/ppermute | solution.py:270
  3.2 0.8 copy.9.owner
  4.0 0.0 copy-start
  4.0 1.2 %copy-done = f32[1,1,512,512]{3,2,1,0:T(8,128)S(1)} copy-done((f32[1,1,512,512]{3,2,1,0:T(8,128)S(1)}, f32[1,1,512,512]{3,2,1,0:T(8,128)}, u32[]{:S(2)}) %copy-start) | copy-done | bytes 1048600
  5.2 0.0 copy-start.2
  5.2 0.1 shard_map.50.packed
  5.3 0.4 collective-permute-done.got
  5.7 0.7 copy-done.2
  6.4 0.1 shard_map.51
  6.6 16.2 %all_to_all.10.got = bf16[4,200,512]{2,1,0:T(8,128)(2,1)S(1)} all-to-all(bf16[4,200,512]{2,1,0:T(8,128)(2,1)S(1)} %shard_map.51), channel_id=1, replica_groups={{0,64,128,192},{32,96,160,224},{256,320,384,448},{288,352,416,480},{1,6..., dimensions={0} | all-to-all | bytes 1638400 | tf_op jit(solution)/shard_map/all_to_all | solution.py:276
  22.7 0.2 shard_map.52
  22.9 36.7 %all-gather = bf16[528,512]{1,0:T(8,128)(2,1)S(1)} all-gather(bf16[264,512]{1,0:T(8,128)(2,1)S(1)} %shard_map.52), channel_id=2, replica_groups={{0,256},{32,288},{64,320},{96,352},{128,384},{160,416},{192,448},{224,4..., dimensions={0}, use_global_device_ids=true | all-gather | bytes 811008 | tf_op jit(solution)/shard_map/all_gather | solution.py:273
  59.6 0.2 shard_map.53
  59.8 16.0 %all_to_all.11.got = bf16[4,264,512]{2,1,0:T(8,128)(2,1)S(1)} all-to-all(bf16[4,264,512]{2,1,0:T(8,128)(2,1)S(1)} %shard_map.53), channel_id=1, replica_groups={{0,64,128,192},{32,96,160,224},{256,320,384,448},{288,352,416,480},{1,6..., dimensions={0} | all-to-all | bytes 2162688 | tf_op jit(solution)/shard_map/all_to_all | solution.py:276
  75.8 0.1 shard_map.55
  75.9 4.7 %collective-permute-start.1 = (bf16[784,512]{1,0:T(8,128)(2,1)S(1)}, bf16[784,512]{1,0:T(8,128)(2,1)S(1)}, u32[]{:S(2)}, u32[]{:S(2)}) collective-permute-start(bf16[784,512]{1,0:T(8,128)(2,1)S(1)} %shard_map.55), channel_id=1, source_target_pairs={{0,32},{32,0},{64,96},{96,64},{128,160},{160,128},{192,224},{224,1... | collective-permute-start | bytes 2408456 | tf_op jit(solution)/shard_map/ppermute | solution.py:270
  80.5 0.9 shard_map.54
  81.4 1.1 %collective-permute-done.1.far = bf16[784,512]{1,0:T(8,128)(2,1)S(1)} collective-permute-done((bf16[784,512]{1,0:T(8,128)(2,1)S(1)}, bf16[784,512]{1,0:T(8,128)(2,1)S(1)}, u32[]{:S(2)}, u32[]{:S(2)}) %collective-permute-start.1) | collective-permute-done | bytes 802848 | tf_op jit(solution)/shard_map/ppermute | solution.py:270
  82.4 0.0 copy-start.1
  82.4 5.3 %shard_map.56.mine = bf16[512,512]{1,0:T(8,128)(2,1)S(1)} custom-call(f32[2,3,256,256]{3,2,1,0:T(8,128)S(1)} %get-tuple-element.8.early, bf16[784,512]{1,0:T(8,128)(2,1)S(1)} %collective-permute-done.1.far, bf16[512,512]{1,0:T(8,128)(2,1)S(1)} %get-tuple-element.7.dense, f32[8,128]{1,0:T(8,128)S(1)} %get-tuple-element.9.sums), custom_call_target="tpu_custom_call" | custom-call | flops 5368709120 | tf_op jit(solution)/shard_map/pallas_call | solution.py:288
  87.7 2.3 %collective-permute-start.2 = (bf16[512,512]{1,0:T(8,128)(2,1)S(1)}, bf16[512,512]{1,0:T(8,128)(2,1)S(1)}, u32[]{:S(2)}, u32[]{:S(2)}) collective-permute-start(bf16[512,512]{1,0:T(8,128)(2,1)S(1)} %shard_map.56.mine), channel_id=1, source_target_pairs={{0,32},{32,0},{64,96},{96,64},{128,160},{160,128},{192,224},{224,1... | collective-permute-start | bytes 1572872 | tf_op jit(solution)/shard_map/ppermute | solution.py:270
  90.0 0.0 copy-done.1
  90.0 1.8 %shard_map.57 = (f32[512,512]{1,0:T(8,128)}, bf16[2,512,512]{2,1,0:T(8,128)(2,1)}) custom-call(s32[32,2]{1,0:T(8,128)S(1)} %copy.9.owner, bf16[512,512]{1,0:T(8,128)(2,1)S(1)} %get-tuple-element.7.dense, bf16[784,512]{1,0:T(8,128)(2,1)S(1)} %collective-permute-done.1.far, f32[512,512]{1,0:T(8,128)S(1)} %bitcast.5, bf16[512,512]{1,0:T(8,128)(2,1)S(1)} %shard_map.56.mine), custom_call_target="tpu_custom_call" | custom-call | flops 268435456 | bytes 3145728 | tf_op jit(solution)/shard_map/pallas_call | solution.py:292
  91.8 0.0 collective-permute-done.2.other
  91.9 0.8 shard_map.58
Async XLA Ops:
  0.6 5.1 %collective-permute-start = (bf16[2,512,512]{2,1,0:T(8,128)(2,1)}, bf16[2,512,512]{2,1,0:T(8,128)(2,1)S(1)}, u32[]{:S(2)}, u32[]{:S(2)}) collective-permute-start(bf16[2,512,512]{2,1,0:T(8,128)(2,1)} %bitcast.7), channel_id=1, source_target_pairs={{0,32},{32,0},{64,96},{96,64},{128,160},{160,128},{192,224},{224,1... | collective-permute-start | bytes 3145736 | tf_op jit(solution)/shard_map/ppermute | solution.py:270
  4.0 1.2 %copy-start = (f32[1,1,512,512]{3,2,1,0:T(8,128)S(1)}, f32[1,1,512,512]{3,2,1,0:T(8,128)}, u32[]{:S(2)}) copy-start(f32[1,1,512,512]{3,2,1,0:T(8,128)} %param.4) | copy-start | bytes 3145732
  5.2 1.2 %copy-start.2 = (bf16[1,2,512,512]{3,2,1,0:T(8,128)(2,1)S(1)}, bf16[1,2,512,512]{3,2,1,0:T(8,128)(2,1)}, u32[]{:S(2)}) copy-start(bf16[1,2,512,512]{3,2,1,0:T(8,128)(2,1)} %param.3) | copy-start | bytes 3145732
  75.9 6.6 %collective-permute-start.1 = (bf16[784,512]{1,0:T(8,128)(2,1)S(1)}, bf16[784,512]{1,0:T(8,128)(2,1)S(1)}, u32[]{:S(2)}, u32[]{:S(2)}) collective-permute-start(bf16[784,512]{1,0:T(8,128)(2,1)S(1)} %shard_map.55), channel_id=1, source_target_pairs={{0,32},{32,0},{64,96},{96,64},{128,160},{160,128},{192,224},{224,1... | collective-permute-start | bytes 2408456 | tf_op jit(solution)/shard_map/ppermute | solution.py:270
  82.4 7.6 %copy-start.1 = (f32[1,1,512,512]{3,2,1,0:T(8,128)S(1)}, f32[1,1,512,512]{3,2,1,0:T(8,128)}, u32[]{:S(2)}) copy-start(f32[1,1,512,512]{3,2,1,0:T(8,128)} %param.4) | copy-start | bytes 3145732
  87.7 4.1 %collective-permute-start.2 = (bf16[512,512]{1,0:T(8,128)(2,1)S(1)}, bf16[512,512]{1,0:T(8,128)(2,1)S(1)}, u32[]{:S(2)}, u32[]{:S(2)}) collective-permute-start(bf16[512,512]{1,0:T(8,128)(2,1)S(1)} %shard_map.56.mine), channel_id=1, source_target_pairs={{0,32},{32,0},{64,96},{96,64},{128,160},{160,128},{192,224},{224,1... | collective-permute-start | bytes 1572872 | tf_op jit(solution)/shard_map/ppermute | solution.py:270

commit v10 on v9

--- a/solution.py
+++ b/solution.py
@@ -180,44 +180,58 @@
     return jnp.sum(matrix * matrix, keepdims=True)
 
 
-def early_kernel(got, shifted, dense, sums):
+def norm_of(corners):
+    return jnp.sqrt(squares(corners[0]) + 2.0 * squares(corners[1]) + squares(corners[2]))
+
+
+def early_kernel(got, gram, low, later, dense, sums, frob, sides):
     core, _, _ = place()
     for y in range(4):
         dense[y * CHUNK : (y + 1) * CHUNK, :] = got[y, 0:CHUNK, :]
     total = dense[...]
-    sums[...] = jnp.broadcast_to(squares(total.astype(F32)), (8, 128))
+    sides[0] = total
+    sides[1] = total.T
     row, col = grid_of(HALF)
     damping = jnp.where(row == col, DAMPING, 0.0)
-    for k, side in enumerate((total, total.T)):
-        gram = corners_of(side, side, 1)
-        shifted[k, 0] = (1.0 - BETA) * gram[0] + damping
-        shifted[k, 1] = (1.0 - BETA) * gram[1]
-        shifted[k, 2] = (1.0 - BETA) * gram[2] + damping
+
+    def damped(side):
+        first, cross, last = corners_of(side, side, 1)
+        return (1.0 - BETA) * first + damping, (1.0 - BETA) * cross, (1.0 - BETA) * last + damping
+
     packed = jnp.concatenate([folded(got, core, y) for y in range(4)], axis=0)
-    for corner, value in enumerate(unpacked(packed, diagonal_of(got, core))):
-        shifted[core, corner] += value
-
-
-def root_kernel(early, far, dense, sums, out, shifted):
-    core, _, _ = place()
-    shifted[...] = early[...]
+    shifted = mix((1, damped(sides[core])), (1, unpacked(packed, diagonal_of(got, core))))
+    norm = norm_of(shifted)
+    after, lows = newton([tuple(corner * (0.25 / norm) for corner in shifted)])
+    low[...] = lows[0]
+    other = damped(sides[1 - core])
+    for corner in range(3):
+        later[corner] = after[0][corner]
+        gram[corner] = other[corner]
+    frob[...] = jnp.broadcast_to(norm, (8, 128))
+    sums[...] = jnp.broadcast_to(squares(total.astype(F32)), (8, 128))
+
+
+def root_kernel(gram, low, later, dense, sums, frob, far, out, factors):
+    core, _, _ = place()
     diagonal = far[BS + 4 * FOLD : BS + 4 * FOLD + TAIL, :].astype(F32)[0:1, :]
-    for corner, value in enumerate(unpacked(far[BS : BS + 4 * FOLD, :], diagonal)):
-        shifted[1 - core, corner] += value
-    sides = [tuple(shifted[k, corner] for corner in range(3)) for k in range(2)]
-    frobs = [jnp.sqrt(squares(m[0]) + 2.0 * squares(m[1]) + squares(m[2])) for m in sides]
-    b0 = [tuple(corner * (0.25 / frob) for corner in m) for m, frob in zip(sides, frobs)]
-    b1, low0 = newton(b0)
-    b2, low1 = newton(b1)
-    n01 = [mix((1, corners_of(p, q, 0)), (-1.25, u), (-1.25, v)) for p, q, u, v in zip(low0, low1, b0, b1)]
-    ends = [corners_of(whole(n), whole(m), 0) for n, m in zip(n01, b2)]
-    left, right = [whole(mix((1.25, n), (-1.5625, m), (-1.0, end))) for n, m, end in zip(n01, b2, ends)]
-    scale = lax.rsqrt(jnp.sqrt(frobs[0])) * lax.rsqrt(jnp.sqrt(frobs[1]))
-    block = dense[...]
-    part = 1.953125 * block.astype(F32) + mm(left, block)
-    precond = 1.953125 * part + mm(part, right)
-    ratio = scale * jnp.sqrt(sums[0:1, 0:1] / (scale * scale * squares(precond) + 1e-06))
-    out[...] = (precond * ratio).astype(BF)
+    given = unpacked(far[BS : BS + 4 * FOLD, :], diagonal)
+    shifted = mix((1, tuple(gram[corner] for corner in range(3))), (1, given))
+    norm = norm_of(shifted)
+    other, lows = newton([tuple(corner * (0.25 / norm) for corner in shifted)])
+    factors[0, core] = low[...]
+    factors[0, 1 - core] = lows[0]
+    last, lows = newton([tuple(later[corner] for corner in range(3)), other[0]])
+    factors[1, core] = lows[0]
+    factors[1, 1 - core] = lows[1]
+    factors[2, core] = whole(last[0])
+    factors[2, 1 - core] = whole(last[1])
+    value = dense[...].astype(F32)
+    for step in range(3):
+        value = 1.25 * value - mm(factors[step, 0], value)
+        value = 1.25 * value - mm(value, factors[step, 1])
+    scale = lax.rsqrt(jnp.sqrt(norm)) * lax.rsqrt(jnp.sqrt(frob[0:1, 0:1]))
+    ratio = scale * jnp.sqrt(sums[0:1, 0:1] / (scale * scale * squares(value) + 1e-06))
+    out[...] = (value * ratio).astype(BF)
 
 
 def stat_kernel(owner, dense, far, stat, mine, out, update, oriented, sem):
@@ -283,11 +297,14 @@
     partial = call(second_kernel, array(ROWS, BS), [VM, VM])(owner, parts)
     parts = exchange(call(third_kernel, array(4, ROWS, BS), [VM, VM])(owner, gather(partial, 8)))
     far = send(call(swap_kernel, array(BS + 4 * FOLD + TAIL, BS), [VM])(parts), 1)
-    corners = array(2, 3, HALF, HALF, dtype=F32)
-    early, dense, sums = call(early_kernel, (corners, array(BS, BS), array(8, 128, dtype=F32)), [VM], flops=4 * BS**3)(parts)
-    mine = call(
-        root_kernel, array(BS, BS), [VM, VM, VM, VM], [pltpu.VMEM((2, 3, HALF, HALF), F32)], flops=20 * 2 * BS**3
-    )(early, far, dense, sums)
+    corners = array(3, HALF, HALF, dtype=F32)
+    square = array(BS, BS)
+    scalar = array(8, 128, dtype=F32)
+    pair = pltpu.VMEM((2, BS, BS), BF)
+    early = call(early_kernel, (corners, square, corners, square, scalar, scalar), [VM], [pair], flops=8 * BS**3)(parts)
+    dense = early[3]
+    factors = pltpu.VMEM((3, 2, BS, BS), BF)
+    mine = call(root_kernel, square, [VM] * 7, [factors], flops=20 * BS**3)(*early, far)
     other = send(mine, 1)
     new_stat, begun = call(
         stat_kernel,

time: 93 us -> 92.7 us (level)
  waiting for transfers between devices: 1.49 us -> 0.44 us
    ppermute x3, waiting for transfers between devices: 1.49 us -> 0.44 us  [send(): return lax.ppermute(value, 'group', [(g, g ^ bits) for g in range(16)])]
  transfers between devices with their start and end apart: 3 -> 3, of which waited for: 2 -> 1; matrix products, arithmetic and copies ran while one was open for 1% -> 1% of each run, Pallas kernels for 3% -> 4%
where the time goes in v10:
time: 92.7 us; the launch traced here: 92.3 us
  blocking collectives  68.9 us (74%)
  Pallas kernels  10.1 us (11%)
  starting transfers between devices  9.41 us (10%)
  local copies, waits for them, and re-layouts  2.73 us (3%)
    all_gather x1, blocking collectives, gather(): lax.all_gather(value, 'group', axis_index_groups=[[g, g ^ bits] for g in...  36.7 us
    all_to_all x2, blocking collectives, exchange(): lax.all_to_all(value, 'group', 0, 0, tiled=True, axis_index_groups=along_y)  32.2 us
    ppermute x3, starting transfers between devices, send(): return lax.ppermute(value, 'group', [(g, g ^ bits) for g in range(16)])  9.41 us
    pallas_call x1, Pallas kernels, body(): call(root_kernel, square, [VM] * 7, [factors], flops=20 * BS ** 3)  4.94 us
    unnamed x7, local copies, waits for them, and re-layouts  2.73 us
    pallas_call x1, Pallas kernels, body(): call(early_kernel, (corners, square, corners, square, scalar, scalar), [V...  2.01 us
  transfers between devices with their start and end apart: 3, of which 1 were waited for; matrix products, arithmetic and copies ran while one was open for 1% of the time, Pallas kernels for 4%

profile of v10, /device:TPU:39, one launch (start us, length us, event | category | flops | bytes accessed | tf_op | source)
XLA Modules:
  0.0 92.3 jit_solution(6318957665382866235)
XLA Ops:
  0.6 2.6 %collective-permute-start = (bf16[2,512,512]{2,1,0:T(8,128)(2,1)}, bf16[2,512,512]{2,1,0:T(8,128)(2,1)S(1)}, u32[]{:S(2)}, u32[]{:S(2)}) collective-permute-start(bf16[2,512,512]{2,1,0:T(8,128)(2,1)} %bitcast.7), channel_id=1, source_target_pairs={{0,32},{32,0},{64,96},{96,64},{128,160},{160,128},{192,224},{224,1... | collective-permute-start | bytes 3145736 | tf_op jit(solution)/shard_map/ppermute | solution.py:284
  3.2 0.8 copy.9.owner
  4.0 0.0 copy-start
  4.0 1.2 %copy-done = f32[1,1,512,512]{3,2,1,0:T(8,128)S(1)} copy-done((f32[1,1,512,512]{3,2,1,0:T(8,128)S(1)}, f32[1,1,512,512]{3,2,1,0:T(8,128)}, u32[]{:S(2)}) %copy-start) | copy-done | bytes 1048600
  5.2 0.0 copy-start.2
  5.2 0.1 shard_map.50.packed
  5.3 0.4 collective-permute-done.got
  5.7 0.7 copy-done.2
  6.4 0.1 shard_map.51
  6.6 16.2 %all_to_all.10.got = bf16[4,200,512]{2,1,0:T(8,128)(2,1)S(1)} all-to-all(bf16[4,200,512]{2,1,0:T(8,128)(2,1)S(1)} %shard_map.51), channel_id=1, replica_groups={{0,64,128,192},{32,96,160,224},{256,320,384,448},{288,352,416,480},{1,6..., dimensions={0} | all-to-all | bytes 1638400 | tf_op jit(solution)/shard_map/all_to_all | solution.py:290
  22.7 0.2 shard_map.52
  22.9 36.7 %all-gather = bf16[528,512]{1,0:T(8,128)(2,1)S(1)} all-gather(bf16[264,512]{1,0:T(8,128)(2,1)S(1)} %shard_map.52), channel_id=2, replica_groups={{0,256},{32,288},{64,320},{96,352},{128,384},{160,416},{192,448},{224,4..., dimensions={0}, use_global_device_ids=true | all-gather | bytes 811008 | tf_op jit(solution)/shard_map/all_gather | solution.py:287
  59.6 0.2 shard_map.53
  59.8 16.0 %all_to_all.11.got = bf16[4,264,512]{2,1,0:T(8,128)(2,1)S(1)} all-to-all(bf16[4,264,512]{2,1,0:T(8,128)(2,1)S(1)} %shard_map.53), channel_id=1, replica_groups={{0,64,128,192},{32,96,160,224},{256,320,384,448},{288,352,416,480},{1,6..., dimensions={0} | all-to-all | bytes 2162688 | tf_op jit(solution)/shard_map/all_to_all | solution.py:290
  75.8 0.1 shard_map.55
  75.9 4.7 %collective-permute-start.1 = (bf16[784,512]{1,0:T(8,128)(2,1)S(1)}, bf16[784,512]{1,0:T(8,128)(2,1)S(1)}, u32[]{:S(2)}, u32[]{:S(2)}) collective-permute-start(bf16[784,512]{1,0:T(8,128)(2,1)S(1)} %shard_map.55), channel_id=1, source_target_pairs={{0,32},{32,0},{64,96},{96,64},{128,160},{160,128},{192,224},{224,1... | collective-permute-start | bytes 2408456 | tf_op jit(solution)/shard_map/ppermute | solution.py:284
  80.5 2.0 %shard_map.54 = (f32[3,256,256]{2,1,0:T(8,128)S(1)}, bf16[512,512]{1,0:T(8,128)(2,1)S(1)}, f32[3,256,256]{2,1,0:T(8,128)S(1)}, bf16[512,512]{1,0:T(8,128)(2,1)S(...) custom-call(bf16[4,264,512]{2,1,0:T(8,128)(2,1)S(1)} %all_to_all.11.got), custom_call_target="tpu_custom_call" | custom-call | flops 1073741824 | tf_op jit(solution)/shard_map/pallas_call | solution.py:304
  82.5 0.0 collective-permute-done.1.far
  82.6 0.0 copy-start.1
  82.6 4.9 %shard_map.56.mine = bf16[512,512]{1,0:T(8,128)(2,1)S(1)} custom-call(f32[3,256,256]{2,1,0:T(8,128)S(1)} %get-tuple-element.11.gram, bf16[512,512]{1,0:T(8,128)(2,1)S(1)} %get-tuple-element.12.low, f32[3,256,256]{2,1,0:T(8,128)S(1)} %get-tuple-element.13.later, bf16[512,512]{1,0:T(8,128)(2,1)S(1)} %get-tuple-element.10.dense, ...), custom_call_target="tpu_custom_call" | custom-call | flops 2684354560 | tf_op jit(solution)/shard_map/pallas_call | solution.py:307
  87.5 2.2 %collective-permute-start.2 = (bf16[512,512]{1,0:T(8,128)(2,1)S(1)}, bf16[512,512]{1,0:T(8,128)(2,1)S(1)}, u32[]{:S(2)}, u32[]{:S(2)}) collective-permute-start(bf16[512,512]{1,0:T(8,128)(2,1)S(1)} %shard_map.56.mine), channel_id=1, source_target_pairs={{0,32},{32,0},{64,96},{96,64},{128,160},{160,128},{192,224},{224,1... | collective-permute-start | bytes 1572872 | tf_op jit(solution)/shard_map/ppermute | solution.py:284
  89.7 0.0 copy-done.1
  89.7 1.8 %shard_map.57 = (f32[512,512]{1,0:T(8,128)}, bf16[2,512,512]{2,1,0:T(8,128)(2,1)}) custom-call(s32[32,2]{1,0:T(8,128)S(1)} %copy.9.owner, bf16[512,512]{1,0:T(8,128)(2,1)S(1)} %get-tuple-element.10.dense, bf16[784,512]{1,0:T(8,128)(2,1)S(1)} %collective-permute-done.1.far, f32[512,512]{1,0:T(8,128)S(1)} %bitcast.5, bf16[512,512]{1,0:T(8,128)(2,1)S(1)} %shard_map.56.mine), custom_call_target="tpu_custom_call" | custom-call | flops 268435456 | bytes 3145728 | tf_op jit(solution)/shard_map/pallas_call | solution.py:309
  91.5 0.0 collective-permute-done.2.other
  91.5 0.8 shard_map.58
Async XLA Ops:
  0.6 5.1 %collective-permute-start = (bf16[2,512,512]{2,1,0:T(8,128)(2,1)}, bf16[2,512,512]{2,1,0:T(8,128)(2,1)S(1)}, u32[]{:S(2)}, u32[]{:S(2)}) collective-permute-start(bf16[2,512,512]{2,1,0:T(8,128)(2,1)} %bitcast.7), channel_id=1, source_target_pairs={{0,32},{32,0},{64,96},{96,64},{128,160},{160,128},{192,224},{224,1... | collective-permute-start | bytes 3145736 | tf_op jit(solution)/shard_map/ppermute | solution.py:284
  4.0 1.2 %copy-start = (f32[1,1,512,512]{3,2,1,0:T(8,128)S(1)}, f32[1,1,512,512]{3,2,1,0:T(8,128)}, u32[]{:S(2)}) copy-start(f32[1,1,512,512]{3,2,1,0:T(8,128)} %param.4) | copy-start | bytes 3145732
  5.2 1.2 %copy-start.2 = (bf16[1,2,512,512]{3,2,1,0:T(8,128)(2,1)S(1)}, bf16[1,2,512,512]{3,2,1,0:T(8,128)(2,1)}, u32[]{:S(2)}) copy-start(bf16[1,2,512,512]{3,2,1,0:T(8,128)(2,1)} %param.3) | copy-start | bytes 3145732
  75.9 6.7 %collective-permute-start.1 = (bf16[784,512]{1,0:T(8,128)(2,1)S(1)}, bf16[784,512]{1,0:T(8,128)(2,1)S(1)}, u32[]{:S(2)}, u32[]{:S(2)}) collective-permute-start(bf16[784,512]{1,0:T(8,128)(2,1)S(1)} %shard_map.55), channel_id=1, source_target_pairs={{0,32},{32,0},{64,96},{96,64},{128,160},{160,128},{192,224},{224,1... | collective-permute-start | bytes 2408456 | tf_op jit(solution)/shard_map/ppermute | solution.py:284
  82.6 7.1 %copy-start.1 = (f32[1,1,512,512]{3,2,1,0:T(8,128)S(1)}, f32[1,1,512,512]{3,2,1,0:T(8,128)}, u32[]{:S(2)}) copy-start(f32[1,1,512,512]{3,2,1,0:T(8,128)} %param.4) | copy-start | bytes 3145732
  87.5 4.0 %collective-permute-start.2 = (bf16[512,512]{1,0:T(8,128)(2,1)S(1)}, bf16[512,512]{1,0:T(8,128)(2,1)S(1)}, u32[]{:S(2)}, u32[]{:S(2)}) collective-permute-start(bf16[512,512]{1,0:T(8,128)(2,1)S(1)} %shard_map.56.mine), channel_id=1, source_target_pairs={{0,32},{32,0},{64,96},{96,64},{128,160},{160,128},{192,224},{224,1... | collective-permute-start | bytes 1572872 | tf_op jit(solution)/shard_map/ppermute | solution.py:284

commit v11 on v10

--- a/solution.py
+++ b/solution.py
@@ -50,8 +50,8 @@
 
 
 def owner_of(owner, block):
-    row = lax.broadcasted_iota(jnp.int32, owner.shape, 0) == lax.axis_index("dp")
-    col = lax.broadcasted_iota(jnp.int32, owner.shape, 1) == block
+    row = lax.broadcasted_iota(jnp.int32, owner.shape, 0) == block
+    col = lax.broadcasted_iota(jnp.int32, owner.shape, 1) == lax.axis_index("dp")
     return jnp.sum(jnp.where(row & col, owner[...], 0))
 
 
@@ -290,6 +290,7 @@
         return lax.all_to_all(value, "group", 0, 0, tiled=True, axis_index_groups=along_y)
 
     block = grad[0]
+    owner = owner.T
     stat = stats[0, 0]
     got = send(block, 1)
     packed = call(pack_kernel, array(4, STAT, BS), [VM], nbytes=3 << 19)(stat)

time: 92.7 us -> 91.8 us (level)
  the two profiles are of different devices: /device:TPU:39 before, /device:TPU:35 now
where the time goes in v11:
time: 91.8 us; the launch traced here: 91.5 us
  blocking collectives  68.8 us (75%)
  Pallas kernels  10.1 us (11%)
  starting transfers between devices  9.41 us (10%)
  local copies, waits for them, and re-layouts  1.23 us (1%)
  waiting for transfers between devices  1.19 us (1%)
    all_gather x1, blocking collectives, gather(): lax.all_gather(value, 'group', axis_index_groups=[[g, g ^ bits] for g in...  36.7 us
    all_to_all x2, blocking collectives, exchange(): lax.all_to_all(value, 'group', 0, 0, tiled=True, axis_index_groups=along_y)  32.1 us
    ppermute x3, starting transfers between devices, send(): return lax.ppermute(value, 'group', [(g, g ^ bits) for g in range(16)])  9.41 us
    pallas_call x1, Pallas kernels, body(): call(root_kernel, square, [VM] * 7, [factors], flops=20 * BS ** 3)  4.94 us
    pallas_call x1, Pallas kernels, body(): call(early_kernel, (corners, square, corners, square, scalar, scalar), [V...  2.01 us
  transfers between devices with their start and end apart: 3, of which 1 were waited for; matrix products, arithmetic and copies ran while one was open for 0% of the time, Pallas kernels for 4%

profile of v11, /device:TPU:35, one launch (start us, length us, event | category | flops | bytes accessed | tf_op | source)
XLA Modules:
  0.0 91.5 jit_solution(4959135473026064594)
XLA Ops:
  0.6 0.0 copy-start.3
  0.6 2.6 %collective-permute-start = (bf16[2,512,512]{2,1,0:T(8,128)(2,1)}, bf16[2,512,512]{2,1,0:T(8,128)(2,1)S(1)}, u32[]{:S(2)}, u32[]{:S(2)}) collective-permute-start(bf16[2,512,512]{2,1,0:T(8,128)(2,1)} %bitcast.8), channel_id=1, source_target_pairs={{0,32},{32,0},{64,96},{96,64},{128,160},{160,128},{192,224},{224,1... | collective-permute-start | bytes 3145736 | tf_op jit(solution)/shard_map/ppermute | solution.py:284
  3.2 0.0 copy-start
  3.2 1.2 %copy-done = f32[1,1,512,512]{3,2,1,0:T(8,128)S(1)} copy-done((f32[1,1,512,512]{3,2,1,0:T(8,128)S(1)}, f32[1,1,512,512]{3,2,1,0:T(8,128)}, u32[]{:S(2)}) %copy-start) | copy-done | bytes 1048600
  4.5 0.0 copy-start.2
  4.5 0.1 shard_map.50.packed
  4.5 1.2 %collective-permute-done.got = bf16[2,512,512]{2,1,0:T(8,128)(2,1)S(1)} collective-permute-done((bf16[2,512,512]{2,1,0:T(8,128)(2,1)}, bf16[2,512,512]{2,1,0:T(8,128)(2,1)S(1)}, u32[]{:S(2)}, u32[]{:S(2)}) %collective-permute-start) | collective-permute-done | bytes 1048608 | tf_op jit(solution)/shard_map/ppermute | solution.py:284
  5.7 0.0 copy-done.3
  5.7 0.0 copy-done.2
  5.7 0.1 shard_map.51
  5.8 16.1 %all_to_all.10.got = bf16[4,200,512]{2,1,0:T(8,128)(2,1)S(1)} all-to-all(bf16[4,200,512]{2,1,0:T(8,128)(2,1)S(1)} %shard_map.51), channel_id=1, replica_groups={{0,64,128,192},{32,96,160,224},{256,320,384,448},{288,352,416,480},{1,6..., dimensions={0} | all-to-all | bytes 1638400 | tf_op jit(solution)/shard_map/all_to_all | solution.py:290
  21.9 0.2 shard_map.52
  22.1 36.7 %all-gather = bf16[528,512]{1,0:T(8,128)(2,1)S(1)} all-gather(bf16[264,512]{1,0:T(8,128)(2,1)S(1)} %shard_map.52), channel_id=2, replica_groups={{0,256},{32,288},{64,320},{96,352},{128,384},{160,416},{192,448},{224,4..., dimensions={0}, use_global_device_ids=true | all-gather | bytes 811008 | tf_op jit(solution)/shard_map/all_gather | solution.py:287
  58.7 0.2 shard_map.53
  58.9 16.0 %all_to_all.11.got = bf16[4,264,512]{2,1,0:T(8,128)(2,1)S(1)} all-to-all(bf16[4,264,512]{2,1,0:T(8,128)(2,1)S(1)} %shard_map.53), channel_id=1, replica_groups={{0,64,128,192},{32,96,160,224},{256,320,384,448},{288,352,416,480},{1,6..., dimensions={0} | all-to-all | bytes 2162688 | tf_op jit(solution)/shard_map/all_to_all | solution.py:290
  75.0 0.1 shard_map.55
  75.0 4.7 %collective-permute-start.1 = (bf16[784,512]{1,0:T(8,128)(2,1)S(1)}, bf16[784,512]{1,0:T(8,128)(2,1)S(1)}, u32[]{:S(2)}, u32[]{:S(2)}) collective-permute-start(bf16[784,512]{1,0:T(8,128)(2,1)S(1)} %shard_map.55), channel_id=1, source_target_pairs={{0,32},{32,0},{64,96},{96,64},{128,160},{160,128},{192,224},{224,1... | collective-permute-start | bytes 2408456 | tf_op jit(solution)/shard_map/ppermute | solution.py:284
  79.7 2.0 %shard_map.54 = (f32[3,256,256]{2,1,0:T(8,128)S(1)}, bf16[512,512]{1,0:T(8,128)(2,1)S(1)}, f32[3,256,256]{2,1,0:T(8,128)S(1)}, bf16[512,512]{1,0:T(8,128)(2,1)S(...) custom-call(bf16[4,264,512]{2,1,0:T(8,128)(2,1)S(1)} %all_to_all.11.got), custom_call_target="tpu_custom_call" | custom-call | flops 1073741824 | tf_op jit(solution)/shard_map/pallas_call | solution.py:305
  81.7 0.0 collective-permute-done.1.far
  81.7 0.0 copy-start.1
  81.7 4.9 %shard_map.56.mine = bf16[512,512]{1,0:T(8,128)(2,1)S(1)} custom-call(f32[3,256,256]{2,1,0:T(8,128)S(1)} %get-tuple-element.11.gram, bf16[512,512]{1,0:T(8,128)(2,1)S(1)} %get-tuple-element.12.low, f32[3,256,256]{2,1,0:T(8,128)S(1)} %get-tuple-element.13.later, bf16[512,512]{1,0:T(8,128)(2,1)S(1)} %get-tuple-element.10.dense, ...), custom_call_target="tpu_custom_call" | custom-call | flops 2684354560 | tf_op jit(solution)/shard_map/pallas_call | solution.py:308
  86.7 2.2 %collective-permute-start.2 = (bf16[512,512]{1,0:T(8,128)(2,1)S(1)}, bf16[512,512]{1,0:T(8,128)(2,1)S(1)}, u32[]{:S(2)}, u32[]{:S(2)}) collective-permute-start(bf16[512,512]{1,0:T(8,128)(2,1)S(1)} %shard_map.56.mine), channel_id=1, source_target_pairs={{0,32},{32,0},{64,96},{96,64},{128,160},{160,128},{192,224},{224,1... | collective-permute-start | bytes 1572872 | tf_op jit(solution)/shard_map/ppermute | solution.py:284
  88.8 0.0 copy-done.1
  88.9 1.8 %shard_map.57 = (f32[512,512]{1,0:T(8,128)}, bf16[2,512,512]{2,1,0:T(8,128)(2,1)}) custom-call(s32[2,32]{1,0:T(2,128)S(1)} %bitcast.13, bf16[512,512]{1,0:T(8,128)(2,1)S(1)} %get-tuple-element.10.dense, bf16[784,512]{1,0:T(8,128)(2,1)S(1)} %collective-permute-done.1.far, f32[512,512]{1,0:T(8,128)S(1)} %bitcast.6, bf16[512,512]{1,0:T(8,128)(2,1)S(1)} %shard_map.56.mine), custom_call_target="tpu_custom_call" | custom-call | flops 268435456 | bytes 3145728 | tf_op jit(solution)/shard_map/pallas_call | solution.py:310
  90.7 0.0 collective-permute-done.2.other
  90.7 0.8 shard_map.58
Async XLA Ops:
  0.6 5.1 %copy-start.3 = (s32[32,2]{0,1:T(2,128)S(1)}, s32[32,2]{0,1:T(2,128)}, u32[]{:S(2)}) copy-start(s32[32,2]{0,1:T(2,128)} %param.5) | copy-start | bytes 772
  0.6 5.1 %collective-permute-start = (bf16[2,512,512]{2,1,0:T(8,128)(2,1)}, bf16[2,512,512]{2,1,0:T(8,128)(2,1)S(1)}, u32[]{:S(2)}, u32[]{:S(2)}) collective-permute-start(bf16[2,512,512]{2,1,0:T(8,128)(2,1)} %bitcast.8), channel_id=1, source_target_pairs={{0,32},{32,0},{64,96},{96,64},{128,160},{160,128},{192,224},{224,1... | collective-permute-start | bytes 3145736 | tf_op jit(solution)/shard_map/ppermute | solution.py:284
  3.2 1.2 %copy-start = (f32[1,1,512,512]{3,2,1,0:T(8,128)S(1)}, f32[1,1,512,512]{3,2,1,0:T(8,128)}, u32[]{:S(2)}) copy-start(f32[1,1,512,512]{3,2,1,0:T(8,128)} %param.4) | copy-start | bytes 3145732
  4.5 1.3 %copy-start.2 = (bf16[1,2,512,512]{3,2,1,0:T(8,128)(2,1)S(1)}, bf16[1,2,512,512]{3,2,1,0:T(8,128)(2,1)}, u32[]{:S(2)}) copy-start(bf16[1,2,512,512]{3,2,1,0:T(8,128)(2,1)} %param.3) | copy-start | bytes 3145732
  75.0 6.7 %collective-permute-start.1 = (bf16[784,512]{1,0:T(8,128)(2,1)S(1)}, bf16[784,512]{1,0:T(8,128)(2,1)S(1)}, u32[]{:S(2)}, u32[]{:S(2)}) collective-permute-start(bf16[784,512]{1,0:T(8,128)(2,1)S(1)} %shard_map.55), channel_id=1, source_target_pairs={{0,32},{32,0},{64,96},{96,64},{128,160},{160,128},{192,224},{224,1... | collective-permute-start | bytes 2408456 | tf_op jit(solution)/shard_map/ppermute | solution.py:284
  81.7 7.1 %copy-start.1 = (f32[1,1,512,512]{3,2,1,0:T(8,128)S(1)}, f32[1,1,512,512]{3,2,1,0:T(8,128)}, u32[]{:S(2)}) copy-start(f32[1,1,512,512]{3,2,1,0:T(8,128)} %param.4) | copy-start | bytes 3145732
  86.7 4.0 %collective-permute-start.2 = (bf16[512,512]{1,0:T(8,128)(2,1)S(1)}, bf16[512,512]{1,0:T(8,128)(2,1)S(1)}, u32[]{:S(2)}, u32[]{:S(2)}) collective-permute-start(bf16[512,512]{1,0:T(8,128)(2,1)S(1)} %shard_map.56.mine), channel_id=1, source_target_pairs={{0,32},{32,0},{64,96},{96,64},{128,160},{160,128},{192,224},{224,1... | collective-permute-start | bytes 1572872 | tf_op jit(solution)/shard_map/ppermute | solution.py:284

commit v12 on v11

--- a/solution.py
+++ b/solution.py
@@ -234,10 +234,10 @@
     out[...] = (value * ratio).astype(BF)
 
 
-def stat_kernel(owner, dense, far, stat, mine, out, update, oriented, sem):
+def stat_kernel(owner, dense, far, stat, mine, out, update, oriented, fresh, sems):
     core, y, half = place()
-    copy = pltpu.make_async_copy(mine, update.at[core], sem)
-    copy.start()
+    copies = [pltpu.make_async_copy(mine, update.at[core], sems.at[4])]
+    copies[0].start()
     pair = half * 4 + y
     own = owner_of(owner, core) == pair
     other = owner_of(owner, 1 - core) == pair
@@ -255,18 +255,23 @@
         oriented[...] = oriented[...].T
 
     active = jnp.logical_or(own, other)
-
-    @pl.when(active)
-    def _():
-        side = oriented[...]
-        gram = lax.dot_general(side, side, (((1,), (1,)), ((), ())), preferred_element_type=F32)
-        out[...] = BETA * stat[...] + (1.0 - BETA) * gram
-
-    @pl.when(jnp.logical_not(active))
-    def _():
-        out[...] = stat[...]
-
-    copy.wait()
+    for tile in range(4):
+        rows = slice(tile * CHUNK, (tile + 1) * CHUNK)
+
+        @pl.when(active)
+        def _():
+            numbers = (((1,), (1,)), ((), ()))
+            gram = lax.dot_general(oriented[rows, :], oriented[...], numbers, preferred_element_type=F32)
+            fresh[rows, :] = BETA * stat[rows, :] + (1.0 - BETA) * gram
+
+        @pl.when(jnp.logical_not(active))
+        def _():
+            fresh[rows, :] = stat[rows, :]
+
+        copies.append(pltpu.make_async_copy(fresh.at[rows, :], out.at[rows, :], sems.at[tile]))
+        copies[-1].start()
+    for copy in copies:
+        copy.wait()
 
 
 def last_kernel(other, begun, out, sem):
@@ -311,10 +316,10 @@
         stat_kernel,
         (array(BS, BS, dtype=F32), array(2, BS, BS)),
         [VM, VM, VM, VM, VM],
-        [pltpu.VMEM((BS, BS), BF), pltpu.SemaphoreType.DMA],
+        [pltpu.VMEM((BS, BS), BF), pltpu.VMEM((BS, BS), F32), pltpu.SemaphoreType.DMA((5,))],
         flops=2 * BS**3,
         nbytes=3 << 20,
-        out_spec=(VM, HBM),
+        out_spec=(HBM, HBM),
     )(owner, dense, far, stat, mine)
     update = call(
         last_kernel,

time: 91.8 us -> 91.6 us (level)
  the two profiles are of different devices: /device:TPU:35 before, /device:TPU:39 now
where the time goes in v12:
time: 91.6 us; the launch traced here: 91.3 us
  blocking collectives  68.8 us (75%)
  Pallas kernels  9.68 us (11%)
  starting transfers between devices  9.41 us (10%)
  waiting for transfers between devices  1.46 us (2%)
  local copies, waits for them, and re-layouts  1.23 us (1%)
    all_gather x1, blocking collectives, gather(): lax.all_gather(value, 'group', axis_index_groups=[[g, g ^ bits] for g in...  36.7 us
    all_to_all x2, blocking collectives, exchange(): lax.all_to_all(value, 'group', 0, 0, tiled=True, axis_index_groups=along_y)  32.1 us
    ppermute x3, starting transfers between devices, send(): return lax.ppermute(value, 'group', [(g, g ^ bits) for g in range(16)])  9.41 us
    pallas_call x1, Pallas kernels, body(): call(root_kernel, square, [VM] * 7, [factors], flops=20 * BS ** 3)  4.94 us
    pallas_call x1, Pallas kernels, body(): call(early_kernel, (corners, square, corners, square, scalar, scalar), [V...  2.01 us
  transfers between devices with their start and end apart: 3, of which 2 were waited for; matrix products, arithmetic and copies ran while one was open for 0% of the time, Pallas kernels for 4%

profile of v12, /device:TPU:39, one launch (start us, length us, event | category | flops | bytes accessed | tf_op | source)
XLA Modules:
  0.0 91.3 jit_solution(4719780631666162621)
XLA Ops:
  0.6 0.0 copy-start.3
  0.6 2.6 %collective-permute-start = (bf16[2,512,512]{2,1,0:T(8,128)(2,1)}, bf16[2,512,512]{2,1,0:T(8,128)(2,1)S(1)}, u32[]{:S(2)}, u32[]{:S(2)}) collective-permute-start(bf16[2,512,512]{2,1,0:T(8,128)(2,1)} %bitcast.8), channel_id=1, source_target_pairs={{0,32},{32,0},{64,96},{96,64},{128,160},{160,128},{192,224},{224,1... | collective-permute-start | bytes 3145736 | tf_op jit(solution)/shard_map/ppermute | solution.py:289
  3.2 0.0 copy-start
  3.2 1.2 %copy-done = f32[1,1,512,512]{3,2,1,0:T(8,128)S(1)} copy-done((f32[1,1,512,512]{3,2,1,0:T(8,128)S(1)}, f32[1,1,512,512]{3,2,1,0:T(8,128)}, u32[]{:S(2)}) %copy-start) | copy-done | bytes 1048600
  4.5 0.0 copy-start.2
  4.5 0.1 shard_map.50.packed
  4.5 1.2 %collective-permute-done.got = bf16[2,512,512]{2,1,0:T(8,128)(2,1)S(1)} collective-permute-done((bf16[2,512,512]{2,1,0:T(8,128)(2,1)}, bf16[2,512,512]{2,1,0:T(8,128)(2,1)S(1)}, u32[]{:S(2)}, u32[]{:S(2)}) %collective-permute-start) | collective-permute-done | bytes 1048608 | tf_op jit(solution)/shard_map/ppermute | solution.py:289
  5.7 0.0 copy-done.3
  5.7 0.0 copy-done.2
  5.7 0.1 shard_map.51
  5.8 16.1 %all_to_all.10.got = bf16[4,200,512]{2,1,0:T(8,128)(2,1)S(1)} all-to-all(bf16[4,200,512]{2,1,0:T(8,128)(2,1)S(1)} %shard_map.51), channel_id=1, replica_groups={{0,64,128,192},{32,96,160,224},{256,320,384,448},{288,352,416,480},{1,6..., dimensions={0} | all-to-all | bytes 1638400 | tf_op jit(solution)/shard_map/all_to_all | solution.py:295
  21.9 0.2 shard_map.52
  22.1 36.7 %all-gather = bf16[528,512]{1,0:T(8,128)(2,1)S(1)} all-gather(bf16[264,512]{1,0:T(8,128)(2,1)S(1)} %shard_map.52), channel_id=2, replica_groups={{0,256},{32,288},{64,320},{96,352},{128,384},{160,416},{192,448},{224,4..., dimensions={0}, use_global_device_ids=true | all-gather | bytes 811008 | tf_op jit(solution)/shard_map/all_gather | solution.py:292
  58.7 0.2 shard_map.53
  58.9 16.0 %all_to_all.11.got = bf16[4,264,512]{2,1,0:T(8,128)(2,1)S(1)} all-to-all(bf16[4,264,512]{2,1,0:T(8,128)(2,1)S(1)} %shard_map.53), channel_id=1, replica_groups={{0,64,128,192},{32,96,160,224},{256,320,384,448},{288,352,416,480},{1,6..., dimensions={0} | all-to-all | bytes 2162688 | tf_op jit(solution)/shard_map/all_to_all | solution.py:295
  75.0 0.1 shard_map.55
  75.0 4.7 %collective-permute-start.1 = (bf16[784,512]{1,0:T(8,128)(2,1)S(1)}, bf16[784,512]{1,0:T(8,128)(2,1)S(1)}, u32[]{:S(2)}, u32[]{:S(2)}) collective-permute-start(bf16[784,512]{1,0:T(8,128)(2,1)S(1)} %shard_map.55), channel_id=1, source_target_pairs={{0,32},{32,0},{64,96},{96,64},{128,160},{160,128},{192,224},{224,1... | collective-permute-start | bytes 2408456 | tf_op jit(solution)/shard_map/ppermute | solution.py:289
  79.7 2.0 %shard_map.54 = (f32[3,256,256]{2,1,0:T(8,128)S(1)}, bf16[512,512]{1,0:T(8,128)(2,1)S(1)}, f32[3,256,256]{2,1,0:T(8,128)S(1)}, bf16[512,512]{1,0:T(8,128)(2,1)S(...) custom-call(bf16[4,264,512]{2,1,0:T(8,128)(2,1)S(1)} %all_to_all.11.got), custom_call_target="tpu_custom_call" | custom-call | flops 1073741824 | tf_op jit(solution)/shard_map/pallas_call | solution.py:310
  81.7 0.0 collective-permute-done.1.far
  81.7 0.0 copy-start.1
  81.7 4.9 %shard_map.56.mine = bf16[512,512]{1,0:T(8,128)(2,1)S(1)} custom-call(f32[3,256,256]{2,1,0:T(8,128)S(1)} %get-tuple-element.11.gram, bf16[512,512]{1,0:T(8,128)(2,1)S(1)} %get-tuple-element.12.low, f32[3,256,256]{2,1,0:T(8,128)S(1)} %get-tuple-element.13.later, bf16[512,512]{1,0:T(8,128)(2,1)S(1)} %get-tuple-element.10.dense, ...), custom_call_target="tpu_custom_call" | custom-call | flops 2684354560 | tf_op jit(solution)/shard_map/pallas_call | solution.py:313
  86.7 2.2 %collective-permute-start.2 = (bf16[512,512]{1,0:T(8,128)(2,1)S(1)}, bf16[512,512]{1,0:T(8,128)(2,1)S(1)}, u32[]{:S(2)}, u32[]{:S(2)}) collective-permute-start(bf16[512,512]{1,0:T(8,128)(2,1)S(1)} %shard_map.56.mine), channel_id=1, source_target_pairs={{0,32},{32,0},{64,96},{96,64},{128,160},{160,128},{192,224},{224,1... | collective-permute-start | bytes 1572872 | tf_op jit(solution)/shard_map/ppermute | solution.py:289
  88.8 0.0 copy-done.1
  88.9 1.4 %shard_map.57 = (f32[512,512]{1,0:T(8,128)}, bf16[2,512,512]{2,1,0:T(8,128)(2,1)}) custom-call(s32[2,32]{1,0:T(2,128)S(1)} %bitcast.13, bf16[512,512]{1,0:T(8,128)(2,1)S(1)} %get-tuple-element.10.dense, bf16[784,512]{1,0:T(8,128)(2,1)S(1)} %collective-permute-done.1.far, f32[512,512]{1,0:T(8,128)S(1)} %bitcast.6, bf16[512,512]{1,0:T(8,128)(2,1)S(1)} %shard_map.56.mine), custom_call_target="tpu_custom_call" | custom-call | flops 268435456 | bytes 3145728 | tf_op jit(solution)/shard_map/pallas_call | solution.py:315
  90.2 0.3 collective-permute-done.2.other
  90.5 0.8 shard_map.58
Async XLA Ops:
  0.6 5.1 %copy-start.3 = (s32[32,2]{0,1:T(2,128)S(1)}, s32[32,2]{0,1:T(2,128)}, u32[]{:S(2)}) copy-start(s32[32,2]{0,1:T(2,128)} %param.5) | copy-start | bytes 772
  0.6 5.1 %collective-permute-start = (bf16[2,512,512]{2,1,0:T(8,128)(2,1)}, bf16[2,512,512]{2,1,0:T(8,128)(2,1)S(1)}, u32[]{:S(2)}, u32[]{:S(2)}) collective-permute-start(bf16[2,512,512]{2,1,0:T(8,128)(2,1)} %bitcast.8), channel_id=1, source_target_pairs={{0,32},{32,0},{64,96},{96,64},{128,160},{160,128},{192,224},{224,1... | collective-permute-start | bytes 3145736 | tf_op jit(solution)/shard_map/ppermute | solution.py:289
  3.2 1.2 %copy-start = (f32[1,1,512,512]{3,2,1,0:T(8,128)S(1)}, f32[1,1,512,512]{3,2,1,0:T(8,128)}, u32[]{:S(2)}) copy-start(f32[1,1,512,512]{3,2,1,0:T(8,128)} %param.4) | copy-start | bytes 3145732
  4.5 1.3 %copy-start.2 = (bf16[1,2,512,512]{3,2,1,0:T(8,128)(2,1)S(1)}, bf16[1,2,512,512]{3,2,1,0:T(8,128)(2,1)}, u32[]{:S(2)}) copy-start(bf16[1,2,512,512]{3,2,1,0:T(8,128)(2,1)} %param.3) | copy-start | bytes 3145732
  75.0 6.7 %collective-permute-start.1 = (bf16[784,512]{1,0:T(8,128)(2,1)S(1)}, bf16[784,512]{1,0:T(8,128)(2,1)S(1)}, u32[]{:S(2)}, u32[]{:S(2)}) collective-permute-start(bf16[784,512]{1,0:T(8,128)(2,1)S(1)} %shard_map.55), channel_id=1, source_target_pairs={{0,32},{32,0},{64,96},{96,64},{128,160},{160,128},{192,224},{224,1... | collective-permute-start | bytes 2408456 | tf_op jit(solution)/shard_map/ppermute | solution.py:289
  81.7 7.1 %copy-start.1 = (f32[1,1,512,512]{3,2,1,0:T(8,128)S(1)}, f32[1,1,512,512]{3,2,1,0:T(8,128)}, u32[]{:S(2)}) copy-start(f32[1,1,512,512]{3,2,1,0:T(8,128)} %param.4) | copy-start | bytes 3145732
  86.7 3.8 %collective-permute-start.2 = (bf16[512,512]{1,0:T(8,128)(2,1)S(1)}, bf16[512,512]{1,0:T(8,128)(2,1)S(1)}, u32[]{:S(2)}, u32[]{:S(2)}) collective-permute-start(bf16[512,512]{1,0:T(8,128)(2,1)S(1)} %shard_map.56.mine), channel_id=1, source_target_pairs={{0,32},{32,0},{64,96},{96,64},{128,160},{160,128},{192,224},{224,1... | collective-permute-start | bytes 1572872 | tf_op jit(solution)/shard_map/ppermute | solution.py:289

commit v13 on v11

--- a/solution.py
+++ b/solution.py
@@ -234,10 +234,10 @@
     out[...] = (value * ratio).astype(BF)
 
 
-def stat_kernel(owner, dense, far, stat, mine, out, update, oriented, sem):
+def stat_kernel(owner, dense, far, stat, mine, out, update, oriented, fresh, sems):
     core, y, half = place()
-    copy = pltpu.make_async_copy(mine, update.at[core], sem)
-    copy.start()
+    copies = [pltpu.make_async_copy(mine, update.at[core], sems.at[4])]
+    copies[0].start()
     pair = half * 4 + y
     own = owner_of(owner, core) == pair
     other = owner_of(owner, 1 - core) == pair
@@ -255,18 +255,25 @@
         oriented[...] = oriented[...].T
 
     active = jnp.logical_or(own, other)
+    tiles = [slice(tile * CHUNK, (tile + 1) * CHUNK) for tile in range(4)]
+    copies += [pltpu.make_async_copy(fresh.at[rows, :], out.at[rows, :], sems.at[k]) for k, rows in enumerate(tiles)]
 
     @pl.when(active)
     def _():
         side = oriented[...]
         gram = lax.dot_general(side, side, (((1,), (1,)), ((), ())), preferred_element_type=F32)
-        out[...] = BETA * stat[...] + (1.0 - BETA) * gram
+        for rows, copy in zip(tiles, copies[1:]):
+            fresh[rows, :] = BETA * stat[rows, :] + (1.0 - BETA) * gram[rows]
+            copy.start()
 
     @pl.when(jnp.logical_not(active))
     def _():
-        out[...] = stat[...]
-
-    copy.wait()
+        for rows, copy in zip(tiles, copies[1:]):
+            fresh[rows, :] = stat[rows, :]
+            copy.start()
+
+    for copy in copies:
+        copy.wait()
 
 
 def last_kernel(other, begun, out, sem):
@@ -311,10 +318,10 @@
         stat_kernel,
         (array(BS, BS, dtype=F32), array(2, BS, BS)),
         [VM, VM, VM, VM, VM],
-        [pltpu.VMEM((BS, BS), BF), pltpu.SemaphoreType.DMA],
+        [pltpu.VMEM((BS, BS), BF), pltpu.VMEM((BS, BS), F32), pltpu.SemaphoreType.DMA((5,))],
         flops=2 * BS**3,
         nbytes=3 << 20,
-        out_spec=(VM, HBM),
+        out_spec=(HBM, HBM),
     )(owner, dense, far, stat, mine)
     update = call(
         last_kernel,

time: 91.8 us -> 91.7 us (level)
  the two profiles are of different devices: /device:TPU:35 before, /device:TPU:39 now
where the time goes in v13:
time: 91.7 us; the launch traced here: 91.4 us
  blocking collectives  68.8 us (75%)
  Pallas kernels  10.1 us (11%)
  starting transfers between devices  9.41 us (10%)
  local copies, waits for them, and re-layouts  1.23 us (1%)
  waiting for transfers between devices  1.19 us (1%)
    all_gather x1, blocking collectives, gather(): lax.all_gather(value, 'group', axis_index_groups=[[g, g ^ bits] for g in...  36.7 us
    all_to_all x2, blocking collectives, exchange(): lax.all_to_all(value, 'group', 0, 0, tiled=True, axis_index_groups=along_y)  32.1 us
    ppermute x3, starting transfers between devices, send(): return lax.ppermute(value, 'group', [(g, g ^ bits) for g in range(16)])  9.41 us
    pallas_call x1, Pallas kernels, body(): call(root_kernel, square, [VM] * 7, [factors], flops=20 * BS ** 3)  4.94 us
    pallas_call x1, Pallas kernels, body(): call(early_kernel, (corners, square, corners, square, scalar, scalar), [V...  2.01 us
  transfers between devices with their start and end apart: 3, of which 1 were waited for; matrix products, arithmetic and copies ran while one was open for 0% of the time, Pallas kernels for 4%

profile of v13, /device:TPU:39, one launch (start us, length us, event | category | flops | bytes accessed | tf_op | source)
XLA Modules:
  0.0 91.4 jit_solution(17859848310846134891)
XLA Ops:
  0.6 0.0 copy-start.3
  0.6 2.6 %collective-permute-start = (bf16[2,512,512]{2,1,0:T(8,128)(2,1)}, bf16[2,512,512]{2,1,0:T(8,128)(2,1)S(1)}, u32[]{:S(2)}, u32[]{:S(2)}) collective-permute-start(bf16[2,512,512]{2,1,0:T(8,128)(2,1)} %bitcast.8), channel_id=1, source_target_pairs={{0,32},{32,0},{64,96},{96,64},{128,160},{160,128},{192,224},{224,1... | collective-permute-start | bytes 3145736 | tf_op jit(solution)/shard_map/ppermute | solution.py:291
  3.2 0.0 copy-start
  3.2 1.2 %copy-done = f32[1,1,512,512]{3,2,1,0:T(8,128)S(1)} copy-done((f32[1,1,512,512]{3,2,1,0:T(8,128)S(1)}, f32[1,1,512,512]{3,2,1,0:T(8,128)}, u32[]{:S(2)}) %copy-start) | copy-done | bytes 1048600
  4.5 0.0 copy-start.2
  4.5 0.1 shard_map.50.packed
  4.5 1.2 %collective-permute-done.got = bf16[2,512,512]{2,1,0:T(8,128)(2,1)S(1)} collective-permute-done((bf16[2,512,512]{2,1,0:T(8,128)(2,1)}, bf16[2,512,512]{2,1,0:T(8,128)(2,1)S(1)}, u32[]{:S(2)}, u32[]{:S(2)}) %collective-permute-start) | collective-permute-done | bytes 1048608 | tf_op jit(solution)/shard_map/ppermute | solution.py:291
  5.7 0.0 copy-done.3
  5.7 0.0 copy-done.2
  5.7 0.1 shard_map.51
  5.8 16.1 %all_to_all.10.got = bf16[4,200,512]{2,1,0:T(8,128)(2,1)S(1)} all-to-all(bf16[4,200,512]{2,1,0:T(8,128)(2,1)S(1)} %shard_map.51), channel_id=1, replica_groups={{0,64,128,192},{32,96,160,224},{256,320,384,448},{288,352,416,480},{1,6..., dimensions={0} | all-to-all | bytes 1638400 | tf_op jit(solution)/shard_map/all_to_all | solution.py:297
  21.9 0.2 shard_map.52
  22.1 36.7 %all-gather = bf16[528,512]{1,0:T(8,128)(2,1)S(1)} all-gather(bf16[264,512]{1,0:T(8,128)(2,1)S(1)} %shard_map.52), channel_id=2, replica_groups={{0,256},{32,288},{64,320},{96,352},{128,384},{160,416},{192,448},{224,4..., dimensions={0}, use_global_device_ids=true | all-gather | bytes 811008 | tf_op jit(solution)/shard_map/all_gather | solution.py:294
  58.7 0.2 shard_map.53
  58.9 16.0 %all_to_all.11.got = bf16[4,264,512]{2,1,0:T(8,128)(2,1)S(1)} all-to-all(bf16[4,264,512]{2,1,0:T(8,128)(2,1)S(1)} %shard_map.53), channel_id=1, replica_groups={{0,64,128,192},{32,96,160,224},{256,320,384,448},{288,352,416,480},{1,6..., dimensions={0} | all-to-all | bytes 2162688 | tf_op jit(solution)/shard_map/all_to_all | solution.py:297
  75.0 0.1 shard_map.55
  75.0 4.7 %collective-permute-start.1 = (bf16[784,512]{1,0:T(8,128)(2,1)S(1)}, bf16[784,512]{1,0:T(8,128)(2,1)S(1)}, u32[]{:S(2)}, u32[]{:S(2)}) collective-permute-start(bf16[784,512]{1,0:T(8,128)(2,1)S(1)} %shard_map.55), channel_id=1, source_target_pairs={{0,32},{32,0},{64,96},{96,64},{128,160},{160,128},{192,224},{224,1... | collective-permute-start | bytes 2408456 | tf_op jit(solution)/shard_map/ppermute | solution.py:291
  79.7 2.0 %shard_map.54 = (f32[3,256,256]{2,1,0:T(8,128)S(1)}, bf16[512,512]{1,0:T(8,128)(2,1)S(1)}, f32[3,256,256]{2,1,0:T(8,128)S(1)}, bf16[512,512]{1,0:T(8,128)(2,1)S(...) custom-call(bf16[4,264,512]{2,1,0:T(8,128)(2,1)S(1)} %all_to_all.11.got), custom_call_target="tpu_custom_call" | custom-call | flops 1073741824 | tf_op jit(solution)/shard_map/pallas_call | solution.py:312
  81.7 0.0 collective-permute-done.1.far
  81.7 0.0 copy-start.1
  81.7 4.9 %shard_map.56.mine = bf16[512,512]{1,0:T(8,128)(2,1)S(1)} custom-call(f32[3,256,256]{2,1,0:T(8,128)S(1)} %get-tuple-element.11.gram, bf16[512,512]{1,0:T(8,128)(2,1)S(1)} %get-tuple-element.12.low, f32[3,256,256]{2,1,0:T(8,128)S(1)} %get-tuple-element.13.later, bf16[512,512]{1,0:T(8,128)(2,1)S(1)} %get-tuple-element.10.dense, ...), custom_call_target="tpu_custom_call" | custom-call | flops 2684354560 | tf_op jit(solution)/shard_map/pallas_call | solution.py:315
  86.7 2.2 %collective-permute-start.2 = (bf16[512,512]{1,0:T(8,128)(2,1)S(1)}, bf16[512,512]{1,0:T(8,128)(2,1)S(1)}, u32[]{:S(2)}, u32[]{:S(2)}) collective-permute-start(bf16[512,512]{1,0:T(8,128)(2,1)S(1)} %shard_map.56.mine), channel_id=1, source_target_pairs={{0,32},{32,0},{64,96},{96,64},{128,160},{160,128},{192,224},{224,1... | collective-permute-start | bytes 1572872 | tf_op jit(solution)/shard_map/ppermute | solution.py:291
  88.8 0.0 copy-done.1
  88.9 1.7 %shard_map.57 = (f32[512,512]{1,0:T(8,128)}, bf16[2,512,512]{2,1,0:T(8,128)(2,1)}) custom-call(s32[2,32]{1,0:T(2,128)S(1)} %bitcast.13, bf16[512,512]{1,0:T(8,128)(2,1)S(1)} %get-tuple-element.10.dense, bf16[784,512]{1,0:T(8,128)(2,1)S(1)} %collective-permute-done.1.far, f32[512,512]{1,0:T(8,128)S(1)} %bitcast.6, bf16[512,512]{1,0:T(8,128)(2,1)S(1)} %shard_map.56.mine), custom_call_target="tpu_custom_call" | custom-call | flops 268435456 | bytes 3145728 | tf_op jit(solution)/shard_map/pallas_call | solution.py:317
  90.6 0.0 collective-permute-done.2.other
  90.6 0.8 shard_map.58
Async XLA Ops:
  0.6 5.1 %copy-start.3 = (s32[32,2]{0,1:T(2,128)S(1)}, s32[32,2]{0,1:T(2,128)}, u32[]{:S(2)}) copy-start(s32[32,2]{0,1:T(2,128)} %param.5) | copy-start | bytes 772
  0.6 5.1 %collective-permute-start = (bf16[2,512,512]{2,1,0:T(8,128)(2,1)}, bf16[2,512,512]{2,1,0:T(8,128)(2,1)S(1)}, u32[]{:S(2)}, u32[]{:S(2)}) collective-permute-start(bf16[2,512,512]{2,1,0:T(8,128)(2,1)} %bitcast.8), channel_id=1, source_target_pairs={{0,32},{32,0},{64,96},{96,64},{128,160},{160,128},{192,224},{224,1... | collective-permute-start | bytes 3145736 | tf_op jit(solution)/shard_map/ppermute | solution.py:291
  3.2 1.2 %copy-start = (f32[1,1,512,512]{3,2,1,0:T(8,128)S(1)}, f32[1,1,512,512]{3,2,1,0:T(8,128)}, u32[]{:S(2)}) copy-start(f32[1,1,512,512]{3,2,1,0:T(8,128)} %param.4) | copy-start | bytes 3145732
  4.5 1.3 %copy-start.2 = (bf16[1,2,512,512]{3,2,1,0:T(8,128)(2,1)S(1)}, bf16[1,2,512,512]{3,2,1,0:T(8,128)(2,1)}, u32[]{:S(2)}) copy-start(bf16[1,2,512,512]{3,2,1,0:T(8,128)(2,1)} %param.3) | copy-start | bytes 3145732
  75.0 6.7 %collective-permute-start.1 = (bf16[784,512]{1,0:T(8,128)(2,1)S(1)}, bf16[784,512]{1,0:T(8,128)(2,1)S(1)}, u32[]{:S(2)}, u32[]{:S(2)}) collective-permute-start(bf16[784,512]{1,0:T(8,128)(2,1)S(1)} %shard_map.55), channel_id=1, source_target_pairs={{0,32},{32,0},{64,96},{96,64},{128,160},{160,128},{192,224},{224,1... | collective-permute-start | bytes 2408456 | tf_op jit(solution)/shard_map/ppermute | solution.py:291
  81.7 7.1 %copy-start.1 = (f32[1,1,512,512]{3,2,1,0:T(8,128)S(1)}, f32[1,1,512,512]{3,2,1,0:T(8,128)}, u32[]{:S(2)}) copy-start(f32[1,1,512,512]{3,2,1,0:T(8,128)} %param.4) | copy-start | bytes 3145732
  86.7 3.9 %collective-permute-start.2 = (bf16[512,512]{1,0:T(8,128)(2,1)S(1)}, bf16[512,512]{1,0:T(8,128)(2,1)S(1)}, u32[]{:S(2)}, u32[]{:S(2)}) collective-permute-start(bf16[512,512]{1,0:T(8,128)(2,1)S(1)} %shard_map.56.mine), channel_id=1, source_target_pairs={{0,32},{32,0},{64,96},{96,64},{128,160},{160,128},{192,224},{224,1... | collective-permute-start | bytes 1572872 | tf_op jit(solution)/shard_map/ppermute | solution.py:291
